TPU v7x, 128 devices: a whole 4x4x4 slice. The times are simulated.
128 devices in a mesh: rec: 4 (over x_hi, core), tm: 32 (over x_lo, y, z).
Axes of the slice: x: 4 (x_hi: 2, x_lo: 2; x = x_hi * 2 + x_lo), y: 4, z: 4, core: 2. Of those that a mesh axis runs over, the one named last changes fastest.
Arguments:
- frames: bfloat16 [4, 16384, 1024], P('rec', 'tm'), may hold values from -6 to 6
- cotangent: bfloat16 [4, 16384, 1024], P('rec', 'tm'), may hold values from -6 to 6
- lengths: int32 [4], P('rec'), may hold values from 2048 to 16384, as said below
- w_query: bfloat16 [1024, 1024], replicated, may hold values from -1 to 1
- w_key: bfloat16 [1024, 1024], replicated, may hold values from -4 to 4
- w_value: bfloat16 [1024, 1024], replicated, may hold values from -0.1875 to 0.1875
- w_out: bfloat16 [1024, 1024], replicated, may hold values from -0.1875 to 0.1875
Outputs:
- grad_frames: bfloat16 [4, 16384, 1024], P('rec', 'tm')
- grad_projections: float32 [1024, 3072], P(('rec', 'tm'))
Inputs may be any that keep to these rules, and one draw needn't show every extreme that they name: `lengths`: one recording is whole in every draw.
All inputs are finite; a program needn't handle non-finite values.
Results may differ from a plain program's by a relative error of at most 0.019.
Values may be sent and summed in bfloat16 or wider, within the bound.
No kernel may reach another device: no remote copies, remote signals or barrier semaphores. Data moves between devices by JAX's collectives and lax.ppermute only.
A program may use at most 128 MiB of HBM per device.

v0:
```python
import jax
import jax.numpy as jnp
from jax import lax
from jax.sharding import PartitionSpec as P

HEADS = 8
WIN = 128


epsilon = 1e-05
masked_value = -1e30


def with_halo(block, sides, width):
    for axis, dim in sides:
        count = lax.axis_size(axis)
        forward = [(i, i + 1) for i in range(count - 1)]
        backward = [(target, source) for source, target in forward]
        low = lax.ppermute(
            lax.slice_in_dim(block, block.shape[dim] - width, None, axis=dim), axis, forward
        )
        high = lax.ppermute(lax.slice_in_dim(block, 0, width, axis=dim), axis, backward)
        block = jnp.concatenate([low, block, high], axis=dim)
    return block


def shifted(value, axis, steps):
    count = lax.axis_size(axis)
    first, last = (max(0, -steps), min(count, count - steps))
    return lax.ppermute(value, axis, [(source, source + steps) for source in range(first, last)])


def normalize(frame_rows):
    values = frame_rows.astype(jnp.float32)
    center = values - jnp.mean(values, -1, keepdims=True)
    inverse = lax.rsqrt(jnp.mean(center * center, -1, keepdims=True) + epsilon)
    return (center * inverse, inverse)


def masked_scores(q_heads, k_heads, q_pos, k_pos, length):
    scale = q_heads.shape[2] ** (-0.5)
    scores = (
        jnp.einsum("qhd,khd->hqk", q_heads, k_heads, preferred_element_type=jnp.float32) * scale
    )
    allowed = (
        (jnp.abs(q_pos[:, None] - k_pos[None, :]) <= WIN)
        & (k_pos[None, :] >= 0)
        & (k_pos[None, :] < length)
    )
    return (jnp.where(allowed[None], scores, masked_value), scale)


def attend(q_rows, k_rows, v_rows, d_rows, q_pos, k_pos, length):
    count = q_rows.shape[0]
    keys_count = k_rows.shape[0]
    q_heads = q_rows.reshape(count, HEADS, -1)
    k_heads = k_rows.reshape(keys_count, HEADS, -1)
    v_heads = v_rows.reshape(keys_count, HEADS, -1)
    d_heads = d_rows.reshape(count, HEADS, -1)
    scores, scale = masked_scores(q_heads, k_heads, q_pos, k_pos, length)
    row_max = jnp.max(scores, 2)
    expo = jnp.exp(scores - row_max[:, :, None])
    row_sum = jnp.sum(expo, 2)
    prob = expo / row_sum[:, :, None]
    prob_b = prob.astype(jnp.bfloat16)
    mixed = jnp.einsum("hqk,khd->qhd", prob_b, v_heads, preferred_element_type=jnp.float32).astype(
        jnp.bfloat16
    )
    d_prob = jnp.einsum("qhd,khd->hqk", d_heads, v_heads, preferred_element_type=jnp.float32)
    row_delta = jnp.sum(d_heads.astype(jnp.float32) * mixed.astype(jnp.float32), 2).T
    d_scores = (prob * (d_prob - row_delta[:, :, None]) * scale).astype(jnp.bfloat16)
    grad_q = jnp.einsum(
        "hqk,khd->qhd", d_scores, k_heads, preferred_element_type=jnp.float32
    ).astype(jnp.bfloat16)
    grad_k = jnp.einsum("hqk,qhd->khd", d_scores, q_heads, preferred_element_type=jnp.float32)
    grad_v = jnp.einsum("hqk,qhd->khd", prob_b, d_heads, preferred_element_type=jnp.float32)
    return (
        grad_q.reshape(count, -1),
        grad_k.reshape(keys_count, -1),
        grad_v.reshape(keys_count, -1),
        row_max,
        row_sum,
        row_delta,
    )


def shards(frames, cotangent, lengths, w_query, w_key, w_value, w_out):
    frame_rows = frames[0]
    grad_rows = cotangent[0]
    length = lengths[0]
    height = frame_rows.shape[0]
    width = frame_rows.shape[1]
    anchor = lax.axis_index("tm") * height
    position = anchor + jnp.arange(height, dtype=jnp.int32)
    normed, inverse = normalize(frame_rows)
    hidden = normed.astype(jnp.bfloat16)
    query = jnp.dot(hidden, w_query, preferred_element_type=jnp.float32).astype(jnp.bfloat16)
    keys = jnp.dot(hidden, w_key, preferred_element_type=jnp.float32).astype(jnp.bfloat16)
    values = jnp.dot(hidden, w_value, preferred_element_type=jnp.float32).astype(jnp.bfloat16)
    masked = jnp.where((position < length)[:, None], grad_rows, jnp.zeros_like(grad_rows))
    d_mixed = jnp.einsum("tg,fg->tf", masked, w_out, preferred_element_type=jnp.float32).astype(
        jnp.bfloat16
    )
    padded = with_halo(jnp.stack([keys, values]), (("tm", 1),), WIN)
    block_rows = min(512, height)
    key_sum = jnp.zeros((height + 2 * WIN, width), jnp.float32)
    value_sum = jnp.zeros((height + 2 * WIN, width), jnp.float32)
    query_parts, max_parts, sum_parts, delta_parts = ([], [], [], [])
    span_end = block_rows + 2 * WIN
    k_pos = anchor - WIN + 0 + jnp.arange(block_rows + 2 * WIN, dtype=jnp.int32)
    grad_q, grad_k, grad_v, row_max, row_sum, row_delta = attend(
        query, padded[0, 0:span_end], padded[1, 0:span_end], d_mixed, position, k_pos, length
    )
    key_sum = key_sum.at[0:span_end].add(grad_k)
    value_sum = value_sum.at[0:span_end].add(grad_v)
    query_parts.append(grad_q)
    max_parts.append(row_max)
    sum_parts.append(row_sum)
    delta_parts.append(row_delta)
    grad_query = query_parts[0]
    key_own = key_sum[WIN : WIN + height]
    value_own = value_sum[WIN : WIN + height]
    toward_left = jnp.stack([key_sum[:WIN], value_sum[:WIN]])
    toward_right = jnp.stack([key_sum[height + WIN :], value_sum[height + WIN :]])
    from_right = shifted(toward_left.astype(jnp.bfloat16), "tm", -1).astype(toward_left.dtype)
    from_left = shifted(toward_right.astype(jnp.bfloat16), "tm", 1).astype(toward_right.dtype)
    key_own = key_own.at[height - WIN :].add(from_right[0]).at[:WIN].add(from_left[0])
    value_own = value_own.at[height - WIN :].add(from_right[1]).at[:WIN].add(from_left[1])
    grad_key = key_own.astype(jnp.bfloat16)
    grad_value = value_own.astype(jnp.bfloat16)
    d_hidden = (
        jnp.einsum("tg,fg->tf", grad_query, w_query, preferred_element_type=jnp.float32)
        + jnp.einsum("tg,fg->tf", grad_key, w_key, preferred_element_type=jnp.float32)
        + jnp.einsum("tg,fg->tf", grad_value, w_value, preferred_element_type=jnp.float32)
    )
    mean_grad = jnp.mean(d_hidden, -1, keepdims=True)
    mean_cross = jnp.mean(d_hidden * normed, -1, keepdims=True)
    grad_frames = (
        grad_rows.astype(jnp.float32) + inverse * (d_hidden - mean_grad - normed * mean_cross)
    ).astype(jnp.bfloat16)
    projected = jnp.concatenate([grad_query, grad_key, grad_value], 1)
    weight_part = lax.psum_scatter(
        jnp.einsum("tf,tg->fg", hidden, projected, preferred_element_type=jnp.float32),
        ("rec", "tm"),
        scatter_dimension=0,
        tiled=True,
    )
    return (grad_frames[None], weight_part)


def solution(mesh):
    placed = (P("rec", "tm", None), P("rec", "tm", None), P("rec"), P(), P(), P(), P())
    return jax.shard_map(
        shards,
        mesh=mesh,
        in_specs=placed,
        out_specs=(P("rec", "tm", None), P(("rec", "tm"), None)),
        check_vma=False,
    )
```

profile of v0, /device:TPU:0, one launch (start us, length us, event | category | flops | bytes accessed | tf_op | source)
XLA Modules:
  0.0 776.5 jit_solution(143546872042103431)
XLA Ops:
  7.2 0.0 copy-start
  7.2 0.0 copy-start.1
  7.2 0.0 reduce-scatter.2.cloned.1.call-start
  7.2 1.6 convert_reduce_fusion
  8.8 1.6 fusion.23
  10.5 0.0 copy-done.1
  10.5 0.0 copy-start.15
  10.5 1.3 fusion.28
  11.8 0.3 copy-done.15
  12.1 1.3 fusion.27
  13.4 1.1 pad_maximum_fusion.2
  14.6 0.2 copy-done.9
  14.8 4.7 collective-permute-start
  19.5 1.5 collective-permute-start.1
  21.6 4.2 convolution_convert_fusion.2
  25.8 2.3 copy.20
  28.1 3.9 convolution_convert_fusion.3
  31.9 2.3 copy.19
  34.2 0.6 fusion.26
  34.8 0.0 collective-permute-done
  34.8 0.2 collective-permute-done.1
  35.1 2.0 pad_maximum_fusion
  37.1 1.9 fusion.53
  39.0 2.6 copy.21
  41.6 2.6 copy.18
  44.2 11.7 %fusion.56 = (f32[8,512]{1,0:T(8,128)}, f32[8,512,768]{2,1,0:T(8,128)}) fusion(pred[512,768]{1,0:T(8,128)(4,1)S(1)} %fusion.26, bf16[512,8,128]{0,2,1:T(8,128)(2,1)} %bitcast.122, bf16[768,8,128]{0,2,1:T(8,128)(2,1)} %bitcast.124), kind=kOutput, calls=%fused_computation.85 | convolution fusion | flops 817890048 | bytes 15613952 | tf_op jit(solution)/shard_map/sub | solution.py:62
  55.9 5.4 fusion.5
  61.3 1.0 fusion.57
  62.3 0.4 copy-done.5
  62.7 2.1 fusion.24
  64.9 0.1 fusion.55
  65.0 6.3 multiply_convert_fusion
  71.4 0.0 copy-done.3
  71.4 1.0 fusion.58
  72.4 0.1 fusion.54
  72.5 0.1 pad_maximum_fusion.3
  72.6 1.4 collective-permute-start.2
  74.0 0.1 pad_maximum_fusion.4
  74.1 5.0 collective-permute-start.3
  79.1 2.1 convolution_convert_fusion
  81.3 0.3 slice.186
  81.6 0.3 slice.195
  81.9 6.5 collective-permute-done.2
  88.4 0.1 convert_element_type.82
  88.5 0.2 fusion.36
  88.7 1.0 collective-permute-done.3
  89.7 0.1 convert_element_type.83
  89.7 0.2 fusion.34
  90.0 0.1 convert_element_type.85
  90.1 0.0 copy-start.6
  90.1 0.1 convert_element_type.84
  90.3 0.8 copy-done.6
  91.1 0.3 copy-done.12
  91.4 9.5 %fusion.6 = f32[1024,3072]{1,0:T(8,128)} fusion(bf16[512,1024]{0,1:T(8,128)(2,1)S(1)} %convert_element_type.85, bf16[512,1024]{0,1:T(8,128)(2,1)S(1)} %convert_element_type.84, bf16[512,1024]{0,1:T(8,128)(2,1)S(1)} %bitcast.130, bf16[1,512,1024]{2,1,0:T(8,128)(2,1)S(1)} %copy-done.1, f32[512]{0:T(512)S(1)} %add_rsqrt_fusion, ...), kind=kOutput, calls=%fused_computation.11 | convolution fusion | flops 3232759808 | bytes 16781312 | tf_op jit(solution)/shard_map/tf,tg->fg/dot_general | solution.py:143
  101.0 0.0 reduce-scatter.2.cloned.1.call-update
  101.0 0.0 copy-start.16
  101.0 3.4 fusion.59
  104.4 0.0 copy-start.7
  104.4 1.3 fusion.60
  105.7 0.0 copy-start.10
  105.7 1.8 fusion.52
  107.5 0.0 copy-done.10
  107.5 1.7 fusion.31
  109.3 660.3 %reduce-scatter.2.cloned.1.call-done = f32[8,3072]{1,0:T(8,128)} async-done(((f32[1024,3072]{1,0:T(8,128)}), f32[8,3072]{1,0:T(8,128)}) %reduce-scatter.2.cloned.1.call-update) | async-done | bytes 98320 | tf_op jit(solution)/shard_map/reduce_scatter | solution.py:142
  (29 shorter events, 0.2 us)
Async XLA Ops:
  7.2 3.3 copy-start
  7.2 3.3 copy-start.1
  7.2 762.4 %reduce-scatter.2.cloned.1.call-start = ((), (), s32[]{:S(2)}) async-start(), calls=%async_computation.1 | async-start | bytes 12681216 | tf_op jit(solution)/shard_map/reduce_scatter | solution.py:142
  10.5 1.6 copy-start.15
  12.1 1.3 copy-start.8
  13.4 1.3 copy-start.9
  14.8 20.1 %collective-permute-start = (bf16[2,128,1024]{2,1,0:T(8,128)(2,1)}, bf16[2,128,1024]{2,1,0:T(8,128)(2,1)}, u32[]{:S(2)}, u32[]{:S(2)}) collective-permute-start(bf16[2,128,1024]{2,1,0:T(8,128)(2,1)} %get-tuple-element.94), channel_id=1, source_target_pairs={{0,1},{1,2},{2,3},{3,4},{4,5},{5,6},{6,7},{7,8},{8,9},{9,10},{10,1... | collective-permute-start | bytes 1572872 | tf_op jit(solution)/shard_map/ppermute | solution.py:19
  19.5 15.6 %collective-permute-start.1 = (bf16[2,128,1024]{2,1,0:T(8,128)(2,1)}, bf16[2,128,1024]{2,1,0:T(8,128)(2,1)}, u32[]{:S(2)}, u32[]{:S(2)}) collective-permute-start(bf16[2,128,1024]{2,1,0:T(8,128)(2,1)} %get-tuple-element.95), channel_id=1, source_target_pairs={{1,0},{2,1},{3,2},{4,3},{5,4},{6,5},{7,6},{8,7},{9,8},{10,9},{11,1... | collective-permute-start | bytes 1572872 | tf_op jit(solution)/shard_map/ppermute | solution.py:22
  55.9 5.4 copy-start.2
  61.3 1.4 copy-start.5
  62.7 2.3 copy-start.14
  65.0 6.4 copy-start.3
  72.4 6.7 copy-start.4
  72.6 15.8 %collective-permute-start.2 = (bf16[2,128,1024]{1,2,0:T(8,128)(2,1)S(1)}, bf16[2,128,1024]{1,2,0:T(8,128)(2,1)S(1)}, u32[]{:S(2)}, u32[]{:S(2)}) collective-permute-start(bf16[2,128,1024]{1,2,0:T(8,128)(2,1)S(1)} %pad_maximum_fusion.3), channel_id=1, source_target_pairs={{1,0},{2,1},{3,2},{4,3},{5,4},{6,5},{7,6},{8,7},{9,8},{10,9},{11,1... | collective-permute-start | bytes 1572872 | tf_op jit(solution)/shard_map/ppermute | solution.py:30
  74.1 15.6 %collective-permute-start.3 = (bf16[2,128,1024]{1,2,0:T(8,128)(2,1)S(1)}, bf16[2,128,1024]{1,2,0:T(8,128)(2,1)S(1)}, u32[]{:S(2)}, u32[]{:S(2)}) collective-permute-start(bf16[2,128,1024]{1,2,0:T(8,128)(2,1)S(1)} %pad_maximum_fusion.4), channel_id=1, source_target_pairs={{0,1},{1,2},{2,3},{3,4},{4,5},{5,6},{6,7},{7,8},{8,9},{9,10},{10,1... | collective-permute-start | bytes 1572872 | tf_op jit(solution)/shard_map/ppermute | solution.py:30
  81.3 9.0 %copy-start.11 = (bf16[8,128,512]{2,1,0:T(8,128)(2,1)}, bf16[8,128,512]{2,1,0:T(8,128)(2,1)S(1)}, u32[]{:S(2)}) copy-start(bf16[8,128,512]{2,1,0:T(8,128)(2,1)S(1)} %convolution_convert_fusion) | copy-start | bytes 3145732
  90.1 1.0 copy-start.6
  90.3 1.2 copy-start.12
  101.0 3.4 copy-start.13
  101.0 3.4 copy-start.16
  104.4 1.3 copy-start.7
  105.7 1.8 copy-start.10
Sparse Core Ops, SparseCore 0:
  101.1 668.4 reduce-scatter.1
where the time goes:
time: 777 us; the launch traced here: 776 us
  waiting for transfers between devices  668 us (86%)
  matrix products  50.9 us (7%)
  other arithmetic  15.1 us (2%)
  between operations  15.1 us (2%)
  local copies, waits for them, and re-layouts  14.6 us (2%)
  starting transfers between devices  12.6 us (2%)
    reduce_scatter x1, waiting for transfers between devices, shards(): lax.psum_scatter(jnp.einsum('tf,tg->fg', hidden, projected, preferred_ele...  660 us
  transfers between devices with their start and end apart: 5, of which 4 were waited for; matrix products, arithmetic and copies ran while one was open for 3% of the time, Pallas kernels for 0%

commit v1 on v0

--- a/solution.py
+++ b/solution.py
@@ -5,6 +5,60 @@
 
 HEADS = 8
 WIN = 128
+
+
+AXES = ("rec", "tm")
+CORE = 32
+NEAR = ((16, 4, 1), (80, 12, 3))
+
+
+def order_of(core):
+    return NEAR[core] + NEAR[1 - core]
+
+
+def exchange(value, masks):
+    count = lax.axis_size(AXES)
+    pairs = [(i, i ^ masks[(i // CORE) % 2]) for i in range(count)]
+    return lax.ppermute(value, AXES, pairs)
+
+
+def row_targets(me):
+    row = jnp.arange(1024, dtype=jnp.int32)
+    far = (row >> 9) & 1
+    core = ((me // CORE) % 2) ^ far
+    target = me ^ (far * CORE)
+    for bit in range(6):
+        mask = jnp.where(core == 0, order_of(0)[bit], order_of(1)[bit])
+        target = target ^ (((row >> (8 - bit)) & 1) * mask)
+    return target * 8 + (row & 7)
+
+
+def halves(value, dim):
+    return lax.index_in_dim(value, 0, dim, False), lax.index_in_dim(value, 1, dim, False)
+
+
+def add(a, b):
+    return (a.astype(jnp.float32) + b.astype(jnp.float32)).astype(jnp.bfloat16)
+
+
+def scatter_sum(parts):
+    masks = list(zip(order_of(0), order_of(1)))
+    values = [part.reshape(2, 2, 2, 2, 2, 2, 8, -1) for part in parts]
+    left = [[0, 1, 2] for _ in values]
+    for step in range(3):
+        sent = []
+        for part in range(3):
+            bit = (part + step) % 3
+            keep, send = halves(values[part], left[part].index(bit))
+            left[part].remove(bit)
+            sent.append((keep, exchange(send, masks[bit])))
+        values = [add(keep, got) for keep, got in sent]
+    value = jnp.concatenate(values, -1)
+    for bit in range(3, 6):
+        keep, send = value[0], value[1]
+        got = exchange(send, masks[bit])
+        value = add(keep, got) if bit < 5 else keep.astype(jnp.float32) + got.astype(jnp.float32)
+    return value
 
 
 epsilon = 1e-05
@@ -138,13 +192,17 @@
     grad_frames = (
         grad_rows.astype(jnp.float32) + inverse * (d_hidden - mean_grad - normed * mean_cross)
     ).astype(jnp.bfloat16)
+    me = lax.axis_index(AXES)
+    targets = row_targets(me)
+    spread = (targets[None, :] == jnp.arange(width, dtype=jnp.int32)[:, None]).astype(jnp.bfloat16)
+    ordered = jnp.dot(hidden, spread, preferred_element_type=jnp.float32).astype(jnp.bfloat16)
     projected = jnp.concatenate([grad_query, grad_key, grad_value], 1)
-    weight_part = lax.psum_scatter(
-        jnp.einsum("tf,tg->fg", hidden, projected, preferred_element_type=jnp.float32),
-        ("rec", "tm"),
-        scatter_dimension=0,
-        tiled=True,
-    )
+    partial = jnp.einsum("tf,tg->fg", ordered, projected, preferred_element_type=jnp.float32).astype(
+        jnp.bfloat16
+    )
+    got = exchange(partial[512:], (CORE, CORE))
+    own = add(partial[:512], got)
+    weight_part = scatter_sum([own[:, :1024], own[:, 1024:2048], own[:, 2048:]])
     return (grad_frames[None], weight_part)
 
 

time: 777 us -> 160 us (0.21)
  waiting for transfers between devices: 668 us -> 29.3 us
  starting transfers between devices: 12.6 us -> 41.7 us
  between operations: 15.1 us -> 1.96 us
    reduce_scatter x1 -> x0, waiting for transfers between devices: 660 us -> none  [shards(): lax.psum_scatter(jnp.einsum('tf,tg->fg', hidden, projected, preferred_ele...]
    ppermute x0 -> x13, starting transfers between devices: none -> 29 us  [exchange(): return lax.ppermute(value, AXES, pairs)]
    ppermute x0 -> x13, waiting for transfers between devices: none -> 22.5 us  [exchange(): return lax.ppermute(value, AXES, pairs)]
  transfers between devices with their start and end apart: 5 -> 17, of which waited for: 4 -> 13; matrix products, arithmetic and copies ran while one was open for 3% -> 15% of each run, Pallas kernels for 0% -> 0%
where the time goes in v1:
time: 160 us; the launch traced here: 159 us
  matrix products  49.8 us (31%)
  starting transfers between devices  41.7 us (26%)
  waiting for transfers between devices  29.3 us (18%)
  other arithmetic  20 us (12%)
  local copies, waits for them, and re-layouts  16.6 us (10%)
  between operations  1.96 us (1%)
    ppermute x13, starting transfers between devices, exchange(): return lax.ppermute(value, AXES, pairs)  29 us
    ppermute x13, waiting for transfers between devices, exchange(): return lax.ppermute(value, AXES, pairs)  22.5 us
    sub x1, matrix products, attend(): expo = jnp.exp(scores - row_max[:, :, None])  11.6 us
    dot_general x1, matrix products, shards(): jnp.einsum('tf,tg->fg', ordered, projected, preferred_element_type=jnp.fl...  9.38 us
    ppermute x2, waiting for transfers between devices, shifted(): lax.ppermute(value, axis, [(source, source + steps) for source in range(f...  6.58 us
    ppermute x2, starting transfers between devices, shifted(): lax.ppermute(value, axis, [(source, source + steps) for source in range(f...  6.51 us
    dot_general x1, matrix products, attend(): jnp.einsum('qhd,khd->hqk', d_heads, v_heads, preferred_element_type=jnp.f...  6.34 us
    convert_element_type x1, other arithmetic, attend(): prob_b = prob.astype(jnp.bfloat16)  5.4 us
  transfers between devices with their start and end apart: 17, of which 13 were waited for; matrix products, arithmetic and copies ran while one was open for 15% of the time, Pallas kernels for 0%

profile of v1, /device:TPU:0, one launch (start us, length us, event | category | flops | bytes accessed | tf_op | source)
XLA Modules:
  0.0 159.3 jit_solution(9337099393431696821)
XLA Ops:
  0.7 1.6 convert_reduce_fusion
  2.2 1.6 %fusion.23 = f32[512]{0:T(512)S(1)} fusion(bf16[1,512,1024]{2,1,0:T(8,128)(2,1)} %param.23, f32[512]{0:T(512)S(1)} %broadcast_multiply_fusion.2), kind=kLoop, calls=%fused_computation.33 | loop fusion | flops 2096640 | bytes 1052672 | tf_op jit(solution)/shard_map/reduce_sum | solution.py:90
  3.9 1.3 fusion.30
  5.2 0.3 copy-done.14
  5.5 1.3 fusion.29
  6.9 1.1 pad_maximum_fusion.2
  8.0 0.2 copy-done.8
  8.2 4.7 %collective-permute-start = (bf16[2,128,1024]{2,1,0:T(8,128)(2,1)}, bf16[2,128,1024]{2,1,0:T(8,128)(2,1)}, u32[]{:S(2)}, u32[]{:S(2)}) collective-permute-start(bf16[2,128,1024]{2,1,0:T(8,128)(2,1)} %get-tuple-element.98), channel_id=1, source_target_pairs={{0,1},{1,2},{2,3},{3,4},{4,5},{5,6},{6,7},{7,8},{8,9},{9,10},{10,1... | collective-permute-start | bytes 1572872 | tf_op jit(solution)/shard_map/ppermute | solution.py:73
  12.9 1.5 collective-permute-start.1
  15.0 4.2 %convolution_convert_fusion.3 = bf16[512,1024]{1,0:T(8,128)(2,1)} fusion(bf16[1024,1024]{1,0:T(8,128)(2,1)} %param.29, bf16[1,512,1024]{2,1,0:T(8,128)(2,1)} %param.24, pred[512]{0:T(512)(128)(4,1)S(1)} %broadcast_compare_fusion), kind=kOutput, calls=%fused_computation.46 | convolution fusion | flops 1074790400 | bytes 4194816 | tf_op jit(solution)/shard_map/tg,fg->tf/dot_general | solution.py:155
  19.2 2.3 %copy.28 = bf16[512,1024]{0,1:T(8,128)(2,1)} copy(bf16[512,1024]{1,0:T(8,128)(2,1)} %convolution_convert_fusion.3) | data formatting | bytes 2097152 | tf_op jit(solution)/shard_map/reshape | solution.py:113
  21.5 3.9 %convolution_convert_fusion.4 = bf16[512,1024]{1,0:T(8,128)(2,1)} fusion(bf16[1024,1024]{1,0:T(8,128)(2,1)} %param.26, bf16[1,512,1024]{2,1,0:T(8,128)(2,1)S(1)} %copy-done.1, f32[512]{0:T(512)S(1)} %add_rsqrt_fusion, f32[512]{0:T(512)S(1)} %broadcast_multiply_fusion.2), kind=kOutput, calls=%fused_computation.47 | convolution fusion | flops 1076363264 | bytes 4198400 | tf_op jit(solution)/shard_map/dot_general | solution.py:151
  25.4 2.3 %copy.27 = bf16[512,1024]{0,1:T(8,128)(2,1)} copy(bf16[512,1024]{1,0:T(8,128)(2,1)} %convolution_convert_fusion.4) | data formatting | bytes 2097152 | tf_op jit(solution)/shard_map/reshape | solution.py:110
  27.7 0.6 fusion.27
  28.5 2.0 %pad_maximum_fusion = bf16[2,768,1024]{2,1,0:T(8,128)(2,1)S(1)} fusion(bf16[2,128,1024]{2,1,0:T(8,128)(2,1)} %collective-permute-done.1, bf16[1,512,1024]{2,1,0:T(8,128)(2,1)} %copy-done.7, bf16[1,512,1024]{2,1,0:T(8,128)(2,1)} %copy-done.8, bf16[2,128,1024]{2,1,0:T(8,128)(2,1)} %collective-permute-done), kind=kLoop, calls=%fused_computation.14 | loop fusion | flops 12582912 | bytes 6291456 | tf_op jit(solution)/shard_map/concatenate | solution.py:77
  30.5 2.0 %fusion.69 = (bf16[1,768,1024]{2,1,0:T(8,128)(2,1)}, bf16[1,768,1024]{2,1,0:T(8,128)(2,1)}) fusion(bf16[2,768,1024]{2,1,0:T(8,128)(2,1)S(1)} %pad_maximum_fusion), kind=kLoop, calls=%fused_computation.138 | loop fusion | bytes 6291456 | tf_op jit(solution)/shard_map/slice | solution.py:166
  32.5 2.6 %copy.29 = bf16[1,768,1024]{1,2,0:T(8,128)(2,1)} copy(bf16[1,768,1024]{2,1,0:T(8,128)(2,1)} %get-tuple-element.96) | data formatting | bytes 3145728 | tf_op jit(solution)/shard_map/reshape;squeeze | solution.py:112
  35.1 2.6 %copy.26 = bf16[1,768,1024]{1,2,0:T(8,128)(2,1)} copy(bf16[1,768,1024]{2,1,0:T(8,128)(2,1)} %get-tuple-element.97) | data formatting | bytes 3145728 | tf_op jit(solution)/shard_map/reshape;squeeze | solution.py:111
  37.7 11.6 %fusion.73 = (f32[8,512]{1,0:T(8,128)}, f32[8,512,768]{2,1,0:T(8,128)}) fusion(pred[512,768]{1,0:T(8,128)(4,1)S(1)} %fusion.27, bf16[512,8,128]{0,2,1:T(8,128)(2,1)} %bitcast.210, bf16[768,8,128]{0,2,1:T(8,128)(2,1)} %bitcast.214), kind=kOutput, calls=%fused_computation.142 | convolution fusion | flops 817890048 | bytes 15613952 | tf_op jit(solution)/shard_map/sub | solution.py:116
  49.3 5.4 %fusion.5 = bf16[8,512,768]{2,1,0:T(8,128)(2,1)S(1)} fusion(f32[8,512,768]{2,1,0:T(8,128)} %get-tuple-element.111, f32[8,512]{1,0:T(8,128)} %get-tuple-element.110), kind=kLoop, calls=%fused_computation.11 | loop fusion | flops 6291456 | bytes 18890752 | tf_op jit(solution)/shard_map/convert_element_type | solution.py:119
  54.7 1.0 fusion.74
  55.8 0.4 copy-done.5
  56.1 2.1 %fusion.24 = f32[512,8]{0,1:T(8,128)S(1)} fusion(bf16[512,8,128]{0,2,1:T(8,128)(2,1)S(1)} %bitcast.206, bf16[768,8,128]{0,2,1:T(8,128)(2,1)S(1)} %bitcast.216, bf16[8,512,768]{2,1,0:T(8,128)(2,1)S(1)} %fusion.5), kind=kOutput, calls=%fused_computation.35 | convolution fusion | flops 807923712 | bytes 8929280 | tf_op jit(solution)/shard_map/hqk,khd->qhd/dot_general | solution.py:120
  58.4 6.3 %multiply_convert_fusion = bf16[8,512,768]{2,1,0:T(8,128)(2,1)S(1)} fusion(f32[8,512]{1,0:T(8,128)S(1)} %bitcast.232, f32[8,512,768]{2,1,0:T(8,128)} %get-tuple-element.111, f32[8,512]{1,0:T(8,128)S(1)} %copy-done.12, bf16[512,8,128]{0,2,1:T(8,128)(2,1)S(1)} %bitcast.207, bf16[768,8,128]{0,2,1:T(8,128)(2,1)S(1)} %bitcast.217), kind=kOutput, calls=%fused_computation.1 | convolution fusion | flops 821035008 | bytes 21528576 | tf_op jit(solution)/shard_map/qhd,khd->hqk/dot_general | solution.py:123
  64.8 1.0 fusion.75
  66.0 1.4 collective-permute-start.2
  67.5 5.1 %collective-permute-start.3 = (bf16[2,128,1024]{1,2,0:T(8,128)(2,1)S(1)}, bf16[2,128,1024]{1,2,0:T(8,128)(2,1)S(1)}, u32[]{:S(2)}, u32[]{:S(2)}) collective-permute-start(bf16[2,128,1024]{1,2,0:T(8,128)(2,1)S(1)} %pad_maximum_fusion.4), channel_id=1, source_target_pairs={{0,1},{1,2},{2,3},{3,4},{4,5},{5,6},{6,7},{7,8},{8,9},{9,10},{10,1... | collective-permute-start | bytes 1572872 | tf_op jit(solution)/shard_map/ppermute | solution.py:84
  72.6 3.1 %convolution_convert_fusion.1 = bf16[8,128,512]{2,1,0:T(8,128)(2,1)} fusion(bf16[768,8,128]{0,2,1:T(8,128)(2,1)S(1)} %bitcast.215, bf16[8,512,768]{2,1,0:T(8,128)(2,1)S(1)} %multiply_convert_fusion), kind=kOutput, calls=%fused_computation.44 | convolution fusion | flops 805830656 | bytes 8912896 | tf_op jit(solution)/shard_map/hqk,khd->qhd/dot_general | solution.py:126
  75.7 0.3 slice.303
  76.1 0.3 slice.312
  76.4 5.6 %collective-permute-done.2 = bf16[2,128,1024]{1,2,0:T(8,128)(2,1)S(1)} collective-permute-done((bf16[2,128,1024]{1,2,0:T(8,128)(2,1)S(1)}, bf16[2,128,1024]{1,2,0:T(8,128)(2,1)S(1)}, u32[]{:S(2)}, u32[]{:S(2)}) %collective-permute-start.2) | collective-permute-done | bytes 524320 | tf_op jit(solution)/shard_map/ppermute | solution.py:84
  82.2 1.0 collective-permute-done.3
  83.2 0.2 fusion.39
  83.5 1.1 convert_element_type.242
  84.6 1.2 convert_element_type.241
  85.8 9.4 %convolution_convert_fusion = bf16[1024,3072]{1,0:T(8,128)(2,1)} fusion(bf16[512,1024]{0,1:T(8,128)(2,1)} %convert_element_type.242, bf16[512,1024]{0,1:T(8,128)(2,1)} %convert_element_type.241, bf16[512,1024]{0,1:T(8,128)(2,1)} %bitcast.224, s32[1024]{0:T(1024)S(1)} %and_add_fusion, bf16[1,512,1024]{2,1,0:T(8,128)(2,1)S(1)} %copy-done.1, ...), kind=kOutput, calls=%fused_computation.10 | convolution fusion | flops 4311220224 | bytes 10493952 | tf_op jit(solution)/shard_map/tf,tg->fg/dot_general | solution.py:200
  95.2 2.2 %slice.318 = bf16[512,3072]{1,0:T(8,128)(2,1)S(1)} slice(bf16[1024,3072]{1,0:T(8,128)(2,1)} %convolution_convert_fusion), slice={[512:1024], [0:3072]} | slice | bytes 6291456 | tf_op jit(solution)/shard_map/slice | solution.py:203
  97.4 0.3 collective-permute-start.4
  97.8 0.2 copy-done.13
  98.0 1.3 fusion.76
  99.5 1.3 fusion.77
  100.8 1.9 %fusion.66 = (f32[512]{0:T(512)S(1)}, f32[512]{0:T(512)S(1)}, f32[512,1024]{1,0:T(8,128)S(1)}) fusion(f32[512]{0:T(512)S(1)} %add_rsqrt_fusion, f32[512]{0:T(512)S(1)} %broadcast_multiply_fusion.2, bf16[1,512,1024]{2,1,0:T(8,128)(2,1)S(1)} %copy-done.1, bf16[512,1024]{0,1:T(8,128)(2,1)S(1)} %copy-done.6, bf16[1024,1024]{1,0:T(8,128)(2,1)S(1)} %copy-done, ...), kind=kOutput, calls=%fused_computation.135 | convolution fusion | flops 1077935104 | bytes 10493952 | tf_op jit(solution)/shard_map/tg,fg->tf/dot_general | solution.py:188
  102.7 0.7 collective-permute-done.4
  103.5 1.2 add_convert_fusion
  104.7 0.2 fusion.68
  104.9 2.6 %collective-permute-start.11 = (bf16[2,2,2,2,2,8,1024]{6,5,4,3,2,1,0:T(8,128)(2,1)S(1)}, bf16[2,2,2,2,2,8,1024]{6,5,4,3,2,1,0:T(8,128)(2,1)S(1)}, u32[]{:S(2)}, u32[]{:S(2)}) collective-permute-start(bf16[2,2,2,2,2,8,1024]{6,5,4,3,2,1,0:T(8,128)(2,1)S(1)} %slice_bitcast_fusion), channel_id=1, source_target_pairs={{0,1},{1,0},{2,3},{3,2},{4,5},{5,4},{6,7},{7,6},{8,9},{9,8},{10,11... | collective-permute-start | bytes 1572872 | tf_op jit(solution)/shard_map/ppermute | solution.py:22
  107.6 4.7 %collective-permute-start.8 = (bf16[2,2,2,2,2,8,1024]{6,5,4,3,2,0,1:T(8,128)(2,1)S(1)}, bf16[2,2,2,2,2,8,1024]{6,5,4,3,2,0,1:T(8,128)(2,1)S(1)}, u32[]{:S(2)}, u32[]{:S(2)}) collective-permute-start(bf16[2,2,2,2,2,8,1024]{6,5,4,3,2,0,1:T(8,128)(2,1)S(1)} %bitcast.230), channel_id=1, source_target_pairs={{0,4},{1,5},{2,6},{3,7},{4,0},{5,1},{6,2},{7,3},{8,12},{9,13},{10,... | collective-permute-start | bytes 1572872 | tf_op jit(solution)/shard_map/ppermute | solution.py:22
  112.4 6.3 %collective-permute-start.5 = (bf16[2,2,2,2,2,8,1024]{6,5,4,3,2,1,0:T(8,128)(2,1)S(1)}, bf16[2,2,2,2,2,8,1024]{6,5,4,3,2,1,0:T(8,128)(2,1)S(1)}, u32[]{:S(2)}, u32[]{:S(2)}) collective-permute-start(bf16[2,2,2,2,2,8,1024]{6,5,4,3,2,1,0:T(8,128)(2,1)S(1)} %bitcast.231), channel_id=1, source_target_pairs={{0,16},{1,17},{2,18},{3,19},{4,20},{5,21},{6,22},{7,23},{8,24},{9,... | collective-permute-start | bytes 1572872 | tf_op jit(solution)/shard_map/ppermute | solution.py:22
  118.7 0.2 fusion.34
  118.9 8.9 %collective-permute-start.12 = (bf16[2,2,2,2,8,1024]{5,4,3,2,1,0:T(8,128)(2,1)S(1)}, bf16[2,2,2,2,8,1024]{5,4,3,2,1,0:T(8,128)(2,1)S(1)}, u32[]{:S(2)}, u32[]{:S(2)}) collective-permute-start(bf16[2,2,2,2,8,1024]{5,4,3,2,1,0:T(8,128)(2,1)S(1)} %slice_bitcast_fusion.6), channel_id=1, source_target_pairs={{0,16},{1,17},{2,18},{3,19},{4,20},{5,21},{6,22},{7,23},{8,24},{9,... | collective-permute-start | bytes 786440 | tf_op jit(solution)/shard_map/ppermute | solution.py:22
  127.8 0.2 fusion.35
  128.1 0.2 fusion.36
  128.4 3.7 %collective-permute-done.12 = bf16[2,2,2,2,8,1024]{5,4,3,2,1,0:T(8,128)(2,1)S(1)} collective-permute-done((bf16[2,2,2,2,8,1024]{5,4,3,2,1,0:T(8,128)(2,1)S(1)}, bf16[2,2,2,2,8,1024]{5,4,3,2,1,0:T(8,128)(2,1)S(1)}, u32[]{:S(2)}, u32[]{:S(2)}) %collective-permute-start.12) | collective-permute-done | bytes 262176 | tf_op jit(solution)/shard_map/ppermute | solution.py:22
  132.3 2.1 %collective-permute-done.9 = bf16[2,2,2,2,8,1024]{5,4,3,2,1,0:T(8,128)(2,1)S(1)} collective-permute-done((bf16[2,2,2,2,8,1024]{5,4,3,2,1,0:T(8,128)(2,1)S(1)}, bf16[2,2,2,2,8,1024]{5,4,3,2,1,0:T(8,128)(2,1)S(1)}, u32[]{:S(2)}, u32[]{:S(2)}) %collective-permute-start.9) | collective-permute-done | bytes 262176 | tf_op jit(solution)/shard_map/ppermute | solution.py:22
  134.9 2.1 %collective-permute-start.7 = (bf16[2,2,2,8,1024]{4,3,2,1,0:T(8,128)(2,1)S(1)}, bf16[2,2,2,8,1024]{4,3,2,1,0:T(8,128)(2,1)S(1)}, u32[]{:S(2)}, u32[]{:S(2)}) collective-permute-start(bf16[2,2,2,8,1024]{4,3,2,1,0:T(8,128)(2,1)S(1)} %slice_bitcast_fusion.18), channel_id=1, source_target_pairs={{0,1},{1,0},{2,3},{3,2},{4,5},{5,4},{6,7},{7,6},{8,9},{9,8},{10,11... | collective-permute-start | bytes 393224 | tf_op jit(solution)/shard_map/ppermute | solution.py:22
  137.0 0.3 collective-permute-done.13
  137.3 2.3 %collective-permute-done.10 = bf16[2,2,2,8,1024]{4,3,2,1,0:T(8,128)(2,1)S(1)} collective-permute-done((bf16[2,2,2,8,1024]{4,3,2,1,0:T(8,128)(2,1)S(1)}, bf16[2,2,2,8,1024]{4,3,2,1,0:T(8,128)(2,1)S(1)}, u32[]{:S(2)}, u32[]{:S(2)}) %collective-permute-start.10) | collective-permute-done | bytes 131104 | tf_op jit(solution)/shard_map/ppermute | solution.py:22
  139.6 0.3 collective-permute-done.7
  140.0 3.5 %collective-permute-start.14 = (bf16[2,2,8,3072]{3,2,1,0:T(8,128)(2,1)S(1)}, bf16[2,2,8,3072]{3,2,1,0:T(8,128)(2,1)S(1)}, u32[]{:S(2)}, u32[]{:S(2)}) collective-permute-start(bf16[2,2,8,3072]{3,2,1,0:T(8,128)(2,1)S(1)} %slice_bitcast_fusion.12), channel_id=1, source_target_pairs={{0,80},{1,81},{2,82},{3,83},{4,84},{5,85},{6,86},{7,87},{8,88},{9,... | collective-permute-start | bytes 589832 | tf_op jit(solution)/shard_map/ppermute | solution.py:22
  143.6 3.6 %collective-permute-done.14 = bf16[2,2,8,3072]{3,2,1,0:T(8,128)(2,1)S(1)} collective-permute-done((bf16[2,2,8,3072]{3,2,1,0:T(8,128)(2,1)S(1)}, bf16[2,2,8,3072]{3,2,1,0:T(8,128)(2,1)S(1)}, u32[]{:S(2)}, u32[]{:S(2)}) %collective-permute-start.14) | collective-permute-done | bytes 196640 | tf_op jit(solution)/shard_map/ppermute | solution.py:22
  147.4 5.8 %collective-permute-done.15 = bf16[2,8,3072]{2,1,0:T(8,128)(2,1)S(1)} collective-permute-done((bf16[2,8,3072]{2,1,0:T(8,128)(2,1)S(1)}, bf16[2,8,3072]{2,1,0:T(8,128)(2,1)S(1)}, u32[]{:S(2)}, u32[]{:S(2)}) %collective-permute-start.15) | collective-permute-done | bytes 98336 | tf_op jit(solution)/shard_map/ppermute | solution.py:22
  153.4 1.8 %fusion.33 = bf16[1,512,1024]{2,1,0:T(8,128)(2,1)} fusion(bf16[1,512,1024]{2,1,0:T(8,128)(2,1)S(1)} %copy-done.1, f32[512,1024]{1,0:T(8,128)S(1)} %get-tuple-element.116, bf16[1,512,1024]{2,1,0:T(8,128)(2,1)S(1)} %copy-done.9, f32[512]{0:T(512)S(1)} %broadcast_multiply_fusion, f32[512]{0:T(512)S(1)} %broadcast_multiply_fusion.1, f32[512]{0:T(512)S(1)} %add_rsqrt_fusion, ...), kind=kLoop, calls=%fused_computation.53 | loop fusion | flops 5242880 | bytes 5251072 | tf_op jit(solution)/shard_map/broadcast_in_dim | solution.py:206
  155.2 3.5 %collective-permute-done.16 = bf16[8,3072]{1,0:T(8,128)(2,1)S(1)} collective-permute-done((bf16[8,3072]{1,0:T(8,128)(2,1)S(1)}, bf16[8,3072]{1,0:T(8,128)(2,1)S(1)}, u32[]{:S(2)}, u32[]{:S(2)}) %collective-permute-start.16) | collective-permute-done | bytes 49184 | tf_op jit(solution)/shard_map/ppermute | solution.py:22
  158.6 0.7 convert_add_fusion.11
  (85 shorter events, 2.6 us)
Async XLA Ops:
  0.6 3.3 %copy-start = (bf16[1024,1024]{1,0:T(8,128)(2,1)S(1)}, bf16[1024,1024]{1,0:T(8,128)(2,1)}, u32[]{:S(2)}) copy-start(bf16[1024,1024]{1,0:T(8,128)(2,1)} %param.28) | copy-start | bytes 6291460
  0.6 3.3 %copy-start.1 = (bf16[1,512,1024]{2,1,0:T(8,128)(2,1)S(1)}, bf16[1,512,1024]{2,1,0:T(8,128)(2,1)}, u32[]{:S(2)}) copy-start(bf16[1,512,1024]{2,1,0:T(8,128)(2,1)} %param.23) | copy-start | bytes 3145732
  3.9 1.6 %copy-start.14 = (bf16[1024,1024]{1,0:T(8,128)(2,1)S(1)}, bf16[1024,1024]{1,0:T(8,128)(2,1)}, u32[]{:S(2)}) copy-start(bf16[1024,1024]{1,0:T(8,128)(2,1)} %param.27) | copy-start | bytes 6291460
  5.5 1.3 copy-start.7
  6.8 1.3 copy-start.8
  8.2 20.1 %collective-permute-start = (bf16[2,128,1024]{2,1,0:T(8,128)(2,1)}, bf16[2,128,1024]{2,1,0:T(8,128)(2,1)}, u32[]{:S(2)}, u32[]{:S(2)}) collective-permute-start(bf16[2,128,1024]{2,1,0:T(8,128)(2,1)} %get-tuple-element.98), channel_id=1, source_target_pairs={{0,1},{1,2},{2,3},{3,4},{4,5},{5,6},{6,7},{7,8},{8,9},{9,10},{10,1... | collective-permute-start | bytes 1572872 | tf_op jit(solution)/shard_map/ppermute | solution.py:73
  12.9 15.6 %collective-permute-start.1 = (bf16[2,128,1024]{2,1,0:T(8,128)(2,1)}, bf16[2,128,1024]{2,1,0:T(8,128)(2,1)}, u32[]{:S(2)}, u32[]{:S(2)}) collective-permute-start(bf16[2,128,1024]{2,1,0:T(8,128)(2,1)} %get-tuple-element.99), channel_id=1, source_target_pairs={{1,0},{2,1},{3,2},{4,3},{5,4},{6,5},{7,6},{8,7},{9,8},{10,9},{11,1... | collective-permute-start | bytes 1572872 | tf_op jit(solution)/shard_map/ppermute | solution.py:76
  49.3 5.4 %copy-start.2 = (bf16[512,1024]{0,1:T(8,128)(2,1)S(1)}, bf16[512,1024]{0,1:T(8,128)(2,1)}, u32[]{:S(2)}) copy-start(bf16[512,1024]{0,1:T(8,128)(2,1)} %copy.28) | copy-start | bytes 3145732
  54.7 1.4 copy-start.5
  56.1 2.3 %copy-start.12 = (f32[8,512]{1,0:T(8,128)S(1)}, f32[8,512]{1,0:T(8,128)}, u32[]{:S(2)}) copy-start(f32[8,512]{1,0:T(8,128)} %get-tuple-element.110) | copy-start | bytes 49156
  58.4 6.4 %copy-start.3 = (bf16[512,1024]{0,1:T(8,128)(2,1)S(1)}, bf16[512,1024]{0,1:T(8,128)(2,1)}, u32[]{:S(2)}) copy-start(bf16[512,1024]{0,1:T(8,128)(2,1)} %copy.27) | copy-start | bytes 3145732
  65.8 6.8 %copy-start.4 = (bf16[1,768,1024]{1,2,0:T(8,128)(2,1)S(1)}, bf16[1,768,1024]{1,2,0:T(8,128)(2,1)}, u32[]{:S(2)}) copy-start(bf16[1,768,1024]{1,2,0:T(8,128)(2,1)} %copy.26) | copy-start | bytes 4718596
  66.0 15.9 %collective-permute-start.2 = (bf16[2,128,1024]{1,2,0:T(8,128)(2,1)S(1)}, bf16[2,128,1024]{1,2,0:T(8,128)(2,1)S(1)}, u32[]{:S(2)}, u32[]{:S(2)}) collective-permute-start(bf16[2,128,1024]{1,2,0:T(8,128)(2,1)S(1)} %pad_maximum_fusion.3), channel_id=1, source_target_pairs={{1,0},{2,1},{3,2},{4,3},{5,4},{6,5},{7,6},{8,7},{9,8},{10,9},{11,1... | collective-permute-start | bytes 1572872 | tf_op jit(solution)/shard_map/ppermute | solution.py:84
  67.5 15.7 %collective-permute-start.3 = (bf16[2,128,1024]{1,2,0:T(8,128)(2,1)S(1)}, bf16[2,128,1024]{1,2,0:T(8,128)(2,1)S(1)}, u32[]{:S(2)}, u32[]{:S(2)}) collective-permute-start(bf16[2,128,1024]{1,2,0:T(8,128)(2,1)S(1)} %pad_maximum_fusion.4), channel_id=1, source_target_pairs={{0,1},{1,2},{2,3},{3,4},{4,5},{5,6},{6,7},{7,8},{8,9},{9,10},{10,1... | collective-permute-start | bytes 1572872 | tf_op jit(solution)/shard_map/ppermute | solution.py:84
  95.2 2.6 %copy-start.10 = (bf16[8,128,512]{2,1,0:T(8,128)(2,1)S(1)}, bf16[8,128,512]{2,1,0:T(8,128)(2,1)}, u32[]{:S(2)}) copy-start(bf16[8,128,512]{2,1,0:T(8,128)(2,1)} %convolution_convert_fusion.1) | copy-start | bytes 3145732
  95.2 2.9 %copy-start.13 = (bf16[1024,1024]{1,0:T(8,128)(2,1)S(1)}, bf16[1024,1024]{1,0:T(8,128)(2,1)}, u32[]{:S(2)}) copy-start(bf16[1024,1024]{1,0:T(8,128)(2,1)} %param.26) | copy-start | bytes 6291460
  97.4 1.9 %copy-start.11 = (bf16[512,1024]{0,1:T(8,128)(2,1)S(1)}, bf16[512,1024]{0,1:T(8,128)(2,1)}, u32[]{:S(2)}) copy-start(bf16[512,1024]{0,1:T(8,128)(2,1)} %convert_element_type.241) | copy-start | bytes 3145732
  97.4 2.0 %copy-start.15 = (bf16[1024,1024]{1,0:T(8,128)(2,1)S(1)}, bf16[1024,1024]{1,0:T(8,128)(2,1)}, u32[]{:S(2)}) copy-start(bf16[1024,1024]{1,0:T(8,128)(2,1)} %param.27) | copy-start | bytes 6291460
  97.4 6.0 %collective-permute-start.4 = (bf16[512,3072]{1,0:T(8,128)(2,1)S(1)}, bf16[512,3072]{1,0:T(8,128)(2,1)S(1)}, u32[]{:S(2)}, u32[]{:S(2)}) collective-permute-start(bf16[512,3072]{1,0:T(8,128)(2,1)S(1)} %slice.318), channel_id=1, source_target_pairs={{0,32},{1,33},{2,34},{3,35},{4,36},{5,37},{6,38},{7,39},{8,40},{9,... | collective-permute-start | bytes 9437192 | tf_op jit(solution)/shard_map/ppermute | solution.py:22
  99.5 1.3 copy-start.6
  99.5 4.0 %slice-start = ((s8[6291456]{0:T(1024)(128)(4,1)}), s8[4194304]{0:T(1024)(128)(4,1)S(1)}, s32[]{:S(2)}) async-start(s8[6291456]{0:T(1024)(128)(4,1)} %bitcast.212), calls=%async_computation | async-start | bytes 8388608
  100.8 2.7 %slice-start.1 = ((s8[6291456]{0:T(1024)(128)(4,1)}), s8[2097152]{0:T(1024)(128)(4,1)S(1)}, s32[]{:S(2)}) async-start(s8[6291456]{0:T(1024)(128)(4,1)} %bitcast.212), calls=%async_computation.1 | async-start | bytes 4194304
  104.9 13.8 %collective-permute-start.11 = (bf16[2,2,2,2,2,8,1024]{6,5,4,3,2,1,0:T(8,128)(2,1)S(1)}, bf16[2,2,2,2,2,8,1024]{6,5,4,3,2,1,0:T(8,128)(2,1)S(1)}, u32[]{:S(2)}, u32[]{:S(2)}) collective-permute-start(bf16[2,2,2,2,2,8,1024]{6,5,4,3,2,1,0:T(8,128)(2,1)S(1)} %slice_bitcast_fusion), channel_id=1, source_target_pairs={{0,1},{1,0},{2,3},{3,2},{4,5},{5,4},{6,7},{7,6},{8,9},{9,8},{10,11... | collective-permute-start | bytes 1572872 | tf_op jit(solution)/shard_map/ppermute | solution.py:22
  107.6 20.2 %collective-permute-start.8 = (bf16[2,2,2,2,2,8,1024]{6,5,4,3,2,0,1:T(8,128)(2,1)S(1)}, bf16[2,2,2,2,2,8,1024]{6,5,4,3,2,0,1:T(8,128)(2,1)S(1)}, u32[]{:S(2)}, u32[]{:S(2)}) collective-permute-start(bf16[2,2,2,2,2,8,1024]{6,5,4,3,2,0,1:T(8,128)(2,1)S(1)} %bitcast.230), channel_id=1, source_target_pairs={{0,4},{1,5},{2,6},{3,7},{4,0},{5,1},{6,2},{7,3},{8,12},{9,13},{10,... | collective-permute-start | bytes 1572872 | tf_op jit(solution)/shard_map/ppermute | solution.py:22
  112.4 15.7 %collective-permute-start.5 = (bf16[2,2,2,2,2,8,1024]{6,5,4,3,2,1,0:T(8,128)(2,1)S(1)}, bf16[2,2,2,2,2,8,1024]{6,5,4,3,2,1,0:T(8,128)(2,1)S(1)}, u32[]{:S(2)}, u32[]{:S(2)}) collective-permute-start(bf16[2,2,2,2,2,8,1024]{6,5,4,3,2,1,0:T(8,128)(2,1)S(1)} %bitcast.231), channel_id=1, source_target_pairs={{0,16},{1,17},{2,18},{3,19},{4,20},{5,21},{6,22},{7,23},{8,24},{9,... | collective-permute-start | bytes 1572872 | tf_op jit(solution)/shard_map/ppermute | solution.py:22
  118.9 13.2 %collective-permute-start.12 = (bf16[2,2,2,2,8,1024]{5,4,3,2,1,0:T(8,128)(2,1)S(1)}, bf16[2,2,2,2,8,1024]{5,4,3,2,1,0:T(8,128)(2,1)S(1)}, u32[]{:S(2)}, u32[]{:S(2)}) collective-permute-start(bf16[2,2,2,2,8,1024]{5,4,3,2,1,0:T(8,128)(2,1)S(1)} %slice_bitcast_fusion.6), channel_id=1, source_target_pairs={{0,16},{1,17},{2,18},{3,19},{4,20},{5,21},{6,22},{7,23},{8,24},{9,... | collective-permute-start | bytes 786440 | tf_op jit(solution)/shard_map/ppermute | solution.py:22
  128.0 6.5 %collective-permute-start.9 = (bf16[2,2,2,2,8,1024]{5,4,3,2,1,0:T(8,128)(2,1)S(1)}, bf16[2,2,2,2,8,1024]{5,4,3,2,1,0:T(8,128)(2,1)S(1)}, u32[]{:S(2)}, u32[]{:S(2)}) collective-permute-start(bf16[2,2,2,2,8,1024]{5,4,3,2,1,0:T(8,128)(2,1)S(1)} %slice_bitcast_fusion.8), channel_id=1, source_target_pairs={{0,1},{1,0},{2,3},{3,2},{4,5},{5,4},{6,7},{7,6},{8,9},{9,8},{10,11... | collective-permute-start | bytes 786440 | tf_op jit(solution)/shard_map/ppermute | solution.py:22
  128.3 6.5 %collective-permute-start.6 = (bf16[2,2,2,2,8,1024]{5,4,3,2,1,0:T(8,128)(2,1)S(1)}, bf16[2,2,2,2,8,1024]{5,4,3,2,1,0:T(8,128)(2,1)S(1)}, u32[]{:S(2)}, u32[]{:S(2)}) collective-permute-start(bf16[2,2,2,2,8,1024]{5,4,3,2,1,0:T(8,128)(2,1)S(1)} %slice_bitcast_fusion.10), channel_id=1, source_target_pairs={{0,4},{1,5},{2,6},{3,7},{4,0},{5,1},{6,2},{7,3},{8,12},{9,13},{10,... | collective-permute-start | bytes 786440 | tf_op jit(solution)/shard_map/ppermute | solution.py:22
  132.2 5.0 %collective-permute-start.13 = (bf16[2,2,2,8,1024]{4,3,2,1,0:T(8,128)(2,1)S(1)}, bf16[2,2,2,8,1024]{4,3,2,1,0:T(8,128)(2,1)S(1)}, u32[]{:S(2)}, u32[]{:S(2)}) collective-permute-start(bf16[2,2,2,8,1024]{4,3,2,1,0:T(8,128)(2,1)S(1)} %slice_bitcast_fusion.14), channel_id=1, source_target_pairs={{0,4},{1,5},{2,6},{3,7},{4,0},{5,1},{6,2},{7,3},{8,12},{9,13},{10,... | collective-permute-start | bytes 393224 | tf_op jit(solution)/shard_map/ppermute | solution.py:22
  134.6 5.0 %collective-permute-start.10 = (bf16[2,2,2,8,1024]{4,3,2,1,0:T(8,128)(2,1)S(1)}, bf16[2,2,2,8,1024]{4,3,2,1,0:T(8,128)(2,1)S(1)}, u32[]{:S(2)}, u32[]{:S(2)}) collective-permute-start(bf16[2,2,2,8,1024]{4,3,2,1,0:T(8,128)(2,1)S(1)} %slice_bitcast_fusion.16), channel_id=1, source_target_pairs={{0,16},{1,17},{2,18},{3,19},{4,20},{5,21},{6,22},{7,23},{8,24},{9,... | collective-permute-start | bytes 393224 | tf_op jit(solution)/shard_map/ppermute | solution.py:22
  134.9 18.5 %copy-start.9 = (bf16[1,512,1024]{2,1,0:T(8,128)(2,1)S(1)}, bf16[1,512,1024]{2,1,0:T(8,128)(2,1)}, u32[]{:S(2)}) copy-start(bf16[1,512,1024]{2,1,0:T(8,128)(2,1)} %param.24) | copy-start | bytes 3145732
  134.9 5.0 %collective-permute-start.7 = (bf16[2,2,2,8,1024]{4,3,2,1,0:T(8,128)(2,1)S(1)}, bf16[2,2,2,8,1024]{4,3,2,1,0:T(8,128)(2,1)S(1)}, u32[]{:S(2)}, u32[]{:S(2)}) collective-permute-start(bf16[2,2,2,8,1024]{4,3,2,1,0:T(8,128)(2,1)S(1)} %slice_bitcast_fusion.18), channel_id=1, source_target_pairs={{0,1},{1,0},{2,3},{3,2},{4,5},{5,4},{6,7},{7,6},{8,9},{9,8},{10,11... | collective-permute-start | bytes 393224 | tf_op jit(solution)/shard_map/ppermute | solution.py:22
  140.0 7.2 %collective-permute-start.14 = (bf16[2,2,8,3072]{3,2,1,0:T(8,128)(2,1)S(1)}, bf16[2,2,8,3072]{3,2,1,0:T(8,128)(2,1)S(1)}, u32[]{:S(2)}, u32[]{:S(2)}) collective-permute-start(bf16[2,2,8,3072]{3,2,1,0:T(8,128)(2,1)S(1)} %slice_bitcast_fusion.12), channel_id=1, source_target_pairs={{0,80},{1,81},{2,82},{3,83},{4,84},{5,85},{6,86},{7,87},{8,88},{9,... | collective-permute-start | bytes 589832 | tf_op jit(solution)/shard_map/ppermute | solution.py:22
  147.3 5.9 %collective-permute-start.15 = (bf16[2,8,3072]{2,1,0:T(8,128)(2,1)S(1)}, bf16[2,8,3072]{2,1,0:T(8,128)(2,1)S(1)}, u32[]{:S(2)}, u32[]{:S(2)}) collective-permute-start(bf16[2,8,3072]{2,1,0:T(8,128)(2,1)S(1)} %slice_bitcast_fusion.20), channel_id=1, source_target_pairs={{0,12},{1,13},{2,14},{3,15},{4,8},{5,9},{6,10},{7,11},{8,4},{9,5},... | collective-permute-start | bytes 294920 | tf_op jit(solution)/shard_map/ppermute | solution.py:22
  153.3 5.4 %collective-permute-start.16 = (bf16[8,3072]{1,0:T(8,128)(2,1)S(1)}, bf16[8,3072]{1,0:T(8,128)(2,1)S(1)}, u32[]{:S(2)}, u32[]{:S(2)}) collective-permute-start(bf16[8,3072]{1,0:T(8,128)(2,1)S(1)} %slice_bitcast_fusion.22), channel_id=1, source_target_pairs={{0,3},{1,2},{2,1},{3,0},{4,7},{5,6},{6,5},{7,4},{8,11},{9,10},{10,... | collective-permute-start | bytes 147464 | tf_op jit(solution)/shard_map/ppermute | solution.py:22

commit v2 on v1

v2 whole, which is shorter than its diff:
```python
import functools
import math

import jax
import jax.numpy as jnp
from jax import lax
from jax.experimental import pallas as pl
from jax.experimental.pallas import tpu as pltpu
from jax.sharding import PartitionSpec as P

HEADS = 8
WIN = 128
HDIM = 128
ROWS = 512
D = 1024
PAIR = 2 * HDIM
STEPS = HEADS // 2
epsilon = 1e-05
masked_value = -1e30
F32 = jnp.float32
BF16 = jnp.bfloat16

AXES = ("rec", "tm")
CORE = 32
NEAR = ((16, 4, 1), (80, 12, 3))


def order_of(core):
    return NEAR[core] + NEAR[1 - core]


def exchange(value, masks):
    count = lax.axis_size(AXES)
    pairs = [(i, i ^ masks[(i // CORE) % 2]) for i in range(count)]
    return lax.ppermute(value, AXES, pairs)


def coordinates(device, core):
    high = [(device >> bit) & 1 for bit in (6, 3, 1)]
    low = [(device >> bit) & 1 for bit in (4, 2, 0)]
    return high if core == 0 else [a ^ b for a, b in zip(high, low)]


def row_targets(me):
    row = jnp.arange(1024, dtype=jnp.int32)
    far = (row >> 9) & 1
    core = ((me // CORE) % 2) ^ far
    target = me ^ (far * CORE)
    for bit in range(6):
        mask = jnp.where(core == 0, order_of(0)[bit], order_of(1)[bit])
        move = (row >> (8 - bit)) & 1
        if bit >= 3:
            move = move ^ jnp.where(core == 0, coordinates(me, 0)[bit - 3], coordinates(me, 1)[bit - 3])
        target = target ^ (move * mask)
    return target * 8 + (row & 7)


def last_groups():
    groups = []
    for device in range(128):
        core = (device // CORE) % 2
        if not any(coordinates(device, core)):
            one, two, three = order_of(core)[3:]
            groups.append([device ^ (a * one) ^ (b * two) ^ (c * three) for a in (0, 1) for b in (0, 1) for c in (0, 1)])
    return groups


def halves(value, dim):
    return lax.index_in_dim(value, 0, dim, False), lax.index_in_dim(value, 1, dim, False)


def add(a, b):
    return (a.astype(jnp.float32) + b.astype(jnp.float32)).astype(jnp.bfloat16)


def scatter_sum(parts, beside):
    masks = list(zip(order_of(0), order_of(1)))
    values = [part.reshape(2, 2, 2, 8, 8, -1) for part in parts]
    left = [[0, 1, 2] for _ in values]
    other = None
    for step in range(3):
        sent = []
        for part in range(3):
            bit = (part + step) % 3
            keep, send = halves(values[part], left[part].index(bit))
            left[part].remove(bit)
            sent.append((keep, exchange(send, masks[bit])))
        if step < len(beside):
            other = beside[step](values[0], other)
        values = [add(keep, got) for keep, got in sent]
        if step < len(beside):
            *values, other = lax.optimization_barrier((*values, other))
    value = jnp.concatenate(values, -1)
    got = lax.all_to_all(value, AXES, 0, 0, axis_index_groups=last_groups(), tiled=True)
    return jnp.sum(got.astype(jnp.float32), 0), other


def dot(a, b):
    return lax.dot_general(a, b, (((1,), (0,)), ((), ())), preferred_element_type=F32)


def dot_nt(a, b):
    return lax.dot_general(a, b, (((1,), (1,)), ((), ())), preferred_element_type=F32)


def dot_tn(a, b):
    return lax.dot_general(a, b, (((0,), (0,)), ((), ())), preferred_element_type=F32)


def normalize(rows):
    values = rows.astype(F32)
    center = values - jnp.mean(values, -1, keepdims=True)
    inverse = lax.rsqrt(jnp.mean(center * center, -1, keepdims=True) + epsilon)
    return center * inverse, inverse


def call(body, outs, ins, in_specs, out_specs, scratch, macs, steps=STEPS, room=30):
    size = sum(math.prod(x.shape) * x.dtype.itemsize for x in (*ins, *jax.tree.leaves(outs)))
    return pl.pallas_call(
        body,
        out_shape=outs,
        grid=(steps,),
        in_specs=in_specs,
        out_specs=out_specs,
        scratch_shapes=scratch,
        compiler_params=pltpu.CompilerParams(vmem_limit_bytes=room * 2**20),
        cost_estimate=pl.CostEstimate(flops=2 * macs, bytes_accessed=size, transcendentals=0),
    )(*ins)


def whole(*shape):
    return pl.BlockSpec(shape, lambda j: (0,) * len(shape))


def columns(rows):
    return pl.BlockSpec((rows, PAIR), lambda j: (0, j))


SCALAR = pl.BlockSpec(memory_space=pltpu.SMEM)


def one_hot(target):
    lane = lax.broadcasted_iota(jnp.int32, (target.shape[0], D), 1)
    return jnp.where(lane == target, 1.0, 0.0).astype(BF16)


def front_body(place, target, frames, grads, w_query, w_key, w_value, w_out, ordered, query, keys, values, d_mixed, hidden, masked):
    @pl.when(pl.program_id(0) == 0)
    def _():
        hidden[...] = normalize(frames[...])[0].astype(BF16)
        row = lax.broadcasted_iota(jnp.int32, (ROWS, D), 0) + place[0]
        masked[...] = jnp.where(row < place[1], grads[...].astype(F32), 0.0).astype(BF16)

    rows = hidden[...]
    query[...] = dot(rows, w_query[...]).astype(BF16)
    keys[...] = dot(rows, w_key[...]).astype(BF16)
    values[...] = dot(rows, w_value[...]).astype(BF16)
    d_mixed[...] = dot_nt(masked[...], w_out[...]).astype(BF16)
    ordered[...] = dot_nt(one_hot(target[...]), rows).astype(BF16)


def front(place, target, frames, grads, w_query, w_key, w_value, w_out):
    wide = jax.ShapeDtypeStruct((ROWS, D), BF16)
    return call(
        front_body,
        [jax.ShapeDtypeStruct((D, ROWS), BF16), wide, wide, wide, wide],
        (place, target, frames, grads, w_query, w_key, w_value, w_out),
        [SCALAR, pl.BlockSpec((PAIR, 1), lambda j: (j, 0)), whole(ROWS, D), whole(ROWS, D)]
        + [columns(D)] * 3
        + [pl.BlockSpec((PAIR, D), lambda j: (j, 0))],
        [pl.BlockSpec((PAIR, ROWS), lambda j: (j, 0))] + [columns(ROWS)] * 4,
        [pltpu.VMEM((ROWS, D), BF16)] * 2,
        5 * ROWS * D * D,
        room=60,
    )


def attend_body(
    place, target, low, high, ordered, query, keys, values, d_mixed, w_key, w_value,
    grad_query, grad_key, grad_value, kept, sent, sides,
    ordered_border, hidden_border, key_value, key_t, pair, score_t, prob_t, border_grads, total,
):
    scale = HDIM ** (-0.5)
    blocks = ROWS // WIN
    row = lax.broadcasted_iota(jnp.int32, (WIN, WIN), 0)
    eye = jnp.where(lax.broadcasted_iota(jnp.int32, (WIN, WIN), 1) == row, 1.0, 0.0).astype(BF16)

    @pl.when(pl.program_id(0) == 0)
    def _():
        hidden_border[:WIN] = normalize(low[...])[0].astype(BF16)
        hidden_border[WIN:] = normalize(high[...])[0].astype(BF16)
        for part in range(4):
            rows = slice(part * PAIR, (part + 1) * PAIR)
            ordered_border[rows] = dot_nt(one_hot(target[rows]), hidden_border[...]).astype(BF16)
        for ref in (pair, score_t, prob_t):
            ref[...] = jnp.zeros_like(ref)
        total[...] = jnp.zeros_like(total)

    key_border = dot(hidden_border[...], w_key[...]).astype(BF16)
    value_border = dot(hidden_border[...], w_value[...]).astype(BF16)
    above = lax.broadcasted_iota(jnp.int32, (3 * WIN, WIN), 0)
    lane = lax.broadcasted_iota(jnp.int32, (1, WIN), 1)

    def lay_out(head):
        cols = slice(head * HDIM, (head + 1) * HDIM)
        for side, own, to in ((key_border, keys, slice(0, HDIM)), (value_border, values, slice(HDIM, PAIR))):
            key_value[head, :WIN, to] = side[:WIN, cols]
            key_value[head, WIN : WIN + ROWS, to] = own[:, cols]
            key_value[head, WIN + ROWS :, to] = side[WIN:, cols]
        key_t[head] = dot_nt(eye, key_value[head, :, :HDIM]).astype(BF16)
        for i in range(blocks):
            mine = slice(i * WIN, (i + 1) * WIN)
            pair[head, i * PAIR : i * PAIR + WIN, :HDIM] = query[mine, cols]
            pair[head, i * PAIR + WIN : (i + 1) * PAIR, HDIM:] = d_mixed[mine, cols]

    def products(head, i):
        return dot_nt(key_value[head, i * WIN : (i + 3) * WIN], pair[head, i * PAIR : (i + 1) * PAIR])

    def soften(head, i, both):
        mine = slice(i * WIN, (i + 1) * WIN)
        reach = slice(i * WIN, (i + 3) * WIN)
        first = (1 - i) * WIN - place[0]
        last = place[1] - place[0] + (1 - i) * WIN - 1
        allowed = (above >= jnp.maximum(lane, first)) & (above <= jnp.minimum(lane + 2 * WIN, last))
        scores = jnp.where(allowed, both[:, :WIN], masked_value)
        d_prob = both[:, WIN:]
        row_max = jnp.max(scores, 0, keepdims=True)
        expo = jnp.exp2((scores - row_max) * (scale * math.log2(math.e)))
        inverse_sum = 1.0 / jnp.sum(expo, 0, keepdims=True)
        row_delta = jnp.sum(expo * d_prob, 0, keepdims=True) * inverse_sum
        score_t[head, reach, mine] = (expo * (inverse_sum * scale) * (d_prob - row_delta)).astype(BF16)
        prob_t[head, reach, mine] = (expo * inverse_sum).astype(BF16)

    def query_grads(head, part):
        cols = slice(head * HDIM, (head + 1) * HDIM)
        mine = slice(part * PAIR, (part + 1) * PAIR)
        reach = slice(part * PAIR, part * PAIR + 2 * PAIR)
        grad_t = dot(key_t[head, :, reach], score_t[head, reach, mine]).astype(BF16)
        for half in (slice(0, WIN), slice(WIN, PAIR)):
            rows = slice(part * PAIR + half.start, part * PAIR + half.stop)
            grad_query[rows, cols] = dot_nt(eye, grad_t[:, half]).astype(BF16)

    def key_grads(head, part):
        cols = slice(head * HDIM, (head + 1) * HDIM)
        here = slice(part * PAIR, (part + 1) * PAIR)
        near = slice(max(0, part - 1) * PAIR, min(2, part + 1) * PAIR)
        g_key = dot(score_t[head, here, near], query[near, cols]).astype(BF16)
        g_value = dot(prob_t[head, here, near], d_mixed[near, cols]).astype(BF16)
        if part == 0:
            border_grads[0, :WIN, cols], border_grads[1, :WIN, cols] = g_key[:WIN], g_value[:WIN]
            grad_key[:WIN, cols], grad_value[:WIN, cols] = g_key[WIN:], g_value[WIN:]
        elif part == 1:
            grad_key[WIN : WIN + PAIR, cols], grad_value[WIN : WIN + PAIR, cols] = g_key, g_value
        else:
            grad_key[ROWS - WIN :, cols], grad_value[ROWS - WIN :, cols] = g_key[:WIN], g_value[:WIN]
            border_grads[0, WIN:, cols], border_grads[1, WIN:, cols] = g_key[WIN:], g_value[WIN:]

    lay_out(0)
    lay_out(1)
    first = [products(0, i) for i in range(blocks)]
    second = []
    for i in range(blocks):
        soften(0, i, first[i])
        second.append(products(1, i))
    jobs = [(query_grads, 0), (query_grads, 1), (key_grads, 0), (key_grads, 1), (key_grads, 2)]
    for i in range(blocks):
        soften(1, i, second[i])
        for job, part in jobs[i : i + 1] if i < 3 else jobs[3:]:
            job(0, part)
    for job, part in jobs:
        job(1, part)
    half = D // 2
    for out, rows in ((sent, slice(half, D)), (kept, slice(0, half))):
        out[0] = dot(ordered[rows], grad_query[...]).astype(BF16)
        out[1] = (dot(ordered[rows], grad_key[...]) + dot(ordered_border[rows], border_grads[0])).astype(BF16)
        out[2] = (dot(ordered[rows], grad_value[...]) + dot(ordered_border[rows], border_grads[1])).astype(BF16)
    total[...] += dot_nt(border_grads[0], w_key[...]) + dot_nt(border_grads[1], w_value[...])

    @pl.when(pl.program_id(0) == STEPS - 1)
    def _():
        sides[...] = total[...].astype(BF16)


def attend(place, target, low, high, ordered, query, keys, values, d_mixed, w_key, w_value):
    own = jax.ShapeDtypeStruct((ROWS, D), BF16)
    half = jax.ShapeDtypeStruct((3, D // 2, D), BF16)
    reach = ROWS + 2 * WIN
    return call(
        attend_body,
        [own] * 3 + [half] * 2 + [jax.ShapeDtypeStruct((2 * WIN, D), BF16)],
        (place, target, low, high, ordered, query, keys, values, d_mixed, w_key, w_value),
        [SCALAR, whole(D, 1), whole(WIN, D), whole(WIN, D), whole(D, ROWS)] + [columns(ROWS)] * 4 + [columns(D)] * 2,
        [columns(ROWS)] * 3 + [pl.BlockSpec((3, D // 2, PAIR), lambda j: (0, 0, j))] * 2 + [whole(2 * WIN, D)],
        [
            pltpu.VMEM((D, 2 * WIN), BF16),
            pltpu.VMEM((2 * WIN, D), BF16),
            pltpu.VMEM((2, reach, PAIR), BF16),
            pltpu.VMEM((2, HDIM, reach), BF16),
            pltpu.VMEM((2, 2 * ROWS, PAIR), BF16),
            pltpu.VMEM((2, reach, ROWS), BF16),
            pltpu.VMEM((2, reach, ROWS), BF16),
            pltpu.VMEM((2, 2 * WIN, PAIR), BF16),
            pltpu.VMEM((2 * WIN, D), F32),
        ],
        D * D * (ROWS * 3 + WIN * 12) + 10 * 4 * 3 * HEADS * WIN**3,
    )


def back_body(grad_query, grad_key, grad_value, w_query, w_key, w_value, total):
    part = dot_nt(grad_query[...], w_query[...]) + dot_nt(grad_key[...], w_key[...]) + dot_nt(grad_value[...], w_value[...])

    @pl.when(pl.program_id(0) == 0)
    def _():
        total[...] = part

    @pl.when(pl.program_id(0) > 0)
    def _():
        total[...] += part


def back(*ins):
    return call(
        back_body,
        jax.ShapeDtypeStruct((ROWS, D), F32),
        ins,
        [columns(ROWS)] * 3 + [columns(D)] * 3,
        whole(ROWS, D),
        [],
        3 * ROWS * D * D,
    )


def finish_body(frames, grads, d_hidden, near, out):
    normed, inverse = normalize(frames[...])
    part = pl.program_id(0)
    inner = jnp.logical_and(part > 0, part < STEPS - 1)
    d_rows = d_hidden[...] + jnp.where(inner, 0.0, near[...].astype(F32))
    mean_grad = jnp.mean(d_rows, -1, keepdims=True)
    mean_cross = jnp.mean(d_rows * normed, -1, keepdims=True)
    out[...] = (grads[...].astype(F32) + inverse * (d_rows - mean_grad - normed * mean_cross)).astype(BF16)


def finish(frames, grads, d_hidden, near):
    block = pl.BlockSpec((WIN, D), lambda j: (j, 0))
    return call(
        finish_body,
        jax.ShapeDtypeStruct((ROWS, D), BF16),
        (frames, grads, d_hidden, near),
        [block] * 3 + [pl.BlockSpec((WIN, D), lambda j: (j // (STEPS - 1), 0))],
        block,
        [],
        ROWS * D * 16,
    )


def swap_borders(first, last):
    count = lax.axis_size("tm")
    even = lax.axis_index("tm") % 2 == 0
    one = [(i, i ^ 1) for i in range(count)]
    two = [(i, i + 1 if i % 2 else i - 1) for i in range(1, count - 1)]
    a = lax.ppermute(jnp.where(even, last, first), "tm", one)
    b = lax.ppermute(jnp.where(even, first, last), "tm", two)
    return jnp.where(even, b, a), jnp.where(even, a, b)


def shards(frames, cotangent, lengths, w_query, w_key, w_value, w_out):
    rows, grads = frames[0], cotangent[0]
    low, high = swap_borders(rows[:WIN], rows[ROWS - WIN :])
    place = jnp.stack([lax.axis_index("tm") * ROWS, lengths[0]]).astype(jnp.int32)
    target = row_targets(lax.axis_index(AXES))[:, None]
    ordered, query, keys, values, d_mixed = front(place, target, rows, grads, w_query, w_key, w_value, w_out)
    grad_query, grad_key, grad_value, kept, sent, sides = attend(
        place, target, low, high, ordered, query, keys, values, d_mixed, w_key, w_value
    )
    got = exchange(sent, (CORE, CORE))
    from_low, from_high = swap_borders(sides[:WIN], sides[WIN:])
    own = add(kept, got)

    def first(after, _):
        query_now, _ = lax.optimization_barrier((grad_query, after))
        return back(query_now, grad_key, grad_value, w_query, w_key, w_value)

    def second(after, d_hidden):
        near, _ = lax.optimization_barrier((jnp.concatenate([from_low, from_high]), after))
        return finish(rows, grads, d_hidden, near)

    weight_part, grad_frames = scatter_sum([own[0], own[1], own[2]], (first, second))
    return (grad_frames[None], weight_part)


def solution(mesh):
    placed = (P("rec", "tm", None), P("rec", "tm", None), P("rec"), P(), P(), P(), P())
    return jax.shard_map(
        shards,
        mesh=mesh,
        in_specs=placed,
        out_specs=(P("rec", "tm", None), P(("rec", "tm"), None)),
        check_vma=False,
    )
```

time: 160 us -> 114 us (0.71)
  matrix products: 49.8 us -> 0 us
  Pallas kernels: 0 us -> 41.9 us
  waiting for transfers between devices: 29.3 us -> 12.1 us
  blocking collectives: 0 us -> 16.1 us
  starting transfers between devices: 41.7 us -> 27.2 us
  other arithmetic: 20 us -> 6.68 us
  local copies, waits for them, and re-layouts: 16.6 us -> 8.2 us
    pallas_call x0 -> x4, Pallas kernels: none -> 41.9 us  [call(): pl.pallas_call(body, out_shape=outs, grid=(steps,), in_specs=in_specs, ou...]
    dot_general x13 -> x0, matrix products: 38.1 us -> none  [the longest x1 9.38 us: shards(): jnp.einsum('tf,tg->fg', ordered, projected, preferred_element_type=jnp.fl...]
    all_to_all x0 -> x1, blocking collectives: none -> 16.1 us  [scatter_sum(): lax.all_to_all(value, AXES, 0, 0, axis_index_groups=last_groups(), tiled=...]
    sub x1 -> x0, matrix products: 11.6 us -> none  [attend(): expo = jnp.exp(scores - row_max[:, :, None])]
    ppermute x13 -> x10, starting transfers between devices: 29 us -> 17.5 us  [exchange(): return lax.ppermute(value, AXES, pairs)]
    ppermute x13 -> x10, waiting for transfers between devices: 22.5 us -> 11.2 us  [exchange(): return lax.ppermute(value, AXES, pairs)]
    convert_element_type x5 -> x0, other arithmetic: 7.86 us -> none  [the longest x1 5.4 us: attend(): prob_b = prob.astype(jnp.bfloat16)]
    unnamed x37 -> x25, local copies, waits for them, and re-layouts: 1.35 us -> 7.77 us
  transfers between devices with their start and end apart: 17 -> 14, of which waited for: 13 -> 8; matrix products, arithmetic and copies ran while one was open for 15% -> 3% of each run, Pallas kernels for 0% -> 17%
where the time goes in v2:
time: 114 us
  Pallas kernels  41.9 us (37%)
  starting transfers between devices  27.2 us (24%)
  blocking collectives  16.1 us (14%)
  waiting for transfers between devices  12.1 us (11%)
  local copies, waits for them, and re-layouts  8.2 us (7%)
  other arithmetic  6.68 us (6%)
  between operations  1.65 us (1%)
    pallas_call x4, Pallas kernels, call(): pl.pallas_call(body, out_shape=outs, grid=(steps,), in_specs=in_specs, ou...  41.9 us
    ppermute x10, starting transfers between devices, exchange(): return lax.ppermute(value, AXES, pairs)  17.5 us
    all_to_all x1, blocking collectives, scatter_sum(): lax.all_to_all(value, AXES, 0, 0, axis_index_groups=last_groups(), tiled=...  16.1 us
    ppermute x10, waiting for transfers between devices, exchange(): return lax.ppermute(value, AXES, pairs)  11.2 us
    ppermute x2, starting transfers between devices, swap_borders(): a = lax.ppermute(jnp.where(even, last, first), 'tm', one)  8.35 us
    unnamed x25, local copies, waits for them, and re-layouts  7.77 us
    convert_element_type x10, other arithmetic, add(): return (a.astype(jnp.float32) + b.astype(jnp.float32)).astype(jnp.bfloat16)  2.48 us
  transfers between devices with their start and end apart: 14, of which 8 were waited for; matrix products, arithmetic and copies ran while one was open for 3% of the time, Pallas kernels for 17%

profile of v2, /device:TPU:0, one launch (start us, length us, event | category | flops | bytes accessed | tf_op | source)
XLA Modules:
  0.0 113.7 jit_solution(16792861479028185051)
XLA Ops:
  0.6 1.1 select_bitcast_fusion
  1.7 2.1 %collective-permute-start.1 = (bf16[128,1024]{1,0:T(8,128)(2,1)S(1)}, bf16[128,1024]{1,0:T(8,128)(2,1)S(1)}, u32[]{:S(2)}, u32[]{:S(2)}) collective-permute-start(bf16[128,1024]{1,0:T(8,128)(2,1)S(1)} %get-tuple-element.48), channel_id=1, source_target_pairs={{0,1},{1,0},{2,3},{3,2},{4,5},{5,4},{6,7},{7,6},{8,9},{9,8},{10,11... | collective-permute-start | bytes 786440 | tf_op jit(solution)/shard_map/ppermute | solution.py:361
  3.8 0.7 collective-permute-start
  5.2 0.7 pad_add_fusion.place
  5.8 1.6 %and_add_fusion.target = s32[1024,1]{1,0:T(8,128)} fusion(s32[]{:T(128)S(6)} %xor.138, s32[]{:T(128)S(6)} %and.133, s32[]{:T(128)S(6)} %xor.135, s32[]{:T(128)S(6)} %and.130, s32[]{:T(128)S(6)} %xor.132, s32[]{:T(128)S(6)} %and.127, s32[]{:T(128)S(6)} %select_n.154, s32[]{:T(128)S(6)} %add.52), kind=kLoop, calls=%fused_computation.19 | loop fusion | flops 46080 | bytes 4128 | tf_op jit(solution)/shard_map/add | solution.py:55
  7.4 0.0 copy-start.2
  7.4 0.0 copy-start.4
  7.4 10.8 %shard_map.86 = (bf16[1024,512]{1,0:T(8,128)(2,1)}, bf16[512,1024]{1,0:T(8,128)(2,1)}, bf16[512,1024]{1,0:T(8,128)(2,1)}, bf16[512,1024]{1,0:T(8,128)(2,1)}, bf16[512,1024]{1,0:T(8,128)(2,1)}) custom-call(s32[2]{0:T(128)} %pad_add_fusion.place, s32[1024,1]{1,0:T(8,128)} %and_add_fusion.target, bf16[512,1024]{1,0:T(8,128)(2,1)} %bitcast.60, ...), custom_call_target="tpu_custom_call" | custom-call | flops 5368709120 | bytes 15732744 | tf_op jit(solution)/shard_map/pallas_call | solution.py:119
  18.2 0.0 collective-permute-done.1
  18.2 0.0 collective-permute-done
  18.3 0.0 copy-done.2
  18.3 0.0 copy-done.4
  18.3 0.0 copy-done.6
  18.3 0.0 copy-start.5
  18.3 1.6 %copy-done.5 = bf16[1024,1024]{1,0:T(8,128)(2,1)S(1)} copy-done((bf16[1024,1024]{1,0:T(8,128)(2,1)S(1)}, bf16[1024,1024]{1,0:T(8,128)(2,1)}, u32[]{:S(2)}) %copy-start.5) | copy-done | bytes 2097176
  19.9 1.2 %copy-done.7 = bf16[1024,512]{1,0:T(8,128)(2,1)S(1)} copy-done((bf16[1024,512]{1,0:T(8,128)(2,1)S(1)}, bf16[1024,512]{1,0:T(8,128)(2,1)}, u32[]{:S(2)}) %copy-start.7) | copy-done | bytes 1048600
  21.1 1.2 %copy-done.8 = bf16[512,1024]{1,0:T(8,128)(2,1)S(1)} copy-done((bf16[512,1024]{1,0:T(8,128)(2,1)S(1)}, bf16[512,1024]{1,0:T(8,128)(2,1)}, u32[]{:S(2)}) %copy-start.8) | copy-done | bytes 1048600
  22.4 1.2 %copy-done.9 = bf16[512,1024]{1,0:T(8,128)(2,1)S(1)} copy-done((bf16[512,1024]{1,0:T(8,128)(2,1)S(1)}, bf16[512,1024]{1,0:T(8,128)(2,1)}, u32[]{:S(2)}) %copy-start.9) | copy-done | bytes 1048600
  23.6 1.2 %copy-done.10 = bf16[512,1024]{1,0:T(8,128)(2,1)S(1)} copy-done((bf16[512,1024]{1,0:T(8,128)(2,1)S(1)}, bf16[512,1024]{1,0:T(8,128)(2,1)}, u32[]{:S(2)}) %copy-start.10) | copy-done | bytes 1048600
  24.8 1.2 %copy-done.11 = bf16[512,1024]{1,0:T(8,128)(2,1)S(1)} copy-done((bf16[512,1024]{1,0:T(8,128)(2,1)S(1)}, bf16[512,1024]{1,0:T(8,128)(2,1)}, u32[]{:S(2)}) %copy-start.11) | copy-done | bytes 1048600
  26.0 22.4 %shard_map.87 = (bf16[512,1024]{1,0:T(8,128)(2,1)S(1)}, bf16[512,1024]{1,0:T(8,128)(2,1)S(1)}, bf16[512,1024]{1,0:T(8,128)(2,1)S(1)}, bf16[3,512,1024]{2,1,0:T(8...) custom-call(s32[2]{0:T(128)S(1)} %copy-done.6, s32[1024,1]{1,0:T(8,128)S(1)} %copy-done.2, ...), custom_call_target="tpu_custom_call" | custom-call | flops 10468982784 | bytes 19927048 | tf_op jit(solution)/shard_map/pallas_call | solution.py:119
  48.4 0.1 collective-permute-start.2
  48.6 0.7 collective-permute-start.9
  49.3 6.3 %collective-permute-start.10 = (bf16[128,1024]{1,0:T(8,128)(2,1)S(1)}, bf16[128,1024]{1,0:T(8,128)(2,1)S(1)}, u32[]{:S(2)}, u32[]{:S(2)}) collective-permute-start(bf16[128,1024]{1,0:T(8,128)(2,1)S(1)} %get-tuple-element.53), channel_id=1, source_target_pairs={{0,1},{1,0},{2,3},{3,2},{4,5},{5,4},{6,7},{7,6},{8,9},{9,8},{10,11... | collective-permute-start | bytes 786440 | tf_op jit(solution)/shard_map/ppermute | solution.py:361
  55.5 0.0 copy-done.3
  55.5 6.1 %shard_map.88.d_hidden = f32[512,1024]{1,0:T(8,128)S(1)} custom-call(bf16[512,1024]{1,0:T(8,128)(2,1)S(1)} %get-tuple-element.29.grad_query, bf16[512,1024]{1,0:T(8,128)(2,1)S(1)} %get-tuple-element.30.grad_key, bf16[512,1024]{1,0:T(8,128)(2,1)S(1)} %get-tuple-element.31.grad_value, bf16[1024,1024]{1,0:T(8,128)(2,1)S(1)} %copy-done.3, ...), custom_call_target="tpu_custom_call" | custom-call | flops 3221225472 | bytes 11534336 | tf_op jit(solution)/shard_map/pallas_call | solution.py:119
  61.6 0.0 collective-permute-done.9
  61.6 0.8 collective-permute-done.10
  62.6 0.0 collective-permute-done.2
  62.6 1.6 %add_convert_fusion = bf16[3,512,1024]{2,1,0:T(8,128)(2,1)S(1)} fusion(bf16[3,512,1024]{2,1,0:T(8,128)(2,1)S(1)} %collective-permute-done.2, bf16[3,512,1024]{2,1,0:T(8,128)(2,1)S(1)} %get-tuple-element.27), kind=kLoop, calls=%fused_computation | loop fusion | flops 6291456 | bytes 9437184 | tf_op jit(solution)/shard_map/convert_element_type | solution.py:73
  64.2 0.2 fusion.9
  64.4 1.8 %collective-permute-start.5 = (bf16[2,2,8,8,1024]{4,3,2,1,0:T(8,128)(2,1)S(1)}, bf16[2,2,8,8,1024]{4,3,2,1,0:T(8,128)(2,1)S(1)}, u32[]{:S(2)}, u32[]{:S(2)}) collective-permute-start(bf16[2,2,8,8,1024]{4,3,2,1,0:T(8,128)(2,1)S(1)} %slice_bitcast_fusion), channel_id=1, source_target_pairs={{0,1},{1,0},{2,3},{3,2},{4,5},{5,4},{6,7},{7,6},{8,9},{9,8},{10,11... | collective-permute-start | bytes 1572872 | tf_op jit(solution)/shard_map/ppermute | solution.py:35
  66.2 0.1 fusion.11
  66.4 2.4 %collective-permute-start.4 = (bf16[2,2,8,8,1024]{4,3,2,0,1:T(8,128)(2,1)S(1)}, bf16[2,2,8,8,1024]{4,3,2,0,1:T(8,128)(2,1)S(1)}, u32[]{:S(2)}, u32[]{:S(2)}) collective-permute-start(bf16[2,2,8,8,1024]{4,3,2,0,1:T(8,128)(2,1)S(1)} %bitcast.69), channel_id=1, source_target_pairs={{0,4},{1,5},{2,6},{3,7},{4,0},{5,1},{6,2},{7,3},{8,12},{9,13},{10,... | collective-permute-start | bytes 1572872 | tf_op jit(solution)/shard_map/ppermute | solution.py:35
  68.7 0.1 fusion.10
  68.8 0.0 copy-start
  68.8 0.0 copy-start.1
  68.8 4.7 %collective-permute-start.3 = (bf16[2,2,8,8,1024]{4,3,2,1,0:T(8,128)(2,1)S(1)}, bf16[2,2,8,8,1024]{4,3,2,1,0:T(8,128)(2,1)S(1)}, u32[]{:S(2)}, u32[]{:S(2)}) collective-permute-start(bf16[2,2,8,8,1024]{4,3,2,1,0:T(8,128)(2,1)S(1)} %bitcast.70), channel_id=1, source_target_pairs={{0,16},{1,17},{2,18},{3,19},{4,20},{5,21},{6,22},{7,23},{8,24},{9,... | collective-permute-start | bytes 1572872 | tf_op jit(solution)/shard_map/ppermute | solution.py:35
  73.5 0.2 collective-permute-done.5
  73.7 0.2 fusion
  73.9 2.0 %collective-permute-done.4 = bf16[2,2,8,8,1024]{4,3,2,0,1:T(8,128)(2,1)S(1)} collective-permute-done((bf16[2,2,8,8,1024]{4,3,2,0,1:T(8,128)(2,1)S(1)}, bf16[2,2,8,8,1024]{4,3,2,0,1:T(8,128)(2,1)S(1)}, u32[]{:S(2)}, u32[]{:S(2)}) %collective-permute-start.4) | collective-permute-done | bytes 524320 | tf_op jit(solution)/shard_map/ppermute | solution.py:35
  75.9 0.2 fusion.1
  76.1 4.6 %collective-permute-done.3 = bf16[2,2,8,8,1024]{4,3,2,1,0:T(8,128)(2,1)S(1)} collective-permute-done((bf16[2,2,8,8,1024]{4,3,2,1,0:T(8,128)(2,1)S(1)}, bf16[2,2,8,8,1024]{4,3,2,1,0:T(8,128)(2,1)S(1)}, u32[]{:S(2)}, u32[]{:S(2)}) %collective-permute-start.3) | collective-permute-done | bytes 524320 | tf_op jit(solution)/shard_map/ppermute | solution.py:35
  80.6 0.2 fusion.2
  80.9 2.1 %collective-permute-start.6 = (bf16[2,8,8,1024]{3,2,1,0:T(8,128)(2,1)S(1)}, bf16[2,8,8,1024]{3,2,1,0:T(8,128)(2,1)S(1)}, u32[]{:S(2)}, u32[]{:S(2)}) collective-permute-start(bf16[2,8,8,1024]{3,2,1,0:T(8,128)(2,1)S(1)} %slice_bitcast_fusion.4), channel_id=1, source_target_pairs={{0,4},{1,5},{2,6},{3,7},{4,0},{5,1},{6,2},{7,3},{8,12},{9,13},{10,... | collective-permute-start | bytes 786440 | tf_op jit(solution)/shard_map/ppermute | solution.py:35
  83.0 2.1 %collective-permute-start.8 = (bf16[2,8,8,1024]{3,2,1,0:T(8,128)(2,1)S(1)}, bf16[2,8,8,1024]{3,2,1,0:T(8,128)(2,1)S(1)}, u32[]{:S(2)}, u32[]{:S(2)}) collective-permute-start(bf16[2,8,8,1024]{3,2,1,0:T(8,128)(2,1)S(1)} %slice_bitcast_fusion.2), channel_id=1, source_target_pairs={{0,16},{1,17},{2,18},{3,19},{4,20},{5,21},{6,22},{7,23},{8,24},{9,... | collective-permute-start | bytes 786440 | tf_op jit(solution)/shard_map/ppermute | solution.py:35
  85.1 2.1 %collective-permute-start.7 = (bf16[2,8,8,1024]{3,2,1,0:T(8,128)(2,1)S(1)}, bf16[2,8,8,1024]{3,2,1,0:T(8,128)(2,1)S(1)}, u32[]{:S(2)}, u32[]{:S(2)}) collective-permute-start(bf16[2,8,8,1024]{3,2,1,0:T(8,128)(2,1)S(1)} %slice_bitcast_fusion.3), channel_id=1, source_target_pairs={{0,1},{1,0},{2,3},{3,2},{4,5},{5,4},{6,7},{7,6},{8,9},{9,8},{10,11... | collective-permute-start | bytes 786440 | tf_op jit(solution)/shard_map/ppermute | solution.py:35
  87.2 0.0 copy-done
  87.2 0.0 copy-done.1
  87.2 2.6 %shard_map.89 = bf16[512,1024]{1,0:T(8,128)(2,1)} custom-call(bf16[512,1024]{1,0:T(8,128)(2,1)S(1)} %bitcast.61, bf16[512,1024]{1,0:T(8,128)(2,1)S(1)} %bitcast.63, f32[512,1024]{1,0:T(8,128)S(1)} %shard_map.88.d_hidden, bf16[256,1024]{1,0:T(8,128)(2,1)S(1)} %pad_maximum_fusion.near), custom_call_target="tpu_custom_call" | custom-call | flops 16777216 | bytes 5767168 | tf_op jit(solution)/shard_map/pallas_call | solution.py:119
  89.8 0.0 collective-permute-done.6
  89.8 0.1 fusion.5
  89.9 0.0 collective-permute-done.8
  89.9 0.1 fusion.3
  90.0 1.6 %collective-permute-done.7 = bf16[2,8,8,1024]{3,2,1,0:T(8,128)(2,1)S(1)} collective-permute-done((bf16[2,8,8,1024]{3,2,1,0:T(8,128)(2,1)S(1)}, bf16[2,8,8,1024]{3,2,1,0:T(8,128)(2,1)S(1)}, u32[]{:S(2)}, u32[]{:S(2)}) %collective-permute-start.7) | collective-permute-done | bytes 262176 | tf_op jit(solution)/shard_map/ppermute | solution.py:35
  91.5 0.1 fusion.4
  91.6 0.1 collective-permute-start.13
  91.8 0.1 collective-permute-start.12
  91.9 2.1 %collective-permute-start.11 = (bf16[8,8,1024]{2,1,0:T(8,128)(2,1)S(1)}, bf16[8,8,1024]{2,1,0:T(8,128)(2,1)S(1)}, u32[]{:S(2)}, u32[]{:S(2)}) collective-permute-start(bf16[8,8,1024]{2,1,0:T(8,128)(2,1)S(1)} %slice_bitcast_fusion.7), channel_id=1, source_target_pairs={{0,1},{1,0},{2,3},{3,2},{4,5},{5,4},{6,7},{7,6},{8,9},{9,8},{10,11... | collective-permute-start | bytes 393224 | tf_op jit(solution)/shard_map/ppermute | solution.py:35
  93.9 2.8 %collective-permute-done.13 = bf16[8,8,1024]{2,1,0:T(8,128)(2,1)S(1)} collective-permute-done((bf16[8,8,1024]{2,1,0:T(8,128)(2,1)S(1)}, bf16[8,8,1024]{2,1,0:T(8,128)(2,1)S(1)}, u32[]{:S(2)}, u32[]{:S(2)}) %collective-permute-start.13) | collective-permute-done | bytes 131104 | tf_op jit(solution)/shard_map/ppermute | solution.py:35
  96.7 0.1 collective-permute-done.12
  96.8 0.1 collective-permute-done.11
  97.0 16.1 %all_to_all.5 = bf16[8,8,3072]{2,1,0:T(8,128)(2,1)S(1)} all-to-all(bf16[8,8,3072]{2,1,0:T(8,128)(2,1)S(1)} %pad_maximum_fusion.1), channel_id=1, replica_groups={{0,3,12,15,80,83,92,95},{1,2,13,14,81,82,93,94},{4,7,8,11,84,87,88,91},..., dimensions={0} | all-to-all | bytes 786432 | tf_op jit(solution)/shard_map/all_to_all | solution.py:94
  113.0 0.7 convert_reduce_fusion
  (23 shorter events, 0.5 us)
Async XLA Ops:
  1.7 16.5 %collective-permute-start.1 = (bf16[128,1024]{1,0:T(8,128)(2,1)S(1)}, bf16[128,1024]{1,0:T(8,128)(2,1)S(1)}, u32[]{:S(2)}, u32[]{:S(2)}) collective-permute-start(bf16[128,1024]{1,0:T(8,128)(2,1)S(1)} %get-tuple-element.48), channel_id=1, source_target_pairs={{0,1},{1,0},{2,3},{3,2},{4,5},{5,4},{6,7},{7,6},{8,9},{9,8},{10,11... | collective-permute-start | bytes 786440 | tf_op jit(solution)/shard_map/ppermute | solution.py:361
  3.8 14.4 %collective-permute-start = (bf16[128,1024]{1,0:T(8,128)(2,1)S(1)}, bf16[128,1024]{1,0:T(8,128)(2,1)S(1)}, u32[]{:S(2)}, u32[]{:S(2)}) collective-permute-start(bf16[128,1024]{1,0:T(8,128)(2,1)S(1)} %get-tuple-element.49), channel_id=1, source_target_pairs={{1,2},{2,1},{3,4},{4,3},{5,6},{6,5},{7,8},{8,7},{9,10},{10,9},{11,... | collective-permute-start | bytes 786440 | tf_op jit(solution)/shard_map/ppermute | solution.py:362
  7.4 10.9 %copy-start.2 = (s32[1024,1]{1,0:T(8,128)S(1)}, s32[1024,1]{1,0:T(8,128)}, u32[]{:S(2)}) copy-start(s32[1024,1]{1,0:T(8,128)} %and_add_fusion.target) | copy-start | bytes 12292
  7.4 10.9 %copy-start.4 = (bf16[1024,1024]{1,0:T(8,128)(2,1)S(1)}, bf16[1024,1024]{1,0:T(8,128)(2,1)}, u32[]{:S(2)}) copy-start(bf16[1024,1024]{1,0:T(8,128)(2,1)} %w_key.5) | copy-start | bytes 6291460
  7.4 10.9 %copy-start.6 = (s32[2]{0:T(128)S(1)}, s32[2]{0:T(128)}, u32[]{:S(2)}) copy-start(s32[2]{0:T(128)} %pad_add_fusion.place) | copy-start | bytes 28
  18.3 1.6 %copy-start.5 = (bf16[1024,1024]{1,0:T(8,128)(2,1)S(1)}, bf16[1024,1024]{1,0:T(8,128)(2,1)}, u32[]{:S(2)}) copy-start(bf16[1024,1024]{1,0:T(8,128)(2,1)} %w_value.5) | copy-start | bytes 6291460
  19.9 1.2 %copy-start.7 = (bf16[1024,512]{1,0:T(8,128)(2,1)S(1)}, bf16[1024,512]{1,0:T(8,128)(2,1)}, u32[]{:S(2)}) copy-start(bf16[1024,512]{1,0:T(8,128)(2,1)} %get-tuple-element.22.ordered) | copy-start | bytes 3145732
  21.1 1.2 %copy-start.8 = (bf16[512,1024]{1,0:T(8,128)(2,1)S(1)}, bf16[512,1024]{1,0:T(8,128)(2,1)}, u32[]{:S(2)}) copy-start(bf16[512,1024]{1,0:T(8,128)(2,1)} %get-tuple-element.23.query) | copy-start | bytes 3145732
  22.4 1.2 %copy-start.9 = (bf16[512,1024]{1,0:T(8,128)(2,1)S(1)}, bf16[512,1024]{1,0:T(8,128)(2,1)}, u32[]{:S(2)}) copy-start(bf16[512,1024]{1,0:T(8,128)(2,1)} %get-tuple-element.24.keys) | copy-start | bytes 3145732
  23.6 1.2 %copy-start.10 = (bf16[512,1024]{1,0:T(8,128)(2,1)S(1)}, bf16[512,1024]{1,0:T(8,128)(2,1)}, u32[]{:S(2)}) copy-start(bf16[512,1024]{1,0:T(8,128)(2,1)} %get-tuple-element.25.values) | copy-start | bytes 3145732
  24.8 1.2 %copy-start.11 = (bf16[512,1024]{1,0:T(8,128)(2,1)S(1)}, bf16[512,1024]{1,0:T(8,128)(2,1)}, u32[]{:S(2)}) copy-start(bf16[512,1024]{1,0:T(8,128)(2,1)} %get-tuple-element.26.d_mixed) | copy-start | bytes 3145732
  26.0 29.5 %copy-start.3 = (bf16[1024,1024]{1,0:T(8,128)(2,1)S(1)}, bf16[1024,1024]{1,0:T(8,128)(2,1)}, u32[]{:S(2)}) copy-start(bf16[1024,1024]{1,0:T(8,128)(2,1)} %w_query.3) | copy-start | bytes 6291460
  48.4 14.1 %collective-permute-start.2 = (bf16[3,512,1024]{2,1,0:T(8,128)(2,1)S(1)}, bf16[3,512,1024]{2,1,0:T(8,128)(2,1)S(1)}, u32[]{:S(2)}, u32[]{:S(2)}) collective-permute-start(bf16[3,512,1024]{2,1,0:T(8,128)(2,1)S(1)} %get-tuple-element.28), channel_id=1, source_target_pairs={{0,32},{1,33},{2,34},{3,35},{4,36},{5,37},{6,38},{7,39},{8,40},{9,... | collective-permute-start | bytes 9437192 | tf_op jit(solution)/shard_map/ppermute | solution.py:35
  48.6 13.1 %collective-permute-start.9 = (bf16[128,1024]{1,0:T(8,128)(2,1)S(1)}, bf16[128,1024]{1,0:T(8,128)(2,1)S(1)}, u32[]{:S(2)}, u32[]{:S(2)}) collective-permute-start(bf16[128,1024]{1,0:T(8,128)(2,1)S(1)} %get-tuple-element.52), channel_id=1, source_target_pairs={{1,2},{2,1},{3,4},{4,3},{5,6},{6,5},{7,8},{8,7},{9,10},{10,9},{11,... | collective-permute-start | bytes 786440 | tf_op jit(solution)/shard_map/ppermute | solution.py:362
  49.3 13.2 %collective-permute-start.10 = (bf16[128,1024]{1,0:T(8,128)(2,1)S(1)}, bf16[128,1024]{1,0:T(8,128)(2,1)S(1)}, u32[]{:S(2)}, u32[]{:S(2)}) collective-permute-start(bf16[128,1024]{1,0:T(8,128)(2,1)S(1)} %get-tuple-element.53), channel_id=1, source_target_pairs={{0,1},{1,0},{2,3},{3,2},{4,5},{5,4},{6,7},{7,6},{8,9},{9,8},{10,11... | collective-permute-start | bytes 786440 | tf_op jit(solution)/shard_map/ppermute | solution.py:361
  64.4 9.3 %collective-permute-start.5 = (bf16[2,2,8,8,1024]{4,3,2,1,0:T(8,128)(2,1)S(1)}, bf16[2,2,8,8,1024]{4,3,2,1,0:T(8,128)(2,1)S(1)}, u32[]{:S(2)}, u32[]{:S(2)}) collective-permute-start(bf16[2,2,8,8,1024]{4,3,2,1,0:T(8,128)(2,1)S(1)} %slice_bitcast_fusion), channel_id=1, source_target_pairs={{0,1},{1,0},{2,3},{3,2},{4,5},{5,4},{6,7},{7,6},{8,9},{9,8},{10,11... | collective-permute-start | bytes 1572872 | tf_op jit(solution)/shard_map/ppermute | solution.py:35
  66.4 9.5 %collective-permute-start.4 = (bf16[2,2,8,8,1024]{4,3,2,0,1:T(8,128)(2,1)S(1)}, bf16[2,2,8,8,1024]{4,3,2,0,1:T(8,128)(2,1)S(1)}, u32[]{:S(2)}, u32[]{:S(2)}) collective-permute-start(bf16[2,2,8,8,1024]{4,3,2,0,1:T(8,128)(2,1)S(1)} %bitcast.69), channel_id=1, source_target_pairs={{0,4},{1,5},{2,6},{3,7},{4,0},{5,1},{6,2},{7,3},{8,12},{9,13},{10,... | collective-permute-start | bytes 1572872 | tf_op jit(solution)/shard_map/ppermute | solution.py:35
  68.8 18.4 %copy-start = (bf16[1,512,1024]{2,1,0:T(8,128)(2,1)S(1)}, bf16[1,512,1024]{2,1,0:T(8,128)(2,1)}, u32[]{:S(2)}) copy-start(bf16[1,512,1024]{2,1,0:T(8,128)(2,1)} %param.7) | copy-start | bytes 3145732
  68.8 18.4 %copy-start.1 = (bf16[1,512,1024]{2,1,0:T(8,128)(2,1)S(1)}, bf16[1,512,1024]{2,1,0:T(8,128)(2,1)}, u32[]{:S(2)}) copy-start(bf16[1,512,1024]{2,1,0:T(8,128)(2,1)} %param.8) | copy-start | bytes 3145732
  68.8 11.8 %collective-permute-start.3 = (bf16[2,2,8,8,1024]{4,3,2,1,0:T(8,128)(2,1)S(1)}, bf16[2,2,8,8,1024]{4,3,2,1,0:T(8,128)(2,1)S(1)}, u32[]{:S(2)}, u32[]{:S(2)}) collective-permute-start(bf16[2,2,8,8,1024]{4,3,2,1,0:T(8,128)(2,1)S(1)} %bitcast.70), channel_id=1, source_target_pairs={{0,16},{1,17},{2,18},{3,19},{4,20},{5,21},{6,22},{7,23},{8,24},{9,... | collective-permute-start | bytes 1572872 | tf_op jit(solution)/shard_map/ppermute | solution.py:35
  80.9 9.0 %collective-permute-start.6 = (bf16[2,8,8,1024]{3,2,1,0:T(8,128)(2,1)S(1)}, bf16[2,8,8,1024]{3,2,1,0:T(8,128)(2,1)S(1)}, u32[]{:S(2)}, u32[]{:S(2)}) collective-permute-start(bf16[2,8,8,1024]{3,2,1,0:T(8,128)(2,1)S(1)} %slice_bitcast_fusion.4), channel_id=1, source_target_pairs={{0,4},{1,5},{2,6},{3,7},{4,0},{5,1},{6,2},{7,3},{8,12},{9,13},{10,... | collective-permute-start | bytes 786440 | tf_op jit(solution)/shard_map/ppermute | solution.py:35
  83.0 6.9 %collective-permute-start.8 = (bf16[2,8,8,1024]{3,2,1,0:T(8,128)(2,1)S(1)}, bf16[2,8,8,1024]{3,2,1,0:T(8,128)(2,1)S(1)}, u32[]{:S(2)}, u32[]{:S(2)}) collective-permute-start(bf16[2,8,8,1024]{3,2,1,0:T(8,128)(2,1)S(1)} %slice_bitcast_fusion.2), channel_id=1, source_target_pairs={{0,16},{1,17},{2,18},{3,19},{4,20},{5,21},{6,22},{7,23},{8,24},{9,... | collective-permute-start | bytes 786440 | tf_op jit(solution)/shard_map/ppermute | solution.py:35
  85.1 6.5 %collective-permute-start.7 = (bf16[2,8,8,1024]{3,2,1,0:T(8,128)(2,1)S(1)}, bf16[2,8,8,1024]{3,2,1,0:T(8,128)(2,1)S(1)}, u32[]{:S(2)}, u32[]{:S(2)}) collective-permute-start(bf16[2,8,8,1024]{3,2,1,0:T(8,128)(2,1)S(1)} %slice_bitcast_fusion.3), channel_id=1, source_target_pairs={{0,1},{1,0},{2,3},{3,2},{4,5},{5,4},{6,7},{7,6},{8,9},{9,8},{10,11... | collective-permute-start | bytes 786440 | tf_op jit(solution)/shard_map/ppermute | solution.py:35
  91.6 5.0 %collective-permute-start.13 = (bf16[8,8,1024]{2,1,0:T(8,128)(2,1)S(1)}, bf16[8,8,1024]{2,1,0:T(8,128)(2,1)S(1)}, u32[]{:S(2)}, u32[]{:S(2)}) collective-permute-start(bf16[8,8,1024]{2,1,0:T(8,128)(2,1)S(1)} %slice_bitcast_fusion.5), channel_id=1, source_target_pairs={{0,4},{1,5},{2,6},{3,7},{4,0},{5,1},{6,2},{7,3},{8,12},{9,13},{10,... | collective-permute-start | bytes 393224 | tf_op jit(solution)/shard_map/ppermute | solution.py:35
  91.8 5.0 %collective-permute-start.12 = (bf16[8,8,1024]{2,1,0:T(8,128)(2,1)S(1)}, bf16[8,8,1024]{2,1,0:T(8,128)(2,1)S(1)}, u32[]{:S(2)}, u32[]{:S(2)}) collective-permute-start(bf16[8,8,1024]{2,1,0:T(8,128)(2,1)S(1)} %slice_bitcast_fusion.6), channel_id=1, source_target_pairs={{0,16},{1,17},{2,18},{3,19},{4,20},{5,21},{6,22},{7,23},{8,24},{9,... | collective-permute-start | bytes 393224 | tf_op jit(solution)/shard_map/ppermute | solution.py:35
  91.9 5.0 %collective-permute-start.11 = (bf16[8,8,1024]{2,1,0:T(8,128)(2,1)S(1)}, bf16[8,8,1024]{2,1,0:T(8,128)(2,1)S(1)}, u32[]{:S(2)}, u32[]{:S(2)}) collective-permute-start(bf16[8,8,1024]{2,1,0:T(8,128)(2,1)S(1)} %slice_bitcast_fusion.7), channel_id=1, source_target_pairs={{0,1},{1,0},{2,3},{3,2},{4,5},{5,4},{6,7},{7,6},{8,9},{9,8},{10,11... | collective-permute-start | bytes 393224 | tf_op jit(solution)/shard_map/ppermute | solution.py:35

commit v3 on v2

--- a/solution.py
+++ b/solution.py
@@ -19,6 +19,7 @@
 masked_value = -1e30
 F32 = jnp.float32
 BF16 = jnp.bfloat16
+ROOM = (30, 30, 30, 30)
 
 AXES = ("rec", "tm")
 CORE = 32
@@ -41,18 +42,20 @@
     return high if core == 0 else [a ^ b for a, b in zip(high, low)]
 
 
-def row_targets(me):
-    row = jnp.arange(1024, dtype=jnp.int32)
-    far = (row >> 9) & 1
-    core = ((me // CORE) % 2) ^ far
+def block_targets():
+    me = lax.axis_index(AXES)
+    block = jnp.arange(128, dtype=jnp.int32)
+    far = block >> 6
+    core = ((me >> 5) & 1) ^ far
     target = me ^ (far * CORE)
     for bit in range(6):
-        mask = jnp.where(core == 0, order_of(0)[bit], order_of(1)[bit])
-        move = (row >> (8 - bit)) & 1
+        masks = order_of(0)[bit], order_of(1)[bit]
+        move = (block >> (5 - bit)) & 1
         if bit >= 3:
-            move = move ^ jnp.where(core == 0, coordinates(me, 0)[bit - 3], coordinates(me, 1)[bit - 3])
-        target = target ^ (move * mask)
-    return target * 8 + (row & 7)
+            zero, one = coordinates(me, 0)[bit - 3], coordinates(me, 1)[bit - 3]
+            move = move ^ (zero + core * (one - zero))
+        target = target ^ (move * (masks[0] + core * (masks[1] - masks[0])))
+    return target
 
 
 def last_groups():
@@ -85,11 +88,10 @@
             keep, send = halves(values[part], left[part].index(bit))
             left[part].remove(bit)
             sent.append((keep, exchange(send, masks[bit])))
-        if step < len(beside):
-            other = beside[step](values[0], other)
+        other = beside[step](values[0], other)
         values = [add(keep, got) for keep, got in sent]
-        if step < len(beside):
-            *values, other = lax.optimization_barrier((*values, other))
+        if step > 0:
+            values, other = lax.optimization_barrier((values, other))
     value = jnp.concatenate(values, -1)
     got = lax.all_to_all(value, AXES, 0, 0, axis_index_groups=last_groups(), tiled=True)
     return jnp.sum(got.astype(jnp.float32), 0), other
@@ -139,51 +141,52 @@
 SCALAR = pl.BlockSpec(memory_space=pltpu.SMEM)
 
 
-def one_hot(target):
-    lane = lax.broadcasted_iota(jnp.int32, (target.shape[0], D), 1)
-    return jnp.where(lane == target, 1.0, 0.0).astype(BF16)
-
-
-def front_body(place, target, frames, grads, w_query, w_key, w_value, w_out, ordered, query, keys, values, d_mixed, hidden, masked):
+def one_hot(target, first, blocks):
+    lane = lax.broadcasted_iota(jnp.int32, (8, D), 1) - lax.broadcasted_iota(jnp.int32, (8, D), 0)
+    rows = [jnp.where(lane == 8 * target[first + block], 1.0, 0.0) for block in range(blocks)]
+    return jnp.concatenate(rows, 0).astype(BF16)
+
+
+def here():
+    return lax.axis_index("tm") * ROWS
+
+
+def front_body(length, target, frames, grads, w_query, w_key, w_value, w_out, ordered, query, keys, values, d_mixed, hidden, masked):
     @pl.when(pl.program_id(0) == 0)
     def _():
         hidden[...] = normalize(frames[...])[0].astype(BF16)
-        row = lax.broadcasted_iota(jnp.int32, (ROWS, D), 0) + place[0]
-        masked[...] = jnp.where(row < place[1], grads[...].astype(F32), 0.0).astype(BF16)
+        row = lax.broadcasted_iota(jnp.int32, (ROWS, D), 0) + here()
+        masked[...] = jnp.where(row < length[0], grads[...].astype(F32), 0.0).astype(BF16)
 
     rows = hidden[...]
+    d_mixed[...] = dot_nt(masked[...], w_out[...]).astype(BF16)
     query[...] = dot(rows, w_query[...]).astype(BF16)
     keys[...] = dot(rows, w_key[...]).astype(BF16)
     values[...] = dot(rows, w_value[...]).astype(BF16)
-    d_mixed[...] = dot_nt(masked[...], w_out[...]).astype(BF16)
-    ordered[...] = dot_nt(one_hot(target[...]), rows).astype(BF16)
-
-
-def front(place, target, frames, grads, w_query, w_key, w_value, w_out):
+    ordered[...] = dot_nt(one_hot(target, pl.program_id(0) * (PAIR // 8), PAIR // 8), rows).astype(BF16)
+
+
+def front(length, target, frames, grads, w_query, w_key, w_value, w_out):
     wide = jax.ShapeDtypeStruct((ROWS, D), BF16)
     return call(
         front_body,
         [jax.ShapeDtypeStruct((D, ROWS), BF16), wide, wide, wide, wide],
-        (place, target, frames, grads, w_query, w_key, w_value, w_out),
-        [SCALAR, pl.BlockSpec((PAIR, 1), lambda j: (j, 0)), whole(ROWS, D), whole(ROWS, D)]
-        + [columns(D)] * 3
-        + [pl.BlockSpec((PAIR, D), lambda j: (j, 0))],
+        (length, target, frames, grads, w_query, w_key, w_value, w_out),
+        [SCALAR, SCALAR, whole(ROWS, D), whole(ROWS, D)] + [columns(D)] * 3 + [pl.BlockSpec((PAIR, D), lambda j: (j, 0))],
         [pl.BlockSpec((PAIR, ROWS), lambda j: (j, 0))] + [columns(ROWS)] * 4,
         [pltpu.VMEM((ROWS, D), BF16)] * 2,
         5 * ROWS * D * D,
-        room=60,
+        room=ROOM[0],
     )
 
 
 def attend_body(
-    place, target, low, high, ordered, query, keys, values, d_mixed, w_key, w_value,
-    grad_query, grad_key, grad_value, kept, sent, sides,
-    ordered_border, hidden_border, key_value, key_t, pair, score_t, prob_t, border_grads, total,
+    length, target, low, high, ordered, query, keys, values, d_mixed, w_key, w_value,
+    grad_query, grad_key, grad_value, border_grads, kept, sent,
+    ordered_border, hidden_border, key_value, pair, score_t, prob_t,
 ):
     scale = HDIM ** (-0.5)
     blocks = ROWS // WIN
-    row = lax.broadcasted_iota(jnp.int32, (WIN, WIN), 0)
-    eye = jnp.where(lax.broadcasted_iota(jnp.int32, (WIN, WIN), 1) == row, 1.0, 0.0).astype(BF16)
 
     @pl.when(pl.program_id(0) == 0)
     def _():
@@ -191,10 +194,9 @@
         hidden_border[WIN:] = normalize(high[...])[0].astype(BF16)
         for part in range(4):
             rows = slice(part * PAIR, (part + 1) * PAIR)
-            ordered_border[rows] = dot_nt(one_hot(target[rows]), hidden_border[...]).astype(BF16)
+            ordered_border[rows] = dot_nt(one_hot(target, part * (PAIR // 8), PAIR // 8), hidden_border[...]).astype(BF16)
         for ref in (pair, score_t, prob_t):
             ref[...] = jnp.zeros_like(ref)
-        total[...] = jnp.zeros_like(total)
 
     key_border = dot(hidden_border[...], w_key[...]).astype(BF16)
     value_border = dot(hidden_border[...], w_value[...]).astype(BF16)
@@ -207,7 +209,6 @@
             key_value[head, :WIN, to] = side[:WIN, cols]
             key_value[head, WIN : WIN + ROWS, to] = own[:, cols]
             key_value[head, WIN + ROWS :, to] = side[WIN:, cols]
-        key_t[head] = dot_nt(eye, key_value[head, :, :HDIM]).astype(BF16)
         for i in range(blocks):
             mine = slice(i * WIN, (i + 1) * WIN)
             pair[head, i * PAIR : i * PAIR + WIN, :HDIM] = query[mine, cols]
@@ -219,8 +220,8 @@
     def soften(head, i, both):
         mine = slice(i * WIN, (i + 1) * WIN)
         reach = slice(i * WIN, (i + 3) * WIN)
-        first = (1 - i) * WIN - place[0]
-        last = place[1] - place[0] + (1 - i) * WIN - 1
+        first = (1 - i) * WIN - here()
+        last = length[0] - here() + (1 - i) * WIN - 1
         allowed = (above >= jnp.maximum(lane, first)) & (above <= jnp.minimum(lane + 2 * WIN, last))
         scores = jnp.where(allowed, both[:, :WIN], masked_value)
         d_prob = both[:, WIN:]
@@ -235,10 +236,7 @@
         cols = slice(head * HDIM, (head + 1) * HDIM)
         mine = slice(part * PAIR, (part + 1) * PAIR)
         reach = slice(part * PAIR, part * PAIR + 2 * PAIR)
-        grad_t = dot(key_t[head, :, reach], score_t[head, reach, mine]).astype(BF16)
-        for half in (slice(0, WIN), slice(WIN, PAIR)):
-            rows = slice(part * PAIR + half.start, part * PAIR + half.stop)
-            grad_query[rows, cols] = dot_nt(eye, grad_t[:, half]).astype(BF16)
+        grad_query[mine, cols] = dot_tn(score_t[head, reach, mine], key_value[head, reach, :HDIM]).astype(BF16)
 
     def key_grads(head, part):
         cols = slice(head * HDIM, (head + 1) * HDIM)
@@ -274,59 +272,61 @@
         out[0] = dot(ordered[rows], grad_query[...]).astype(BF16)
         out[1] = (dot(ordered[rows], grad_key[...]) + dot(ordered_border[rows], border_grads[0])).astype(BF16)
         out[2] = (dot(ordered[rows], grad_value[...]) + dot(ordered_border[rows], border_grads[1])).astype(BF16)
-    total[...] += dot_nt(border_grads[0], w_key[...]) + dot_nt(border_grads[1], w_value[...])
-
-    @pl.when(pl.program_id(0) == STEPS - 1)
-    def _():
-        sides[...] = total[...].astype(BF16)
-
-
-def attend(place, target, low, high, ordered, query, keys, values, d_mixed, w_key, w_value):
+
+
+def attend(length, target, low, high, ordered, query, keys, values, d_mixed, w_key, w_value):
     own = jax.ShapeDtypeStruct((ROWS, D), BF16)
     half = jax.ShapeDtypeStruct((3, D // 2, D), BF16)
     reach = ROWS + 2 * WIN
     return call(
         attend_body,
-        [own] * 3 + [half] * 2 + [jax.ShapeDtypeStruct((2 * WIN, D), BF16)],
-        (place, target, low, high, ordered, query, keys, values, d_mixed, w_key, w_value),
-        [SCALAR, whole(D, 1), whole(WIN, D), whole(WIN, D), whole(D, ROWS)] + [columns(ROWS)] * 4 + [columns(D)] * 2,
-        [columns(ROWS)] * 3 + [pl.BlockSpec((3, D // 2, PAIR), lambda j: (0, 0, j))] * 2 + [whole(2 * WIN, D)],
+        [own] * 3 + [jax.ShapeDtypeStruct((2, 2 * WIN, D), BF16)] + [half] * 2,
+        (length, target, low, high, ordered, query, keys, values, d_mixed, w_key, w_value),
+        [SCALAR, SCALAR, whole(WIN, D), whole(WIN, D), whole(D, ROWS)] + [columns(ROWS)] * 4 + [columns(D)] * 2,
+        [columns(ROWS)] * 3
+        + [pl.BlockSpec((2, 2 * WIN, PAIR), lambda j: (0, 0, j))]
+        + [pl.BlockSpec((3, D // 2, PAIR), lambda j: (0, 0, j))] * 2,
         [
             pltpu.VMEM((D, 2 * WIN), BF16),
             pltpu.VMEM((2 * WIN, D), BF16),
             pltpu.VMEM((2, reach, PAIR), BF16),
-            pltpu.VMEM((2, HDIM, reach), BF16),
             pltpu.VMEM((2, 2 * ROWS, PAIR), BF16),
             pltpu.VMEM((2, reach, ROWS), BF16),
             pltpu.VMEM((2, reach, ROWS), BF16),
-            pltpu.VMEM((2, 2 * WIN, PAIR), BF16),
-            pltpu.VMEM((2 * WIN, D), F32),
         ],
-        D * D * (ROWS * 3 + WIN * 12) + 10 * 4 * 3 * HEADS * WIN**3,
-    )
-
-
-def back_body(grad_query, grad_key, grad_value, w_query, w_key, w_value, total):
+        D * D * (ROWS * 3 + WIN * 8) + 10 * 4 * 3 * HEADS * WIN**3,
+        room=ROOM[2],
+    )
+
+
+def back_body(grad_query, grad_key, grad_value, border_grads, w_query, w_key, w_value, total, sides, border_total):
     part = dot_nt(grad_query[...], w_query[...]) + dot_nt(grad_key[...], w_key[...]) + dot_nt(grad_value[...], w_value[...])
+    border_part = dot_nt(border_grads[0], w_key[...]) + dot_nt(border_grads[1], w_value[...])
 
     @pl.when(pl.program_id(0) == 0)
     def _():
         total[...] = part
+        border_total[...] = border_part
 
     @pl.when(pl.program_id(0) > 0)
     def _():
         total[...] += part
+        border_total[...] += border_part
+
+    @pl.when(pl.program_id(0) == STEPS - 1)
+    def _():
+        sides[...] = border_total[...].astype(BF16)
 
 
 def back(*ins):
     return call(
         back_body,
-        jax.ShapeDtypeStruct((ROWS, D), F32),
+        [jax.ShapeDtypeStruct((ROWS, D), F32), jax.ShapeDtypeStruct((2 * WIN, D), BF16)],
         ins,
-        [columns(ROWS)] * 3 + [columns(D)] * 3,
-        whole(ROWS, D),
-        [],
-        3 * ROWS * D * D,
+        [columns(ROWS)] * 3 + [pl.BlockSpec((2, 2 * WIN, PAIR), lambda j: (0, 0, j))] + [columns(D)] * 3,
+        [whole(ROWS, D), whole(2 * WIN, D)],
+        [pltpu.VMEM((2 * WIN, D), F32)],
+        (3 * ROWS + 4 * WIN) * D * D,
     )
 
 
@@ -353,38 +353,50 @@
     )
 
 
-def swap_borders(first, last):
+def swap(first, last, pairs):
     count = lax.axis_size("tm")
     even = lax.axis_index("tm") % 2 == 0
-    one = [(i, i ^ 1) for i in range(count)]
-    two = [(i, i + 1 if i % 2 else i - 1) for i in range(1, count - 1)]
-    a = lax.ppermute(jnp.where(even, last, first), "tm", one)
-    b = lax.ppermute(jnp.where(even, first, last), "tm", two)
-    return jnp.where(even, b, a), jnp.where(even, a, b)
+    if pairs == 0:
+        return lax.ppermute(jnp.where(even, last, first), "tm", [(i, i ^ 1) for i in range(count)])
+    across = [(i, i + 1 if i % 2 else i - 1) for i in range(1, count - 1)]
+    return lax.ppermute(jnp.where(even, first, last), "tm", across)
+
+
+def in_order(within, across):
+    even = lax.axis_index("tm") % 2 == 0
+    return jnp.where(even, across, within), jnp.where(even, within, across)
+
+
+def in_hbm(*arrays):
+    return [pltpu.with_memory_space_constraint(array, pltpu.HBM) for array in arrays]
 
 
 def shards(frames, cotangent, lengths, w_query, w_key, w_value, w_out):
     rows, grads = frames[0], cotangent[0]
-    low, high = swap_borders(rows[:WIN], rows[ROWS - WIN :])
-    place = jnp.stack([lax.axis_index("tm") * ROWS, lengths[0]]).astype(jnp.int32)
-    target = row_targets(lax.axis_index(AXES))[:, None]
-    ordered, query, keys, values, d_mixed = front(place, target, rows, grads, w_query, w_key, w_value, w_out)
-    grad_query, grad_key, grad_value, kept, sent, sides = attend(
-        place, target, low, high, ordered, query, keys, values, d_mixed, w_key, w_value
+    w_query, w_key, w_value, w_out = in_hbm(w_query, w_key, w_value, w_out)
+    top, end = rows[:WIN], rows[ROWS - WIN :]
+    within, across = swap(top, end, 0), swap(top, end, 1)
+    target = block_targets()
+    ordered, query, keys, values, d_mixed = front(lengths, target, *in_hbm(rows, grads), w_query, w_key, w_value, w_out)
+    low, high = in_order(within, across)
+    grad_query, grad_key, grad_value, border_grads, kept, sent = attend(
+        lengths, target, low, high, ordered, query, keys, values, d_mixed, w_key, w_value
     )
     got = exchange(sent, (CORE, CORE))
-    from_low, from_high = swap_borders(sides[:WIN], sides[WIN:])
+    d_hidden, sides = back(grad_query, grad_key, grad_value, border_grads, w_query, w_key, w_value)
     own = add(kept, got)
 
     def first(after, _):
-        query_now, _ = lax.optimization_barrier((grad_query, after))
-        return back(query_now, grad_key, grad_value, w_query, w_key, w_value)
-
-    def second(after, d_hidden):
-        near, _ = lax.optimization_barrier((jnp.concatenate([from_low, from_high]), after))
-        return finish(rows, grads, d_hidden, near)
-
-    weight_part, grad_frames = scatter_sum([own[0], own[1], own[2]], (first, second))
+        return swap(sides[:WIN], sides[WIN:], 0), swap(sides[:WIN], sides[WIN:], 1)
+
+    def second(after, both):
+        now, _ = lax.optimization_barrier((both, after))
+        return finish(rows, grads, d_hidden, jnp.concatenate(in_order(*now)))
+
+    def third(after, done):
+        return done
+
+    weight_part, grad_frames = scatter_sum([own[0], own[1], own[2]], (first, second, third))
     return (grad_frames[None], weight_part)
 
 

time: 114 us -> 101 us (0.89)
  local copies, waits for them, and re-layouts: 8.2 us -> 0.98 us
  starting transfers between devices: 27.2 us -> 24.4 us
  blocking collectives: 16.1 us -> 18.7 us
  other arithmetic: 6.68 us -> 4.44 us
  Pallas kernels: 41.9 us -> 40.1 us
  waiting for transfers between devices: 12.1 us -> 10.6 us
    unnamed x25 -> x5, local copies, waits for them, and re-layouts: 7.77 us -> 0.55 us
    all_to_all x1, blocking collectives: 16.1 us -> 18.7 us  [scatter_sum(): lax.all_to_all(value, AXES, 0, 0, axis_index_groups=last_groups(), tiled=...]
    ppermute x10, starting transfers between devices: 17.5 us -> 14.9 us  [exchange(): return lax.ppermute(value, AXES, pairs)]
    pallas_call x4, Pallas kernels: 41.9 us -> 40.1 us  [call(): pl.pallas_call(body, out_shape=outs, grid=(steps,), in_specs=in_specs, ou...]
    add x1 -> x0, other arithmetic: 1.6 us -> none  [row_targets(): return target * 8 + (row & 7)]
  transfers between devices with their start and end apart: 14 -> 14, of which waited for: 8 -> 7; matrix products, arithmetic and copies ran while one was open for 3% -> 3% of each run, Pallas kernels for 17% -> 21%
where the time goes in v3:
time: 101 us
  Pallas kernels  40.1 us (40%)
  starting transfers between devices  24.4 us (24%)
  blocking collectives  18.7 us (19%)
  waiting for transfers between devices  10.6 us (10%)
  other arithmetic  4.44 us (4%)
  between operations  1.6 us (2%)
    pallas_call x4, Pallas kernels, call(): pl.pallas_call(body, out_shape=outs, grid=(steps,), in_specs=in_specs, ou...  40.1 us
    all_to_all x1, blocking collectives, scatter_sum(): lax.all_to_all(value, AXES, 0, 0, axis_index_groups=last_groups(), tiled=...  18.7 us
    ppermute x10, starting transfers between devices, exchange(): return lax.ppermute(value, AXES, pairs)  14.9 us
    ppermute x10, waiting for transfers between devices, exchange(): return lax.ppermute(value, AXES, pairs)  10.6 us
    ppermute x2, starting transfers between devices, swap(): lax.ppermute(jnp.where(even, last, first), 'tm', [(i, i ^ 1) for i in ran...  8.17 us
    convert_element_type x10, other arithmetic, add(): return (a.astype(jnp.float32) + b.astype(jnp.float32)).astype(jnp.bfloat16)  2.48 us
  transfers between devices with their start and end apart: 14, of which 7 were waited for; matrix products, arithmetic and copies ran while one was open for 3% of the time, Pallas kernels for 21%

profile of v3, /device:TPU:0, one launch (start us, length us, event | category | flops | bytes accessed | tf_op | source)
XLA Modules:
  0.0 100.9 jit_solution(4168896942091297628)
XLA Ops:
  0.6 1.1 %select_bitcast_fusion = (bf16[128,1024]{1,0:T(8,128)(2,1)S(1)}, bf16[128,1024]{1,0:T(8,128)(2,1)S(1)}) fusion(pred[]{:T(512)S(6)} %eq.15, bf16[1,512,1024]{2,1,0:T(8,128)(2,1)} %param.7), kind=kLoop, calls=%fused_computation.32 | loop fusion | flops 262144 | bytes 1048577 | tf_op jit(solution)/shard_map/jit(_where)/select_n | solution.py:360
  1.7 2.1 %collective-permute-start.1 = (bf16[128,1024]{1,0:T(8,128)(2,1)S(1)}, bf16[128,1024]{1,0:T(8,128)(2,1)S(1)}, u32[]{:S(2)}, u32[]{:S(2)}) collective-permute-start(bf16[128,1024]{1,0:T(8,128)(2,1)S(1)} %get-tuple-element.54), channel_id=1, source_target_pairs={{0,1},{1,0},{2,3},{3,2},{4,5},{5,4},{6,7},{7,6},{8,9},{9,8},{10,11... | collective-permute-start | bytes 786440 | tf_op jit(solution)/shard_map/ppermute | solution.py:360
  3.8 0.7 collective-permute-start
  5.2 10.2 %shard_map.86 = (bf16[1024,512]{1,0:T(8,128)(2,1)S(1)}, bf16[512,1024]{1,0:T(8,128)(2,1)S(1)}, bf16[512,1024]{1,0:T(8,128)(2,1)S(1)}, bf16[512,1024]{1,0:T(8,128)(2,1)S(1)}, bf16[512,1024]{1,0:T(8,128)(2,1)S(1)}) custom-call(s32[1]{0:T(128)S(6)} %copy.20.length, s32[128]{0:T(128)S(1)} %multiply_xor_fusion.target, bf16[512,1024]{1,0:T(8,128)(2,1)} %bitcast.65, ...), custom_call_target="tpu_custom_call" | custom-call | flops 5368709120 | bytes 15729156 | tf_op jit(solution)/shard_map/pallas_call | solution.py:121
  15.4 0.0 collective-permute-done.1
  15.4 0.0 collective-permute-done
  15.5 19.1 %shard_map.87 = (bf16[512,1024]{1,0:T(8,128)(2,1)S(1)}, bf16[512,1024]{1,0:T(8,128)(2,1)S(1)}, bf16[512,1024]{1,0:T(8,128)(2,1)S(1)}, bf16[2,256,1024]{2,1,0:T(8...) custom-call(s32[1]{0:T(128)S(6)} %copy.20.length, s32[128]{0:T(128)S(1)} %multiply_xor_fusion.target, ...), custom_call_target="tpu_custom_call" | custom-call | flops 9395240960 | bytes 20447748 | tf_op jit(solution)/shard_map/pallas_call | solution.py:121
  34.5 0.1 collective-permute-start.2
  34.6 8.2 %shard_map.88 = (f32[512,1024]{1,0:T(8,128)S(1)}, bf16[256,1024]{1,0:T(8,128)(2,1)S(1)}) custom-call(bf16[512,1024]{1,0:T(8,128)(2,1)S(1)} %get-tuple-element.32.grad_query, bf16[512,1024]{1,0:T(8,128)(2,1)S(1)} %get-tuple-element.33.grad_key, bf16[512,1024]{1,0:T(8,128)(2,1)S(1)} %get-tuple-element.34.grad_value, ...), custom_call_target="tpu_custom_call" | custom-call | flops 4294967296 | bytes 13107200 | tf_op jit(solution)/shard_map/pallas_call | solution.py:121
  42.9 0.7 collective-permute-start.10
  43.6 6.1 %collective-permute-start.9 = (bf16[128,1024]{1,0:T(8,128)(2,1)S(1)}, bf16[128,1024]{1,0:T(8,128)(2,1)S(1)}, u32[]{:S(2)}, u32[]{:S(2)}) collective-permute-start(bf16[128,1024]{1,0:T(8,128)(2,1)S(1)} %get-tuple-element.59), channel_id=1, source_target_pairs={{0,1},{1,0},{2,3},{3,2},{4,5},{5,4},{6,7},{7,6},{8,9},{9,8},{10,11... | collective-permute-start | bytes 786440 | tf_op jit(solution)/shard_map/ppermute | solution.py:360
  49.7 0.0 collective-permute-done.2
  49.7 1.6 %add_convert_fusion = bf16[3,512,1024]{2,1,0:T(8,128)(2,1)S(1)} fusion(bf16[3,512,1024]{2,1,0:T(8,128)(2,1)S(1)} %collective-permute-done.2, bf16[3,512,1024]{2,1,0:T(8,128)(2,1)S(1)} %get-tuple-element.30), kind=kLoop, calls=%fused_computation | loop fusion | flops 6291456 | bytes 9437184 | tf_op jit(solution)/shard_map/convert_element_type | solution.py:76
  51.3 0.2 fusion.9
  51.5 0.3 collective-permute-start.7
  51.8 0.1 fusion.11
  51.9 4.2 %collective-permute-start.5 = (bf16[2,2,8,8,1024]{4,3,2,0,1:T(8,128)(2,1)S(1)}, bf16[2,2,8,8,1024]{4,3,2,0,1:T(8,128)(2,1)S(1)}, u32[]{:S(2)}, u32[]{:S(2)}) collective-permute-start(bf16[2,2,8,8,1024]{4,3,2,0,1:T(8,128)(2,1)S(1)} %bitcast.74), channel_id=1, source_target_pairs={{0,4},{1,5},{2,6},{3,7},{4,0},{5,1},{6,2},{7,3},{8,12},{9,13},{10,... | collective-permute-start | bytes 1572872 | tf_op jit(solution)/shard_map/ppermute | solution.py:36
  56.1 0.1 fusion.10
  56.2 2.1 %collective-permute-start.3 = (bf16[2,2,8,8,1024]{4,3,2,1,0:T(8,128)(2,1)S(1)}, bf16[2,2,8,8,1024]{4,3,2,1,0:T(8,128)(2,1)S(1)}, u32[]{:S(2)}, u32[]{:S(2)}) collective-permute-start(bf16[2,2,8,8,1024]{4,3,2,1,0:T(8,128)(2,1)S(1)} %bitcast.75), channel_id=1, source_target_pairs={{0,16},{1,17},{2,18},{3,19},{4,20},{5,21},{6,22},{7,23},{8,24},{9,... | collective-permute-start | bytes 1572872 | tf_op jit(solution)/shard_map/ppermute | solution.py:36
  58.3 3.9 %collective-permute-done.7 = bf16[2,2,8,8,1024]{4,3,2,1,0:T(8,128)(2,1)S(1)} collective-permute-done((bf16[2,2,8,8,1024]{4,3,2,1,0:T(8,128)(2,1)S(1)}, bf16[2,2,8,8,1024]{4,3,2,1,0:T(8,128)(2,1)S(1)}, u32[]{:S(2)}, u32[]{:S(2)}) %collective-permute-start.7) | collective-permute-done | bytes 524320 | tf_op jit(solution)/shard_map/ppermute | solution.py:36
  62.2 0.2 fusion
  62.4 5.7 %collective-permute-start.8 = (bf16[2,8,8,1024]{3,2,1,0:T(8,128)(2,1)S(1)}, bf16[2,8,8,1024]{3,2,1,0:T(8,128)(2,1)S(1)}, u32[]{:S(2)}, u32[]{:S(2)}) collective-permute-start(bf16[2,8,8,1024]{3,2,1,0:T(8,128)(2,1)S(1)} %slice_bitcast_fusion.2), channel_id=1, source_target_pairs={{0,16},{1,17},{2,18},{3,19},{4,20},{5,21},{6,22},{7,23},{8,24},{9,... | collective-permute-start | bytes 786440 | tf_op jit(solution)/shard_map/ppermute | solution.py:36
  68.2 0.0 collective-permute-done.5
  68.2 0.0 copy-start
  68.2 0.0 copy-start.1
  68.2 0.2 fusion.1
  68.4 0.4 collective-permute-start.6
  68.8 0.0 collective-permute-done.3
  68.8 0.2 fusion.2
  69.0 0.0 collective-permute-done.10
  69.0 0.0 collective-permute-done.9
  69.0 0.1 collective-permute-start.4
  69.2 0.2 copy-done
  69.4 0.3 copy-done.1
  69.7 2.6 %shard_map.89 = bf16[512,1024]{1,0:T(8,128)(2,1)} custom-call(bf16[512,1024]{1,0:T(8,128)(2,1)S(1)} %bitcast.66, bf16[512,1024]{1,0:T(8,128)(2,1)S(1)} %bitcast.68, f32[512,1024]{1,0:T(8,128)S(1)} %get-tuple-element.36.d_hidden, bf16[256,1024]{1,0:T(8,128)(2,1)S(1)} %pad_maximum_fusion.near), custom_call_target="tpu_custom_call" | custom-call | flops 16777216 | bytes 5767168 | tf_op jit(solution)/shard_map/pallas_call | solution.py:121
  72.4 0.2 collective-permute-done.8
  72.5 0.1 fusion.3
  72.6 2.3 %collective-permute-done.6 = bf16[2,8,8,1024]{3,2,1,0:T(8,128)(2,1)S(1)} collective-permute-done((bf16[2,8,8,1024]{3,2,1,0:T(8,128)(2,1)S(1)}, bf16[2,8,8,1024]{3,2,1,0:T(8,128)(2,1)S(1)}, u32[]{:S(2)}, u32[]{:S(2)}) %collective-permute-start.6) | collective-permute-done | bytes 262176 | tf_op jit(solution)/shard_map/ppermute | solution.py:36
  74.9 0.1 fusion.4
  74.9 0.5 collective-permute-done.4
  75.5 0.1 fusion.5
  75.6 0.1 collective-permute-start.13
  75.7 0.7 collective-permute-start.12
  76.4 1.2 %collective-permute-start.11 = (bf16[8,8,1024]{2,1,0:T(8,128)(2,1)S(1)}, bf16[8,8,1024]{2,1,0:T(8,128)(2,1)S(1)}, u32[]{:S(2)}, u32[]{:S(2)}) collective-permute-start(bf16[8,8,1024]{2,1,0:T(8,128)(2,1)S(1)} %slice_bitcast_fusion.10), channel_id=1, source_target_pairs={{0,1},{1,0},{2,3},{3,2},{4,5},{5,4},{6,7},{7,6},{8,9},{9,8},{10,11... | collective-permute-start | bytes 393224 | tf_op jit(solution)/shard_map/ppermute | solution.py:36
  77.6 3.0 %collective-permute-done.13 = bf16[8,8,1024]{2,1,0:T(8,128)(2,1)S(1)} collective-permute-done((bf16[8,8,1024]{2,1,0:T(8,128)(2,1)S(1)}, bf16[8,8,1024]{2,1,0:T(8,128)(2,1)S(1)}, u32[]{:S(2)}, u32[]{:S(2)}) %collective-permute-start.13) | collective-permute-done | bytes 131104 | tf_op jit(solution)/shard_map/ppermute | solution.py:36
  80.7 0.1 collective-permute-done.12
  80.8 0.7 collective-permute-done.11
  81.5 18.7 %all_to_all.5 = bf16[8,8,3072]{2,1,0:T(8,128)(2,1)S(1)} all-to-all(bf16[8,8,3072]{2,1,0:T(8,128)(2,1)S(1)} %pad_maximum_fusion.1), channel_id=1, replica_groups={{0,3,12,15,80,83,92,95},{1,2,13,14,81,82,93,94},{4,7,8,11,84,87,88,91},..., dimensions={0} | all-to-all | bytes 786432 | tf_op jit(solution)/shard_map/all_to_all | solution.py:96
  100.3 0.7 convert_reduce_fusion
  (17 shorter events, 0.5 us)
Async XLA Ops:
  1.7 13.7 %collective-permute-start.1 = (bf16[128,1024]{1,0:T(8,128)(2,1)S(1)}, bf16[128,1024]{1,0:T(8,128)(2,1)S(1)}, u32[]{:S(2)}, u32[]{:S(2)}) collective-permute-start(bf16[128,1024]{1,0:T(8,128)(2,1)S(1)} %get-tuple-element.54), channel_id=1, source_target_pairs={{0,1},{1,0},{2,3},{3,2},{4,5},{5,4},{6,7},{7,6},{8,9},{9,8},{10,11... | collective-permute-start | bytes 786440 | tf_op jit(solution)/shard_map/ppermute | solution.py:360
  3.8 11.6 %collective-permute-start = (bf16[128,1024]{1,0:T(8,128)(2,1)S(1)}, bf16[128,1024]{1,0:T(8,128)(2,1)S(1)}, u32[]{:S(2)}, u32[]{:S(2)}) collective-permute-start(bf16[128,1024]{1,0:T(8,128)(2,1)S(1)} %get-tuple-element.55), channel_id=1, source_target_pairs={{1,2},{2,1},{3,4},{4,3},{5,6},{6,5},{7,8},{8,7},{9,10},{10,9},{11,... | collective-permute-start | bytes 786440 | tf_op jit(solution)/shard_map/ppermute | solution.py:362
  34.5 15.1 %collective-permute-start.2 = (bf16[3,512,1024]{2,1,0:T(8,128)(2,1)S(1)}, bf16[3,512,1024]{2,1,0:T(8,128)(2,1)S(1)}, u32[]{:S(2)}, u32[]{:S(2)}) collective-permute-start(bf16[3,512,1024]{2,1,0:T(8,128)(2,1)S(1)} %get-tuple-element.31), channel_id=1, source_target_pairs={{0,32},{1,33},{2,34},{3,35},{4,36},{5,37},{6,38},{7,39},{8,40},{9,... | collective-permute-start | bytes 9437192 | tf_op jit(solution)/shard_map/ppermute | solution.py:36
  42.9 26.1 %collective-permute-start.10 = (bf16[128,1024]{1,0:T(8,128)(2,1)S(1)}, bf16[128,1024]{1,0:T(8,128)(2,1)S(1)}, u32[]{:S(2)}, u32[]{:S(2)}) collective-permute-start(bf16[128,1024]{1,0:T(8,128)(2,1)S(1)} %get-tuple-element.58), channel_id=1, source_target_pairs={{1,2},{2,1},{3,4},{4,3},{5,6},{6,5},{7,8},{8,7},{9,10},{10,9},{11,... | collective-permute-start | bytes 786440 | tf_op jit(solution)/shard_map/ppermute | solution.py:362
  43.6 25.4 %collective-permute-start.9 = (bf16[128,1024]{1,0:T(8,128)(2,1)S(1)}, bf16[128,1024]{1,0:T(8,128)(2,1)S(1)}, u32[]{:S(2)}, u32[]{:S(2)}) collective-permute-start(bf16[128,1024]{1,0:T(8,128)(2,1)S(1)} %get-tuple-element.59), channel_id=1, source_target_pairs={{0,1},{1,0},{2,3},{3,2},{4,5},{5,4},{6,7},{7,6},{8,9},{9,8},{10,11... | collective-permute-start | bytes 786440 | tf_op jit(solution)/shard_map/ppermute | solution.py:360
  51.5 10.7 %collective-permute-start.7 = (bf16[2,2,8,8,1024]{4,3,2,1,0:T(8,128)(2,1)S(1)}, bf16[2,2,8,8,1024]{4,3,2,1,0:T(8,128)(2,1)S(1)}, u32[]{:S(2)}, u32[]{:S(2)}) collective-permute-start(bf16[2,2,8,8,1024]{4,3,2,1,0:T(8,128)(2,1)S(1)} %slice_bitcast_fusion), channel_id=1, source_target_pairs={{0,1},{1,0},{2,3},{3,2},{4,5},{5,4},{6,7},{7,6},{8,9},{9,8},{10,11... | collective-permute-start | bytes 1572872 | tf_op jit(solution)/shard_map/ppermute | solution.py:36
  51.9 16.3 %collective-permute-start.5 = (bf16[2,2,8,8,1024]{4,3,2,0,1:T(8,128)(2,1)S(1)}, bf16[2,2,8,8,1024]{4,3,2,0,1:T(8,128)(2,1)S(1)}, u32[]{:S(2)}, u32[]{:S(2)}) collective-permute-start(bf16[2,2,8,8,1024]{4,3,2,0,1:T(8,128)(2,1)S(1)} %bitcast.74), channel_id=1, source_target_pairs={{0,4},{1,5},{2,6},{3,7},{4,0},{5,1},{6,2},{7,3},{8,12},{9,13},{10,... | collective-permute-start | bytes 1572872 | tf_op jit(solution)/shard_map/ppermute | solution.py:36
  56.2 12.6 %collective-permute-start.3 = (bf16[2,2,8,8,1024]{4,3,2,1,0:T(8,128)(2,1)S(1)}, bf16[2,2,8,8,1024]{4,3,2,1,0:T(8,128)(2,1)S(1)}, u32[]{:S(2)}, u32[]{:S(2)}) collective-permute-start(bf16[2,2,8,8,1024]{4,3,2,1,0:T(8,128)(2,1)S(1)} %bitcast.75), channel_id=1, source_target_pairs={{0,16},{1,17},{2,18},{3,19},{4,20},{5,21},{6,22},{7,23},{8,24},{9,... | collective-permute-start | bytes 1572872 | tf_op jit(solution)/shard_map/ppermute | solution.py:36
  62.4 10.1 %collective-permute-start.8 = (bf16[2,8,8,1024]{3,2,1,0:T(8,128)(2,1)S(1)}, bf16[2,8,8,1024]{3,2,1,0:T(8,128)(2,1)S(1)}, u32[]{:S(2)}, u32[]{:S(2)}) collective-permute-start(bf16[2,8,8,1024]{3,2,1,0:T(8,128)(2,1)S(1)} %slice_bitcast_fusion.2), channel_id=1, source_target_pairs={{0,16},{1,17},{2,18},{3,19},{4,20},{5,21},{6,22},{7,23},{8,24},{9,... | collective-permute-start | bytes 786440 | tf_op jit(solution)/shard_map/ppermute | solution.py:36
  68.2 1.2 %copy-start = (bf16[1,512,1024]{2,1,0:T(8,128)(2,1)S(1)}, bf16[1,512,1024]{2,1,0:T(8,128)(2,1)}, u32[]{:S(2)}) copy-start(bf16[1,512,1024]{2,1,0:T(8,128)(2,1)} %param.7) | copy-start | bytes 3145732
  68.2 1.5 %copy-start.1 = (bf16[1,512,1024]{2,1,0:T(8,128)(2,1)S(1)}, bf16[1,512,1024]{2,1,0:T(8,128)(2,1)}, u32[]{:S(2)}) copy-start(bf16[1,512,1024]{2,1,0:T(8,128)(2,1)} %param.8) | copy-start | bytes 3145732
  68.4 6.5 %collective-permute-start.6 = (bf16[2,8,8,1024]{3,2,1,0:T(8,128)(2,1)S(1)}, bf16[2,8,8,1024]{3,2,1,0:T(8,128)(2,1)S(1)}, u32[]{:S(2)}, u32[]{:S(2)}) collective-permute-start(bf16[2,8,8,1024]{3,2,1,0:T(8,128)(2,1)S(1)} %slice_bitcast_fusion.4), channel_id=1, source_target_pairs={{0,1},{1,0},{2,3},{3,2},{4,5},{5,4},{6,7},{7,6},{8,9},{9,8},{10,11... | collective-permute-start | bytes 786440 | tf_op jit(solution)/shard_map/ppermute | solution.py:36
  69.0 6.5 %collective-permute-start.4 = (bf16[2,8,8,1024]{3,2,1,0:T(8,128)(2,1)S(1)}, bf16[2,8,8,1024]{3,2,1,0:T(8,128)(2,1)S(1)}, u32[]{:S(2)}, u32[]{:S(2)}) collective-permute-start(bf16[2,8,8,1024]{3,2,1,0:T(8,128)(2,1)S(1)} %slice_bitcast_fusion.6), channel_id=1, source_target_pairs={{0,4},{1,5},{2,6},{3,7},{4,0},{5,1},{6,2},{7,3},{8,12},{9,13},{10,... | collective-permute-start | bytes 786440 | tf_op jit(solution)/shard_map/ppermute | solution.py:36
  75.6 5.0 %collective-permute-start.13 = (bf16[8,8,1024]{2,1,0:T(8,128)(2,1)S(1)}, bf16[8,8,1024]{2,1,0:T(8,128)(2,1)S(1)}, u32[]{:S(2)}, u32[]{:S(2)}) collective-permute-start(bf16[8,8,1024]{2,1,0:T(8,128)(2,1)S(1)} %slice_bitcast_fusion.8), channel_id=1, source_target_pairs={{0,4},{1,5},{2,6},{3,7},{4,0},{5,1},{6,2},{7,3},{8,12},{9,13},{10,... | collective-permute-start | bytes 393224 | tf_op jit(solution)/shard_map/ppermute | solution.py:36
  75.7 5.0 %collective-permute-start.12 = (bf16[8,8,1024]{2,1,0:T(8,128)(2,1)S(1)}, bf16[8,8,1024]{2,1,0:T(8,128)(2,1)S(1)}, u32[]{:S(2)}, u32[]{:S(2)}) collective-permute-start(bf16[8,8,1024]{2,1,0:T(8,128)(2,1)S(1)} %slice_bitcast_fusion.9), channel_id=1, source_target_pairs={{0,16},{1,17},{2,18},{3,19},{4,20},{5,21},{6,22},{7,23},{8,24},{9,... | collective-permute-start | bytes 393224 | tf_op jit(solution)/shard_map/ppermute | solution.py:36
  76.4 5.0 %collective-permute-start.11 = (bf16[8,8,1024]{2,1,0:T(8,128)(2,1)S(1)}, bf16[8,8,1024]{2,1,0:T(8,128)(2,1)S(1)}, u32[]{:S(2)}, u32[]{:S(2)}) collective-permute-start(bf16[8,8,1024]{2,1,0:T(8,128)(2,1)S(1)} %slice_bitcast_fusion.10), channel_id=1, source_target_pairs={{0,1},{1,0},{2,3},{3,2},{4,5},{5,4},{6,7},{7,6},{8,9},{9,8},{10,11... | collective-permute-start | bytes 393224 | tf_op jit(solution)/shard_map/ppermute | solution.py:36

commit v4 on v3

--- a/solution.py
+++ b/solution.py
@@ -88,13 +88,13 @@
             keep, send = halves(values[part], left[part].index(bit))
             left[part].remove(bit)
             sent.append((keep, exchange(send, masks[bit])))
-        other = beside[step](values[0], other)
-        values = [add(keep, got) for keep, got in sent]
-        if step > 0:
-            values, other = lax.optimization_barrier((values, other))
+        other, ready = beside[step](values, other)
+        arrived = tie([got for _, got in sent], ready)
+        values = [add(keep, got) for (keep, _), got in zip(sent, arrived)]
     value = jnp.concatenate(values, -1)
-    got = lax.all_to_all(value, AXES, 0, 0, axis_index_groups=last_groups(), tiled=True)
-    return jnp.sum(got.astype(jnp.float32), 0), other
+    got = lax.all_to_all(value.reshape(64, -1), AXES, 0, 0, axis_index_groups=last_groups(), tiled=True)
+    chosen = jnp.arange(64)[None, :] % 8 == jnp.arange(8)[:, None]
+    return jnp.dot(chosen.astype(got.dtype), got, preferred_element_type=jnp.float32), other
 
 
 def dot(a, b):
@@ -139,6 +139,8 @@
 
 
 SCALAR = pl.BlockSpec(memory_space=pltpu.SMEM)
+HELD = pl.BlockSpec(memory_space=pltpu.VMEM)
+AFTER = pl.BlockSpec(memory_space=pl.ANY)
 
 
 def one_hot(target, first, blocks):
@@ -149,6 +151,22 @@
 
 def here():
     return lax.axis_index("tm") * ROWS
+
+
+def tie_body(*refs):
+    pass
+
+
+def tie(values, after):
+    return pl.pallas_call(
+        tie_body,
+        out_shape=[jax.ShapeDtypeStruct(value.shape, value.dtype) for value in values],
+        in_specs=[AFTER] * (len(values) + 1),
+        out_specs=[AFTER] * len(values),
+        input_output_aliases={i: i for i in range(len(values))},
+        compiler_params=pltpu.CompilerParams(vmem_limit_bytes=2**20),
+        cost_estimate=pl.CostEstimate(flops=0, bytes_accessed=0, transcendentals=0),
+    )(*values, after)
 
 
 def front_body(length, target, frames, grads, w_query, w_key, w_value, w_out, ordered, query, keys, values, d_mixed, hidden, masked):
@@ -181,9 +199,9 @@
 
 
 def attend_body(
-    length, target, low, high, ordered, query, keys, values, d_mixed, w_key, w_value,
-    grad_query, grad_key, grad_value, border_grads, kept, sent,
-    ordered_border, hidden_border, key_value, pair, score_t, prob_t,
+    length, target, low, high, query, keys, values, d_mixed, w_key, w_value,
+    grad_query, grad_key, grad_value, border_grads, ordered_border,
+    hidden_border, key_value, pair, score_t, prob_t,
 ):
     scale = HDIM ** (-0.5)
     blocks = ROWS // WIN
@@ -267,70 +285,99 @@
             job(0, part)
     for job, part in jobs:
         job(1, part)
-    half = D // 2
-    for out, rows in ((sent, slice(half, D)), (kept, slice(0, half))):
-        out[0] = dot(ordered[rows], grad_query[...]).astype(BF16)
-        out[1] = (dot(ordered[rows], grad_key[...]) + dot(ordered_border[rows], border_grads[0])).astype(BF16)
-        out[2] = (dot(ordered[rows], grad_value[...]) + dot(ordered_border[rows], border_grads[1])).astype(BF16)
-
-
-def attend(length, target, low, high, ordered, query, keys, values, d_mixed, w_key, w_value):
+
+
+def attend(length, target, low, high, query, keys, values, d_mixed, w_key, w_value):
     own = jax.ShapeDtypeStruct((ROWS, D), BF16)
-    half = jax.ShapeDtypeStruct((3, D // 2, D), BF16)
     reach = ROWS + 2 * WIN
     return call(
         attend_body,
-        [own] * 3 + [jax.ShapeDtypeStruct((2, 2 * WIN, D), BF16)] + [half] * 2,
-        (length, target, low, high, ordered, query, keys, values, d_mixed, w_key, w_value),
-        [SCALAR, SCALAR, whole(WIN, D), whole(WIN, D), whole(D, ROWS)] + [columns(ROWS)] * 4 + [columns(D)] * 2,
-        [columns(ROWS)] * 3
-        + [pl.BlockSpec((2, 2 * WIN, PAIR), lambda j: (0, 0, j))]
-        + [pl.BlockSpec((3, D // 2, PAIR), lambda j: (0, 0, j))] * 2,
+        [own] * 3 + [jax.ShapeDtypeStruct((2, 2 * WIN, D), BF16), jax.ShapeDtypeStruct((D, 2 * WIN), BF16)],
+        (length, target, low, high, query, keys, values, d_mixed, w_key, w_value),
+        [SCALAR, SCALAR, whole(WIN, D), whole(WIN, D)] + [columns(ROWS)] * 4 + [columns(D)] * 2,
+        [columns(ROWS)] * 3 + [pl.BlockSpec((2, 2 * WIN, PAIR), lambda j: (0, 0, j)), whole(D, 2 * WIN)],
         [
-            pltpu.VMEM((D, 2 * WIN), BF16),
             pltpu.VMEM((2 * WIN, D), BF16),
             pltpu.VMEM((2, reach, PAIR), BF16),
             pltpu.VMEM((2, 2 * ROWS, PAIR), BF16),
             pltpu.VMEM((2, reach, ROWS), BF16),
             pltpu.VMEM((2, reach, ROWS), BF16),
         ],
-        D * D * (ROWS * 3 + WIN * 8) + 10 * 4 * 3 * HEADS * WIN**3,
+        D * D * WIN * 4 + 10 * 4 * 3 * HEADS * WIN**3,
         room=ROOM[2],
     )
 
 
-def back_body(grad_query, grad_key, grad_value, border_grads, w_query, w_key, w_value, total, sides, border_total):
-    part = dot_nt(grad_query[...], w_query[...]) + dot_nt(grad_key[...], w_key[...]) + dot_nt(grad_value[...], w_value[...])
-    border_part = dot_nt(border_grads[0], w_key[...]) + dot_nt(border_grads[1], w_value[...])
-
-    @pl.when(pl.program_id(0) == 0)
-    def _():
-        total[...] = part
-        border_total[...] = border_part
-
-    @pl.when(pl.program_id(0) > 0)
-    def _():
-        total[...] += part
-        border_total[...] += border_part
-
-    @pl.when(pl.program_id(0) == STEPS - 1)
-    def _():
-        sides[...] = border_total[...].astype(BF16)
+def pair_columns():
+    return pl.ds(pl.multiple_of(pl.program_id(0) * PAIR, PAIR), PAIR)
+
+
+def project_body(ordered, grad, kept, sent):
+    half = D // 2
+    columns = grad[:, pair_columns()]
+    sent[...] = dot(ordered[half:], columns).astype(BF16)
+    kept[...] = dot(ordered[:half], columns).astype(BF16)
+
+
+def project_border_body(part, ordered, grad, ordered_border, border_grads, kept, sent):
+    half = D // 2
+    columns, border_columns = grad[:, pair_columns()], border_grads[part, :, pair_columns()]
+    for out, rows in ((sent, slice(half, D)), (kept, slice(0, half))):
+        out[...] = (dot(ordered[rows], columns) + dot(ordered_border[rows], border_columns)).astype(BF16)
+
+
+def project(ordered, grad, ordered_border=None, border_grads=None, part=0):
+    half = jax.ShapeDtypeStruct((D // 2, D), BF16)
+    if ordered_border is None:
+        body, ins = project_body, (ordered, grad)
+    else:
+        body, ins = functools.partial(project_border_body, part), (ordered, grad, ordered_border, border_grads)
+    return call(body, [half] * 2, ins, [HELD] * len(ins), [columns(D // 2)] * 2, [], D * D * (ROWS + 2 * WIN), room=20)
+
+
+def back_body(grad_query, grad_key, grad_value, w_query, w_key, w_value, *rest):
+    total = rest[-1]
+    total[...] = (
+        dot_nt(grad_query[...], w_query[...]) + dot_nt(grad_key[...], w_key[...]) + dot_nt(grad_value[...], w_value[...])
+    )
+
+
+def rows_of(columns):
+    return pl.BlockSpec((PAIR, columns), lambda j: (j, 0))
 
 
 def back(*ins):
     return call(
         back_body,
-        [jax.ShapeDtypeStruct((ROWS, D), F32), jax.ShapeDtypeStruct((2 * WIN, D), BF16)],
+        jax.ShapeDtypeStruct((ROWS, D), F32),
         ins,
-        [columns(ROWS)] * 3 + [pl.BlockSpec((2, 2 * WIN, PAIR), lambda j: (0, 0, j))] + [columns(D)] * 3,
-        [whole(ROWS, D), whole(2 * WIN, D)],
-        [pltpu.VMEM((2 * WIN, D), F32)],
-        (3 * ROWS + 4 * WIN) * D * D,
-    )
-
-
-def finish_body(frames, grads, d_hidden, near, out):
+        [HELD] * 3 + [rows_of(D)] * 3 + [AFTER] * 3,
+        columns(ROWS),
+        [],
+        3 * ROWS * D * D,
+        room=24,
+    )
+
+
+def back_border_body(grads, w_key, w_value, *rest):
+    sides = rest[-1]
+    sides[...] = (dot_nt(grads[0], w_key[...]) + dot_nt(grads[1], w_value[...])).astype(BF16)
+
+
+def back_border(*ins):
+    return call(
+        back_border_body,
+        jax.ShapeDtypeStruct((2 * WIN, D), BF16),
+        ins,
+        [HELD] + [rows_of(D)] * 2 + [AFTER] * 3,
+        columns(2 * WIN),
+        [],
+        4 * WIN * D * D,
+        room=16,
+    )
+
+
+def finish_body(frames, grads, d_hidden, near, after, out):
     normed, inverse = normalize(frames[...])
     part = pl.program_id(0)
     inner = jnp.logical_and(part > 0, part < STEPS - 1)
@@ -340,26 +387,50 @@
     out[...] = (grads[...].astype(F32) + inverse * (d_rows - mean_grad - normed * mean_cross)).astype(BF16)
 
 
-def finish(frames, grads, d_hidden, near):
+def finish(frames, grads, d_hidden, near, after):
     block = pl.BlockSpec((WIN, D), lambda j: (j, 0))
     return call(
         finish_body,
         jax.ShapeDtypeStruct((ROWS, D), BF16),
-        (frames, grads, d_hidden, near),
-        [block] * 3 + [pl.BlockSpec((WIN, D), lambda j: (j // (STEPS - 1), 0))],
+        (frames, grads, d_hidden, near, after),
+        [block] * 3 + [pl.BlockSpec((WIN, D), lambda j: (j // (STEPS - 1), 0)), AFTER],
         block,
         [],
         ROWS * D * 16,
+        room=16,
     )
 
 
 def swap(first, last, pairs):
+    even = lax.axis_index("tm") % 2 == 0
+    return send(jnp.where(even, last, first) if pairs == 0 else jnp.where(even, first, last), pairs)
+
+
+def send(rows, pairs):
     count = lax.axis_size("tm")
+    if pairs == 0:
+        return lax.ppermute(rows, "tm", [(i, i ^ 1) for i in range(count)])
+    return lax.ppermute(rows, "tm", [(i, i + 1 if i % 2 else i - 1) for i in range(1, count - 1)])
+
+
+def choose_body(sides, *rest):
+    within, across = rest[-2:]
     even = lax.axis_index("tm") % 2 == 0
-    if pairs == 0:
-        return lax.ppermute(jnp.where(even, last, first), "tm", [(i, i ^ 1) for i in range(count)])
-    across = [(i, i + 1 if i % 2 else i - 1) for i in range(1, count - 1)]
-    return lax.ppermute(jnp.where(even, first, last), "tm", across)
+
+    @pl.when(even)
+    def _():
+        within[...] = sides[WIN:]
+        across[...] = sides[:WIN]
+
+    @pl.when(jnp.logical_not(even))
+    def _():
+        within[...] = sides[:WIN]
+        across[...] = sides[WIN:]
+
+
+def choose(sides, *after):
+    half = jax.ShapeDtypeStruct((WIN, D), BF16)
+    return call(choose_body, [half] * 2, (sides, *after), [whole(2 * WIN, D)] + [AFTER] * 3, [whole(WIN, D)] * 2, [], 0, steps=1, room=8)
 
 
 def in_order(within, across):
@@ -379,24 +450,31 @@
     target = block_targets()
     ordered, query, keys, values, d_mixed = front(lengths, target, *in_hbm(rows, grads), w_query, w_key, w_value, w_out)
     low, high = in_order(within, across)
-    grad_query, grad_key, grad_value, border_grads, kept, sent = attend(
-        lengths, target, low, high, ordered, query, keys, values, d_mixed, w_key, w_value
-    )
-    got = exchange(sent, (CORE, CORE))
-    d_hidden, sides = back(grad_query, grad_key, grad_value, border_grads, w_query, w_key, w_value)
-    own = add(kept, got)
+    grad_query, grad_key, grad_value, border_grads, ordered_border = attend(
+        lengths, target, low, high, query, keys, values, d_mixed, w_key, w_value
+    )
+    shares = [
+        project(ordered, grad_query),
+        project(ordered, grad_key, ordered_border, border_grads, 0),
+        project(ordered, grad_value, ordered_border, border_grads, 1),
+    ]
+    own = [add(kept, exchange(sent, (CORE, CORE))) for kept, sent in shares]
 
     def first(after, _):
-        return swap(sides[:WIN], sides[WIN:], 0), swap(sides[:WIN], sides[WIN:], 1)
-
-    def second(after, both):
-        now, _ = lax.optimization_barrier((both, after))
-        return finish(rows, grads, d_hidden, jnp.concatenate(in_order(*now)))
-
-    def third(after, done):
-        return done
-
-    weight_part, grad_frames = scatter_sum([own[0], own[1], own[2]], (first, second, third))
+        d_hidden = back(grad_query, grad_key, grad_value, w_query, w_key, w_value, *after)
+        return d_hidden, d_hidden
+
+    def second(after, d_hidden):
+        sides = back_border(border_grads, w_key, w_value, *after)
+        return (d_hidden, sides), sides
+
+    def third(after, before):
+        d_hidden, sides = before
+        within, across = choose(sides, *after)
+        return (d_hidden, send(within, 0), send(across, 1)), within
+
+    weight_part, (d_hidden, within, across) = scatter_sum(own, (first, second, third))
+    grad_frames = finish(rows, grads, d_hidden, jnp.concatenate(in_order(within, across)), own[2])
     return (grad_frames[None], weight_part)
 
 

time: 101 us -> 94.1 us (0.932)
  blocking collectives: 18.7 us -> 0 us
  starting transfers between devices: 24.4 us -> 30.2 us
  Pallas kernels: 40.1 us -> 44.3 us
  matrix products: 0 us -> 1.8 us
    all_to_all x1 -> x0, blocking collectives: 18.7 us -> none  [scatter_sum(): lax.all_to_all(value, AXES, 0, 0, axis_index_groups=last_groups(), tiled=...]
    all_to_all x0 -> x1, starting transfers between devices: none -> 7.88 us  [scatter_sum(): lax.all_to_all(value.reshape(64, -1), AXES, 0, 0, axis_index_groups=last_...]
    ppermute x10 -> x12, waiting for transfers between devices: 10.6 us -> 3.22 us  [exchange(): return lax.ppermute(value, AXES, pairs)]
    all_to_all x0 -> x1, waiting for transfers between devices: none -> 6.54 us  [scatter_sum(): lax.all_to_all(value.reshape(64, -1), AXES, 0, 0, axis_index_groups=last_...]
    pallas_call x4 -> x9, Pallas kernels: 40.1 us -> 44.3 us  [call(): pl.pallas_call(body, out_shape=outs, grid=(steps,), in_specs=in_specs, ou...]
    dot_general x0 -> x1, matrix products: none -> 1.8 us  [scatter_sum(): jnp.dot(chosen.astype(got.dtype), got, preferred_element_type=jnp.float32)]
    ppermute x4, starting transfers between devices: 9.51 us -> 7.94 us  [the longest x2 5.9 us: send(): return lax.ppermute(rows, 'tm', [(i, i ^ 1) for i in range(count)])]
    select_n x2, other arithmetic: 0.08 us -> 1.25 us  [in_order(): return (jnp.where(even, across, within), jnp.where(even, within, across))]
  transfers between devices with their start and end apart: 14 -> 17, of which waited for: 7 -> 5; matrix products, arithmetic and copies ran while one was open for 3% -> 4% of each run, Pallas kernels for 21% -> 30%
where the time goes in v4:
time: 94.1 us; the launch traced here: 93.7 us
  Pallas kernels  44.3 us (47%)
  starting transfers between devices  30.2 us (32%)
  waiting for transfers between devices  9.77 us (10%)
  other arithmetic  5.23 us (6%)
  matrix products  1.8 us (2%)
  between operations  1.63 us (2%)
    pallas_call x9, Pallas kernels, call(): pl.pallas_call(body, out_shape=outs, grid=(steps,), in_specs=in_specs, ou...  44.3 us
    ppermute x12, starting transfers between devices, exchange(): return lax.ppermute(value, AXES, pairs)  14.4 us
    all_to_all x1, starting transfers between devices, scatter_sum(): lax.all_to_all(value.reshape(64, -1), AXES, 0, 0, axis_index_groups=last_...  7.88 us
    all_to_all x1, waiting for transfers between devices, scatter_sum(): lax.all_to_all(value.reshape(64, -1), AXES, 0, 0, axis_index_groups=last_...  6.54 us
    ppermute x2, starting transfers between devices, send(): return lax.ppermute(rows, 'tm', [(i, i ^ 1) for i in range(count)])  5.9 us
    ppermute x12, waiting for transfers between devices, exchange(): return lax.ppermute(value, AXES, pairs)  3.22 us
    convert_element_type x11, other arithmetic, add(): return (a.astype(jnp.float32) + b.astype(jnp.float32)).astype(jnp.bfloat16)  2.07 us
    ppermute x2, starting transfers between devices, send(): lax.ppermute(rows, 'tm', [(i, i + 1 if i % 2 else i - 1) for i in range(1...  2.04 us
  transfers between devices with their start and end apart: 17, of which 5 were waited for; matrix products, arithmetic and copies ran while one was open for 4% of the time, Pallas kernels for 30%

profile of v4, /device:TPU:0, one launch (start us, length us, event | category | flops | bytes accessed | tf_op | source)
XLA Modules:
  0.0 93.7 jit_solution(9364703212540664826)
XLA Ops:
  0.6 1.1 %select_bitcast_fusion = (bf16[128,1024]{1,0:T(8,128)(2,1)S(1)}, bf16[128,1024]{1,0:T(8,128)(2,1)S(1)}) fusion(pred[]{:T(512)S(6)} %eq.26, bf16[1,512,1024]{2,1,0:T(8,128)(2,1)} %param.7), kind=kLoop, calls=%fused_computation.35 | loop fusion | flops 262144 | bytes 1048577 | tf_op jit(solution)/shard_map/jit(_where)/select_n | solution.py:406
  1.7 0.7 collective-permute-start
  2.4 5.2 %collective-permute-start.1 = (bf16[128,1024]{1,0:T(8,128)(2,1)S(1)}, bf16[128,1024]{1,0:T(8,128)(2,1)S(1)}, u32[]{:S(2)}, u32[]{:S(2)}) collective-permute-start(bf16[128,1024]{1,0:T(8,128)(2,1)S(1)} %get-tuple-element.60), channel_id=1, source_target_pairs={{0,1},{1,0},{2,3},{3,2},{4,5},{5,4},{6,7},{7,6},{8,9},{9,8},{10,11... | collective-permute-start | bytes 786440 | tf_op jit(solution)/shard_map/ppermute | solution.py:412
  8.3 10.2 %shard_map.86 = (bf16[1024,512]{1,0:T(8,128)(2,1)S(1)}, bf16[512,1024]{1,0:T(8,128)(2,1)S(1)}, bf16[512,1024]{1,0:T(8,128)(2,1)S(1)}, bf16[512,1024]{1,0:T(8,128)(2,1)S(1)}, bf16[512,1024]{1,0:T(8,128)(2,1)S(1)}) custom-call(s32[1]{0:T(128)S(6)} %copy.46.length, s32[128]{0:T(128)S(1)} %multiply_xor_fusion.target, bf16[512,1024]{1,0:T(8,128)(2,1)} %bitcast.84, ...), custom_call_target="tpu_custom_call" | custom-call | flops 5368709120 | bytes 15729156 | tf_op jit(solution)/shard_map/pallas_call | solution.py:121
  18.5 0.0 collective-permute-done
  18.6 0.0 collective-permute-done.1
  18.6 13.7 %shard_map.87 = (bf16[512,1024]{1,0:T(8,128)(2,1)S(1)}, bf16[512,1024]{1,0:T(8,128)(2,1)S(1)}, bf16[512,1024]{1,0:T(8,128)(2,1)S(1)}, bf16[2,256,1024]{2,1,0:T(8,128)(2,1)S(1)}, bf16[1024,256]{1,0:T(8,128)(2,1)S(1)}) custom-call(s32[1]{0:T(128)S(6)} %copy.46.length, s32[128]{0:T(128)S(1)} %multiply_xor_fusion.target, ...), custom_call_target="tpu_custom_call" | custom-call | flops 5100273664 | bytes 13632004 | tf_op jit(solution)/shard_map/pallas_call | solution.py:121
  32.3 2.6 %shard_map.90 = (bf16[512,1024]{1,0:T(8,128)(2,1)S(1)}, bf16[512,1024]{1,0:T(8,128)(2,1)S(1)}) custom-call(bf16[1024,512]{1,0:T(8,128)(2,1)S(1)} %get-tuple-element.36.ordered, bf16[512,1024]{1,0:T(8,128)(2,1)S(1)} %get-tuple-element.35.grad.grad_value, bf16[1024,256]{1,0:T(8,128)(2,1)S(1)} %get-tuple-element.39.ordered_border, ...), custom_call_target="tpu_custom_call" | custom-call | flops 1610612736 | bytes 5767168 | tf_op jit(solution)/shard_map/pallas_call | solution.py:121
  34.9 0.1 collective-permute-start.4
  35.0 2.6 %shard_map.89 = (bf16[512,1024]{1,0:T(8,128)(2,1)S(1)}, bf16[512,1024]{1,0:T(8,128)(2,1)S(1)}) custom-call(bf16[1024,512]{1,0:T(8,128)(2,1)S(1)} %get-tuple-element.36.ordered, bf16[512,1024]{1,0:T(8,128)(2,1)S(1)} %get-tuple-element.34.grad.grad_key, bf16[1024,256]{1,0:T(8,128)(2,1)S(1)} %get-tuple-element.39.ordered_border, ...), custom_call_target="tpu_custom_call" | custom-call | flops 1610612736 | bytes 5767168 | tf_op jit(solution)/shard_map/pallas_call | solution.py:121
  37.5 0.6 collective-permute-start.3
  38.1 2.0 %shard_map.88 = (bf16[512,1024]{1,0:T(8,128)(2,1)S(1)}, bf16[512,1024]{1,0:T(8,128)(2,1)S(1)}) custom-call(bf16[1024,512]{1,0:T(8,128)(2,1)S(1)} %get-tuple-element.36.ordered, bf16[512,1024]{1,0:T(8,128)(2,1)S(1)} %get-tuple-element.33.grad.grad_query), custom_call_target="tpu_custom_call" | custom-call | flops 1610612736 | bytes 4194304 | tf_op jit(solution)/shard_map/pallas_call | solution.py:121
  40.1 0.1 collective-permute-start.2
  40.2 0.0 collective-permute-done.4
  40.2 0.4 add_convert_fusion.after
  40.7 0.1 collective-permute-start.7
  40.8 0.0 collective-permute-done.3
  40.8 0.4 add_convert_fusion.1
  41.2 0.1 fusion.12
  41.3 3.7 %collective-permute-start.6 = (bf16[2,2,8,8,1024]{4,3,2,1,0:T(8,128)(2,1)S(1)}, bf16[2,2,8,8,1024]{4,3,2,1,0:T(8,128)(2,1)S(1)}, u32[]{:S(2)}, u32[]{:S(2)}) collective-permute-start(bf16[2,2,8,8,1024]{4,3,2,1,0:T(8,128)(2,1)S(1)} %get-tuple-element.57), channel_id=1, source_target_pairs={{0,4},{1,5},{2,6},{3,7},{4,0},{5,1},{6,2},{7,3},{8,12},{9,13},{10,... | collective-permute-start | bytes 1572872 | tf_op jit(solution)/shard_map/ppermute | solution.py:36
  45.0 0.0 collective-permute-done.2
  45.0 0.4 add_convert_fusion.2
  45.4 0.1 fusion.13
  45.5 2.5 %collective-permute-start.5 = (bf16[2,2,8,8,1024]{4,3,2,1,0:T(8,128)(2,1)S(1)}, bf16[2,2,8,8,1024]{4,3,2,1,0:T(8,128)(2,1)S(1)}, u32[]{:S(2)}, u32[]{:S(2)}) collective-permute-start(bf16[2,2,8,8,1024]{4,3,2,1,0:T(8,128)(2,1)S(1)} %bitcast.90), channel_id=1, source_target_pairs={{0,16},{1,17},{2,18},{3,19},{4,20},{5,21},{6,22},{7,23},{8,24},{9,... | collective-permute-start | bytes 1572872 | tf_op jit(solution)/shard_map/ppermute | solution.py:36
  48.0 5.9 %shard_map.91.refs_3_.d_hidden = f32[512,1024]{1,0:T(8,128)S(1)} custom-call(bf16[512,1024]{1,0:T(8,128)(2,1)S(1)} %get-tuple-element.33.grad.grad_query, bf16[512,1024]{1,0:T(8,128)(2,1)S(1)} %get-tuple-element.34.grad.grad_key, bf16[512,1024]{1,0:T(8,128)(2,1)S(1)} %get-tuple-element.35.grad.grad_value, bf16[1024,1024]{1,0:T(8,128)(2,1)} %w_query.3, ...), custom_call_target="tpu_custom_call" | custom-call | flops 3221225472 | bytes 14680064 | tf_op jit(solution)/shard_map/pallas_call | solution.py:121
  54.0 0.0 collective-permute-done.7.refs_2_
  54.0 0.0 collective-permute-done.6.refs_1_
  54.0 1.2 %collective-permute-done.5.refs_0_ = bf16[2,2,8,8,1024]{4,3,2,1,0:T(8,128)(2,1)S(1)} collective-permute-done((bf16[2,2,8,8,1024]{4,3,2,1,0:T(8,128)(2,1)S(1)}, bf16[2,2,8,8,1024]{4,3,2,1,0:T(8,128)(2,1)S(1)}, u32[]{:S(2)}, u32[]{:S(2)}) %collective-permute-start.5) | collective-permute-done | bytes 524320 | tf_op jit(solution)/shard_map/ppermute | solution.py:36
  55.2 0.2 fusion.rest_2_
  55.4 2.3 %collective-permute-start.10 = (bf16[2,8,8,1024]{3,2,1,0:T(8,128)(2,1)S(1)}, bf16[2,8,8,1024]{3,2,1,0:T(8,128)(2,1)S(1)}, u32[]{:S(2)}, u32[]{:S(2)}) collective-permute-start(bf16[2,8,8,1024]{3,2,1,0:T(8,128)(2,1)S(1)} %slice_bitcast_fusion.5), channel_id=1, source_target_pairs={{0,16},{1,17},{2,18},{3,19},{4,20},{5,21},{6,22},{7,23},{8,24},{9,... | collective-permute-start | bytes 786440 | tf_op jit(solution)/shard_map/ppermute | solution.py:36
  57.7 0.2 fusion.1
  57.9 1.6 %collective-permute-start.9 = (bf16[2,8,8,1024]{3,2,1,0:T(8,128)(2,1)S(1)}, bf16[2,8,8,1024]{3,2,1,0:T(8,128)(2,1)S(1)}, u32[]{:S(2)}, u32[]{:S(2)}) collective-permute-start(bf16[2,8,8,1024]{3,2,1,0:T(8,128)(2,1)S(1)} %slice_bitcast_fusion.6), channel_id=1, source_target_pairs={{0,1},{1,0},{2,3},{3,2},{4,5},{5,4},{6,7},{7,6},{8,9},{9,8},{10,11... | collective-permute-start | bytes 786440 | tf_op jit(solution)/shard_map/ppermute | solution.py:36
  59.5 0.2 fusion.2.rest_0_
  59.7 0.6 collective-permute-start.8
  60.4 4.0 %shard_map.93.refs_3_.sides = bf16[256,1024]{1,0:T(8,128)(2,1)S(1)} custom-call(bf16[2,256,1024]{2,1,0:T(8,128)(2,1)S(1)} %get-tuple-element.40.border_grads.grads, bf16[1024,1024]{1,0:T(8,128)(2,1)} %w_key.7, bf16[1024,1024]{1,0:T(8,128)(2,1)} %w_value.7, bf16[2,2,8,8,1024]{4,3,2,1,0:T(8,128)(2,1)S(1)} %fusion.2.rest_0_, ...), custom_call_target="tpu_custom_call" | custom-call | flops 1073741824 | bytes 7340032 | tf_op jit(solution)/shard_map/pallas_call | solution.py:121
  64.4 0.0 collective-permute-done.10.refs_2_
  64.4 0.0 collective-permute-done.9.refs_1_
  64.4 1.8 %collective-permute-done.8.refs_0_ = bf16[2,8,8,1024]{3,2,1,0:T(8,128)(2,1)S(1)} collective-permute-done((bf16[2,8,8,1024]{3,2,1,0:T(8,128)(2,1)S(1)}, bf16[2,8,8,1024]{3,2,1,0:T(8,128)(2,1)S(1)}, u32[]{:S(2)}, u32[]{:S(2)}) %collective-permute-start.8) | collective-permute-done | bytes 262176 | tf_op jit(solution)/shard_map/ppermute | solution.py:36
  66.2 0.1 fusion.3.rest_2_
  66.3 0.1 fusion.4.rest_1_
  66.3 0.1 fusion.5.rest_0_
  66.4 0.6 collective-permute-start.15
  67.1 0.1 collective-permute-start.14
  67.2 2.1 %collective-permute-start.13 = (bf16[8,8,1024]{2,1,0:T(8,128)(2,1)S(1)}, bf16[8,8,1024]{2,1,0:T(8,128)(2,1)S(1)}, u32[]{:S(2)}, u32[]{:S(2)}) collective-permute-start(bf16[8,8,1024]{2,1,0:T(8,128)(2,1)S(1)} %slice_bitcast_fusion.13), channel_id=1, source_target_pairs={{0,1},{1,0},{2,3},{3,2},{4,5},{5,4},{6,7},{7,6},{8,9},{9,8},{10,11... | collective-permute-start | bytes 393224 | tf_op jit(solution)/shard_map/ppermute | solution.py:36
  69.2 0.7 shard_map.95
  70.0 1.4 %collective-permute-start.11 = (bf16[128,1024]{1,0:T(8,128)(2,1)}, bf16[128,1024]{1,0:T(8,128)(2,1)}, u32[]{:S(2)}, u32[]{:S(2)}) collective-permute-start(bf16[128,1024]{1,0:T(8,128)(2,1)} %get-tuple-element.51), channel_id=1, source_target_pairs={{1,2},{2,1},{3,4},{4,3},{5,6},{6,5},{7,8},{8,7},{9,10},{10,9},{11,... | collective-permute-start | bytes 786440 | tf_op jit(solution)/shard_map/ppermute | solution.py:413
  71.3 0.7 collective-permute-start.12
  72.0 0.0 collective-permute-done.15.refs_2_
  72.0 0.1 collective-permute-done.14.refs_1_
  72.1 0.1 collective-permute-done.13.refs_0_
  72.3 0.1 fusion.8
  72.3 0.8 pad_maximum_fusion.1
  73.1 7.9 %all-to-all-start = ((bf16[8,8,3072]{2,1,0:T(8,128)(2,1)}), bf16[8,8,3072]{2,1,0:T(8,128)(2,1)}, u32[]{:S(2)}, u32[]{:S(2)}) async-start(bf16[8,8,3072]{2,1,0:T(8,128)(2,1)} %pad_maximum_fusion.1), calls=%async_computation | async-start | bytes 786432 | tf_op jit(solution)/shard_map/all_to_all | solution.py:95
  81.0 0.0 copy-start
  81.0 0.0 copy-start.1
  81.0 0.0 collective-permute-done.11
  81.0 0.0 collective-permute-done.12
  81.0 1.2 %broadcast_select_fusion.1 = (bf16[128,1024]{1,0:T(8,128)(2,1)S(1)}, bf16[128,1024]{1,0:T(8,128)(2,1)S(1)}) fusion(bf16[128,1024]{1,0:T(8,128)(2,1)} %collective-permute-done.11, bf16[128,1024]{1,0:T(8,128)(2,1)} %collective-permute-done.12, pred[]{:T(512)S(6)} %eq.26), kind=kLoop, calls=%fused_computation.38 | loop fusion | flops 262144 | bytes 1048577 | tf_op jit(solution)/shard_map/jit(_where)/select_n | solution.py:438
  82.3 0.1 copy-done
  82.4 0.3 copy-done.1
  82.7 2.6 %shard_map.96 = bf16[512,1024]{1,0:T(8,128)(2,1)} custom-call(bf16[512,1024]{1,0:T(8,128)(2,1)S(1)} %bitcast.85, bf16[512,1024]{1,0:T(8,128)(2,1)S(1)} %bitcast.87, f32[512,1024]{1,0:T(8,128)S(1)} %shard_map.91.refs_3_.d_hidden, bf16[256,1024]{1,0:T(8,128)(2,1)S(1)} %pad_maximum_fusion.near, bf16[512,1024]{1,0:T(8,128)(2,1)S(1)} %add_convert_fusion.after), custom_call_target="tpu_custom_call" | custom-call | flops 16777216 | bytes 6815744 | tf_op jit(solution)/shard_map/pallas_call | solution.py:121
  85.3 6.5 %all-to-all-done = bf16[8,8,3072]{2,1,0:T(8,128)(2,1)} async-done(((bf16[8,8,3072]{2,1,0:T(8,128)(2,1)}), bf16[8,8,3072]{2,1,0:T(8,128)(2,1)}, u32[]{:S(2)}, u32[]{:S(2)}) %all-to-all-start) | async-done | bytes 393248 | tf_op jit(solution)/shard_map/all_to_all | solution.py:95
  91.9 1.8 %fusion.6 = f32[8,3072]{1,0:T(8,128)} fusion(bf16[8,8,3072]{2,1,0:T(8,128)(2,1)} %all-to-all-done, s32[64]{0:T(128)S(1)} %and_select_fusion), kind=kOutput, calls=%fused_computation.21 | convolution fusion | flops 3146240 | bytes 491776 | tf_op jit(solution)/shard_map/dot_general | solution.py:97
  (16 shorter events, 0.3 us)
Async XLA Ops:
  1.7 16.8 %collective-permute-start = (bf16[128,1024]{1,0:T(8,128)(2,1)S(1)}, bf16[128,1024]{1,0:T(8,128)(2,1)S(1)}, u32[]{:S(2)}, u32[]{:S(2)}) collective-permute-start(bf16[128,1024]{1,0:T(8,128)(2,1)S(1)} %get-tuple-element.61), channel_id=1, source_target_pairs={{1,2},{2,1},{3,4},{4,3},{5,6},{6,5},{7,8},{8,7},{9,10},{10,9},{11,... | collective-permute-start | bytes 786440 | tf_op jit(solution)/shard_map/ppermute | solution.py:413
  2.4 16.2 %collective-permute-start.1 = (bf16[128,1024]{1,0:T(8,128)(2,1)S(1)}, bf16[128,1024]{1,0:T(8,128)(2,1)S(1)}, u32[]{:S(2)}, u32[]{:S(2)}) collective-permute-start(bf16[128,1024]{1,0:T(8,128)(2,1)S(1)} %get-tuple-element.60), channel_id=1, source_target_pairs={{0,1},{1,0},{2,3},{3,2},{4,5},{5,4},{6,7},{7,6},{8,9},{9,8},{10,11... | collective-permute-start | bytes 786440 | tf_op jit(solution)/shard_map/ppermute | solution.py:412
  34.9 5.3 %collective-permute-start.4 = (bf16[512,1024]{1,0:T(8,128)(2,1)S(1)}, bf16[512,1024]{1,0:T(8,128)(2,1)S(1)}, u32[]{:S(2)}, u32[]{:S(2)}) collective-permute-start(bf16[512,1024]{1,0:T(8,128)(2,1)S(1)} %get-tuple-element.44), channel_id=1, source_target_pairs={{0,32},{1,33},{2,34},{3,35},{4,36},{5,37},{6,38},{7,39},{8,40},{9,... | collective-permute-start | bytes 3145736 | tf_op jit(solution)/shard_map/ppermute | solution.py:36
  37.5 3.2 %collective-permute-start.3 = (bf16[512,1024]{1,0:T(8,128)(2,1)S(1)}, bf16[512,1024]{1,0:T(8,128)(2,1)S(1)}, u32[]{:S(2)}, u32[]{:S(2)}) collective-permute-start(bf16[512,1024]{1,0:T(8,128)(2,1)S(1)} %get-tuple-element.42), channel_id=1, source_target_pairs={{0,32},{1,33},{2,34},{3,35},{4,36},{5,37},{6,38},{7,39},{8,40},{9,... | collective-permute-start | bytes 3145736 | tf_op jit(solution)/shard_map/ppermute | solution.py:36
  40.1 4.9 %collective-permute-start.2 = (bf16[512,1024]{1,0:T(8,128)(2,1)S(1)}, bf16[512,1024]{1,0:T(8,128)(2,1)S(1)}, u32[]{:S(2)}, u32[]{:S(2)}) collective-permute-start(bf16[512,1024]{1,0:T(8,128)(2,1)S(1)} %get-tuple-element.38), channel_id=1, source_target_pairs={{0,32},{1,33},{2,34},{3,35},{4,36},{5,37},{6,38},{7,39},{8,40},{9,... | collective-permute-start | bytes 3145736 | tf_op jit(solution)/shard_map/ppermute | solution.py:36
  40.7 13.3 %collective-permute-start.7 = (bf16[2,2,8,8,1024]{4,3,2,1,0:T(8,128)(2,1)S(1)}, bf16[2,2,8,8,1024]{4,3,2,1,0:T(8,128)(2,1)S(1)}, u32[]{:S(2)}, u32[]{:S(2)}) collective-permute-start(bf16[2,2,8,8,1024]{4,3,2,1,0:T(8,128)(2,1)S(1)} %slice_bitcast_fusion.1), channel_id=1, source_target_pairs={{0,1},{1,0},{2,3},{3,2},{4,5},{5,4},{6,7},{7,6},{8,9},{9,8},{10,11... | collective-permute-start | bytes 1572872 | tf_op jit(solution)/shard_map/ppermute | solution.py:36
  41.3 12.7 %collective-permute-start.6 = (bf16[2,2,8,8,1024]{4,3,2,1,0:T(8,128)(2,1)S(1)}, bf16[2,2,8,8,1024]{4,3,2,1,0:T(8,128)(2,1)S(1)}, u32[]{:S(2)}, u32[]{:S(2)}) collective-permute-start(bf16[2,2,8,8,1024]{4,3,2,1,0:T(8,128)(2,1)S(1)} %get-tuple-element.57), channel_id=1, source_target_pairs={{0,4},{1,5},{2,6},{3,7},{4,0},{5,1},{6,2},{7,3},{8,12},{9,13},{10,... | collective-permute-start | bytes 1572872 | tf_op jit(solution)/shard_map/ppermute | solution.py:36
  45.5 9.7 %collective-permute-start.5 = (bf16[2,2,8,8,1024]{4,3,2,1,0:T(8,128)(2,1)S(1)}, bf16[2,2,8,8,1024]{4,3,2,1,0:T(8,128)(2,1)S(1)}, u32[]{:S(2)}, u32[]{:S(2)}) collective-permute-start(bf16[2,2,8,8,1024]{4,3,2,1,0:T(8,128)(2,1)S(1)} %bitcast.90), channel_id=1, source_target_pairs={{0,16},{1,17},{2,18},{3,19},{4,20},{5,21},{6,22},{7,23},{8,24},{9,... | collective-permute-start | bytes 1572872 | tf_op jit(solution)/shard_map/ppermute | solution.py:36
  55.4 8.9 %collective-permute-start.10 = (bf16[2,8,8,1024]{3,2,1,0:T(8,128)(2,1)S(1)}, bf16[2,8,8,1024]{3,2,1,0:T(8,128)(2,1)S(1)}, u32[]{:S(2)}, u32[]{:S(2)}) collective-permute-start(bf16[2,8,8,1024]{3,2,1,0:T(8,128)(2,1)S(1)} %slice_bitcast_fusion.5), channel_id=1, source_target_pairs={{0,16},{1,17},{2,18},{3,19},{4,20},{5,21},{6,22},{7,23},{8,24},{9,... | collective-permute-start | bytes 786440 | tf_op jit(solution)/shard_map/ppermute | solution.py:36
  57.9 6.5 %collective-permute-start.9 = (bf16[2,8,8,1024]{3,2,1,0:T(8,128)(2,1)S(1)}, bf16[2,8,8,1024]{3,2,1,0:T(8,128)(2,1)S(1)}, u32[]{:S(2)}, u32[]{:S(2)}) collective-permute-start(bf16[2,8,8,1024]{3,2,1,0:T(8,128)(2,1)S(1)} %slice_bitcast_fusion.6), channel_id=1, source_target_pairs={{0,1},{1,0},{2,3},{3,2},{4,5},{5,4},{6,7},{7,6},{8,9},{9,8},{10,11... | collective-permute-start | bytes 786440 | tf_op jit(solution)/shard_map/ppermute | solution.py:36
  59.7 6.5 %collective-permute-start.8 = (bf16[2,8,8,1024]{3,2,1,0:T(8,128)(2,1)S(1)}, bf16[2,8,8,1024]{3,2,1,0:T(8,128)(2,1)S(1)}, u32[]{:S(2)}, u32[]{:S(2)}) collective-permute-start(bf16[2,8,8,1024]{3,2,1,0:T(8,128)(2,1)S(1)} %slice_bitcast_fusion.7), channel_id=1, source_target_pairs={{0,4},{1,5},{2,6},{3,7},{4,0},{5,1},{6,2},{7,3},{8,12},{9,13},{10,... | collective-permute-start | bytes 786440 | tf_op jit(solution)/shard_map/ppermute | solution.py:36
  66.4 5.6 %collective-permute-start.15 = (bf16[8,8,1024]{2,1,0:T(8,128)(2,1)S(1)}, bf16[8,8,1024]{2,1,0:T(8,128)(2,1)S(1)}, u32[]{:S(2)}, u32[]{:S(2)}) collective-permute-start(bf16[8,8,1024]{2,1,0:T(8,128)(2,1)S(1)} %slice_bitcast_fusion.11), channel_id=1, source_target_pairs={{0,4},{1,5},{2,6},{3,7},{4,0},{5,1},{6,2},{7,3},{8,12},{9,13},{10,... | collective-permute-start | bytes 393224 | tf_op jit(solution)/shard_map/ppermute | solution.py:36
  67.1 5.0 %collective-permute-start.14 = (bf16[8,8,1024]{2,1,0:T(8,128)(2,1)S(1)}, bf16[8,8,1024]{2,1,0:T(8,128)(2,1)S(1)}, u32[]{:S(2)}, u32[]{:S(2)}) collective-permute-start(bf16[8,8,1024]{2,1,0:T(8,128)(2,1)S(1)} %slice_bitcast_fusion.12), channel_id=1, source_target_pairs={{0,16},{1,17},{2,18},{3,19},{4,20},{5,21},{6,22},{7,23},{8,24},{9,... | collective-permute-start | bytes 393224 | tf_op jit(solution)/shard_map/ppermute | solution.py:36
  67.2 5.0 %collective-permute-start.13 = (bf16[8,8,1024]{2,1,0:T(8,128)(2,1)S(1)}, bf16[8,8,1024]{2,1,0:T(8,128)(2,1)S(1)}, u32[]{:S(2)}, u32[]{:S(2)}) collective-permute-start(bf16[8,8,1024]{2,1,0:T(8,128)(2,1)S(1)} %slice_bitcast_fusion.13), channel_id=1, source_target_pairs={{0,1},{1,0},{2,3},{3,2},{4,5},{5,4},{6,7},{7,6},{8,9},{9,8},{10,11... | collective-permute-start | bytes 393224 | tf_op jit(solution)/shard_map/ppermute | solution.py:36
  70.0 11.0 %collective-permute-start.11 = (bf16[128,1024]{1,0:T(8,128)(2,1)}, bf16[128,1024]{1,0:T(8,128)(2,1)}, u32[]{:S(2)}, u32[]{:S(2)}) collective-permute-start(bf16[128,1024]{1,0:T(8,128)(2,1)} %get-tuple-element.51), channel_id=1, source_target_pairs={{1,2},{2,1},{3,4},{4,3},{5,6},{6,5},{7,8},{8,7},{9,10},{10,9},{11,... | collective-permute-start | bytes 786440 | tf_op jit(solution)/shard_map/ppermute | solution.py:413
  71.3 9.7 %collective-permute-start.12 = (bf16[128,1024]{1,0:T(8,128)(2,1)S(1)}, bf16[128,1024]{1,0:T(8,128)(2,1)}, u32[]{:S(2)}, u32[]{:S(2)}) collective-permute-start(bf16[128,1024]{1,0:T(8,128)(2,1)S(1)} %get-tuple-element.52.refs_3_), channel_id=1, source_target_pairs={{0,1},{1,0},{2,3},{3,2},{4,5},{5,4},{6,7},{7,6},{8,9},{9,8},{10,11... | collective-permute-start | bytes 786440 | tf_op jit(solution)/shard_map/ppermute | solution.py:412
  73.1 18.8 %all-to-all-start = ((bf16[8,8,3072]{2,1,0:T(8,128)(2,1)}), bf16[8,8,3072]{2,1,0:T(8,128)(2,1)}, u32[]{:S(2)}, u32[]{:S(2)}) async-start(bf16[8,8,3072]{2,1,0:T(8,128)(2,1)} %pad_maximum_fusion.1), calls=%async_computation | async-start | bytes 786432 | tf_op jit(solution)/shard_map/all_to_all | solution.py:95
  81.0 1.4 %copy-start = (bf16[1,512,1024]{2,1,0:T(8,128)(2,1)S(1)}, bf16[1,512,1024]{2,1,0:T(8,128)(2,1)}, u32[]{:S(2)}) copy-start(bf16[1,512,1024]{2,1,0:T(8,128)(2,1)} %param.7) | copy-start | bytes 3145732
  81.0 1.7 %copy-start.1 = (bf16[1,512,1024]{2,1,0:T(8,128)(2,1)S(1)}, bf16[1,512,1024]{2,1,0:T(8,128)(2,1)}, u32[]{:S(2)}) copy-start(bf16[1,512,1024]{2,1,0:T(8,128)(2,1)} %param.8) | copy-start | bytes 3145732

commit v5 on v4

--- a/solution.py
+++ b/solution.py
@@ -68,29 +68,31 @@
     return groups
 
 
-def halves(value, dim):
-    return lax.index_in_dim(value, 0, dim, False), lax.index_in_dim(value, 1, dim, False)
-
-
-def add(a, b):
-    return (a.astype(jnp.float32) + b.astype(jnp.float32)).astype(jnp.bfloat16)
-
-
-def scatter_sum(parts, beside):
+def total(terms):
+    return sum((term.astype(jnp.float32) for term in terms[1:]), terms[0].astype(jnp.float32)).astype(jnp.bfloat16)
+
+
+def split(terms, dim):
+    shape = [term.reshape(2, 2, 2, 8, 8, -1) if term.ndim == 2 else term for term in terms]
+    stay = [lax.index_in_dim(term, 0, dim, False) for term in shape]
+    return stay, total([lax.index_in_dim(term, 1, dim, False) for term in shape])
+
+
+def scatter_sum(first, beside):
     masks = list(zip(order_of(0), order_of(1)))
-    values = [part.reshape(2, 2, 2, 8, 8, -1) for part in parts]
-    left = [[0, 1, 2] for _ in values]
-    other = None
+    left = [[bit for bit in range(3) if bit != part] for part in range(3)]
+    parts, other = first, None
     for step in range(3):
-        sent = []
-        for part in range(3):
-            bit = (part + step) % 3
-            keep, send = halves(values[part], left[part].index(bit))
-            left[part].remove(bit)
-            sent.append((keep, exchange(send, masks[bit])))
-        other, ready = beside[step](values, other)
-        arrived = tie([got for _, got in sent], ready)
-        values = [add(keep, got) for (keep, _), got in zip(sent, arrived)]
+        got = [exchange(go, masks[(part + step) % 3]) for part, (_, go) in enumerate(parts)]
+        other, ready = beside[step]([go for _, go in parts], other)
+        values = [stay + [come] for (stay, _), come in zip(parts, tie(got, ready))]
+        if step < 2:
+            parts = []
+            for part, terms in enumerate(values):
+                bit = (part + step + 1) % 3
+                parts.append(split(terms, left[part].index(bit)))
+                left[part].remove(bit)
+    values = [total(terms) for terms in values]
     value = jnp.concatenate(values, -1)
     got = lax.all_to_all(value.reshape(64, -1), AXES, 0, 0, axis_index_groups=last_groups(), tiled=True)
     chosen = jnp.arange(64)[None, :] % 8 == jnp.arange(8)[:, None]
@@ -198,8 +200,12 @@
     )
 
 
+def pair_columns():
+    return pl.ds(pl.multiple_of(pl.program_id(0) * PAIR, PAIR), PAIR)
+
+
 def attend_body(
-    length, target, low, high, query, keys, values, d_mixed, w_key, w_value,
+    length, target, low, high, query_all, keys_all, values_all, d_mixed_all, w_key, w_value,
     grad_query, grad_key, grad_value, border_grads, ordered_border,
     hidden_border, key_value, pair, score_t, prob_t,
 ):
@@ -213,9 +219,17 @@
         for part in range(4):
             rows = slice(part * PAIR, (part + 1) * PAIR)
             ordered_border[rows] = dot_nt(one_hot(target, part * (PAIR // 8), PAIR // 8), hidden_border[...]).astype(BF16)
-        for ref in (pair, score_t, prob_t):
-            ref[...] = jnp.zeros_like(ref)
-
+        pair[...] = jnp.zeros_like(pair)
+        outside = jnp.zeros((WIN, WIN), BF16)
+        for ref in (score_t, prob_t):
+            for head in range(2):
+                for i in range(0, blocks, 2):
+                    ref[head, (i + 3) * WIN : (i + 4) * WIN, i * WIN : (i + 1) * WIN] = outside
+                    ref[head, i * WIN : (i + 1) * WIN, (i + 1) * WIN : (i + 2) * WIN] = outside
+
+    query, keys, values, d_mixed = (
+        ref.at[:, pair_columns()] for ref in (query_all, keys_all, values_all, d_mixed_all)
+    )
     key_border = dot(hidden_border[...], w_key[...]).astype(BF16)
     value_border = dot(hidden_border[...], w_value[...]).astype(BF16)
     above = lax.broadcasted_iota(jnp.int32, (3 * WIN, WIN), 0)
@@ -294,7 +308,7 @@
         attend_body,
         [own] * 3 + [jax.ShapeDtypeStruct((2, 2 * WIN, D), BF16), jax.ShapeDtypeStruct((D, 2 * WIN), BF16)],
         (length, target, low, high, query, keys, values, d_mixed, w_key, w_value),
-        [SCALAR, SCALAR, whole(WIN, D), whole(WIN, D)] + [columns(ROWS)] * 4 + [columns(D)] * 2,
+        [SCALAR, SCALAR, whole(WIN, D), whole(WIN, D)] + [HELD] * 4 + [columns(D)] * 2,
         [columns(ROWS)] * 3 + [pl.BlockSpec((2, 2 * WIN, PAIR), lambda j: (0, 0, j)), whole(D, 2 * WIN)],
         [
             pltpu.VMEM((2 * WIN, D), BF16),
@@ -308,10 +322,6 @@
     )
 
 
-def pair_columns():
-    return pl.ds(pl.multiple_of(pl.program_id(0) * PAIR, PAIR), PAIR)
-
-
 def project_body(ordered, grad, kept, sent):
     half = D // 2
     columns = grad[:, pair_columns()]
@@ -319,20 +329,19 @@
     kept[...] = dot(ordered[:half], columns).astype(BF16)
 
 
-def project_border_body(part, ordered, grad, ordered_border, border_grads, kept, sent):
+def project_border_body(part, ordered, grad, ordered_border, border_grads, *rest):
+    kept, sent = rest[-2:]
     half = D // 2
-    columns, border_columns = grad[:, pair_columns()], border_grads[part, :, pair_columns()]
+    columns, border_columns = grad[:, pair_columns()], border_grads[part - 1, :, pair_columns()]
     for out, rows in ((sent, slice(half, D)), (kept, slice(0, half))):
         out[...] = (dot(ordered[rows], columns) + dot(ordered_border[rows], border_columns)).astype(BF16)
 
 
-def project(ordered, grad, ordered_border=None, border_grads=None, part=0):
+def project(part, *ins):
     half = jax.ShapeDtypeStruct((D // 2, D), BF16)
-    if ordered_border is None:
-        body, ins = project_body, (ordered, grad)
-    else:
-        body, ins = functools.partial(project_border_body, part), (ordered, grad, ordered_border, border_grads)
-    return call(body, [half] * 2, ins, [HELD] * len(ins), [columns(D // 2)] * 2, [], D * D * (ROWS + 2 * WIN), room=20)
+    body = functools.partial(project_border_body, part) if part else project_body
+    specs = [HELD] * min(len(ins), 4) + [AFTER] * (len(ins) - 4)
+    return call(body, [half] * 2, ins, specs, [columns(D // 2)] * 2, [], D * D * (ROWS + 2 * WIN), room=20)
 
 
 def back_body(grad_query, grad_key, grad_value, w_query, w_key, w_value, *rest):
@@ -453,12 +462,16 @@
     grad_query, grad_key, grad_value, border_grads, ordered_border = attend(
         lengths, target, low, high, query, keys, values, d_mixed, w_key, w_value
     )
-    shares = [
-        project(ordered, grad_query),
-        project(ordered, grad_key, ordered_border, border_grads, 0),
-        project(ordered, grad_value, ordered_border, border_grads, 1),
-    ]
-    own = [add(kept, exchange(sent, (CORE, CORE))) for kept, sent in shares]
+    parts = []
+    for part, ins in enumerate(
+        (
+            (ordered, grad_query),
+            (ordered, grad_key, ordered_border, border_grads),
+            (ordered, grad_value, ordered_border, border_grads),
+        )
+    ):
+        kept, sent = project(part, *ins, *(parts[0][1:] if part == 2 else ()))
+        parts.append(split([kept, exchange(sent, (CORE, CORE))], part))
 
     def first(after, _):
         d_hidden = back(grad_query, grad_key, grad_value, w_query, w_key, w_value, *after)
@@ -473,8 +486,8 @@
         within, across = choose(sides, *after)
         return (d_hidden, send(within, 0), send(across, 1)), within
 
-    weight_part, (d_hidden, within, across) = scatter_sum(own, (first, second, third))
-    grad_frames = finish(rows, grads, d_hidden, jnp.concatenate(in_order(within, across)), own[2])
+    weight_part, (d_hidden, within, across) = scatter_sum(parts, (first, second, third))
+    grad_frames = finish(rows, grads, d_hidden, jnp.concatenate(in_order(within, across)), parts[2][1])
     return (grad_frames[None], weight_part)
 
 

time: 94.1 us -> 90.7 us (0.964)
  starting transfers between devices: 30.2 us -> 28.5 us
  waiting for transfers between devices: 9.77 us -> 10.9 us
  matrix products: 1.8 us -> 0.81 us
    all_to_all x1, starting transfers between devices: 7.88 us -> 4.78 us  [scatter_sum(): lax.all_to_all(value.reshape(64, -1), AXES, 0, 0, axis_index_groups=last_...]
    ppermute x2, starting transfers between devices: 5.9 us -> 7.85 us  [send(): return lax.ppermute(rows, 'tm', [(i, i ^ 1) for i in range(count)])]
    ppermute x12, waiting for transfers between devices: 3.22 us -> 4.43 us  [exchange(): return lax.ppermute(value, AXES, pairs)]
    dot_general x1, matrix products: 1.8 us -> 0.81 us  [scatter_sum(): jnp.dot(chosen.astype(got.dtype), got, preferred_element_type=jnp.float32)]
  transfers between devices with their start and end apart: 17 -> 17, of which waited for: 5 -> 6; matrix products, arithmetic and copies ran while one was open for 4% -> 4% of each run, Pallas kernels for 30% -> 31%
where the time goes in v5:
time: 90.7 us; the launch traced here: 90.3 us
  Pallas kernels  43.4 us (48%)
  starting transfers between devices  28.5 us (31%)
  waiting for transfers between devices  10.9 us (12%)
  other arithmetic  4.61 us (5%)
  between operations  1.59 us (2%)
    pallas_call x9, Pallas kernels, call(): pl.pallas_call(body, out_shape=outs, grid=(steps,), in_specs=in_specs, ou...  43.4 us
    ppermute x12, starting transfers between devices, exchange(): return lax.ppermute(value, AXES, pairs)  13.8 us
    ppermute x2, starting transfers between devices, send(): return lax.ppermute(rows, 'tm', [(i, i ^ 1) for i in range(count)])  7.85 us
    all_to_all x1, waiting for transfers between devices, scatter_sum(): lax.all_to_all(value.reshape(64, -1), AXES, 0, 0, axis_index_groups=last_...  6.44 us
    all_to_all x1, starting transfers between devices, scatter_sum(): lax.all_to_all(value.reshape(64, -1), AXES, 0, 0, axis_index_groups=last_...  4.78 us
    ppermute x12, waiting for transfers between devices, exchange(): return lax.ppermute(value, AXES, pairs)  4.43 us
    ppermute x2, starting transfers between devices, send(): lax.ppermute(rows, 'tm', [(i, i + 1 if i % 2 else i - 1) for i in range(1...  2.05 us
  transfers between devices with their start and end apart: 17, of which 6 were waited for; matrix products, arithmetic and copies ran while one was open for 4% of the time, Pallas kernels for 31%

profile of v5, /device:TPU:0, one launch (start us, length us, event | category | flops | bytes accessed | tf_op | source)
XLA Modules:
  0.0 90.3 jit_solution(891076212783715644)
XLA Ops:
  0.6 1.1 %select_bitcast_fusion = (bf16[128,1024]{1,0:T(8,128)(2,1)S(1)}, bf16[128,1024]{1,0:T(8,128)(2,1)S(1)}) fusion(pred[]{:T(512)S(6)} %eq.26, bf16[1,512,1024]{2,1,0:T(8,128)(2,1)} %param.7), kind=kLoop, calls=%fused_computation.39 | loop fusion | flops 262144 | bytes 1048577 | tf_op jit(solution)/shard_map/jit(_where)/select_n | solution.py:415
  1.7 0.7 collective-permute-start
  2.4 5.2 %collective-permute-start.1 = (bf16[128,1024]{1,0:T(8,128)(2,1)S(1)}, bf16[128,1024]{1,0:T(8,128)(2,1)S(1)}, u32[]{:S(2)}, u32[]{:S(2)}) collective-permute-start(bf16[128,1024]{1,0:T(8,128)(2,1)S(1)} %get-tuple-element.56), channel_id=1, source_target_pairs={{0,1},{1,0},{2,3},{3,2},{4,5},{5,4},{6,7},{7,6},{8,9},{9,8},{10,11... | collective-permute-start | bytes 786440 | tf_op jit(solution)/shard_map/ppermute | solution.py:421
  8.3 10.2 %shard_map.86 = (bf16[1024,512]{1,0:T(8,128)(2,1)S(1)}, bf16[512,1024]{1,0:T(8,128)(2,1)S(1)}, bf16[512,1024]{1,0:T(8,128)(2,1)S(1)}, bf16[512,1024]{1,0:T(8,128)(2,1)S(1)}, bf16[512,1024]{1,0:T(8,128)(2,1)S(1)}) custom-call(s32[1]{0:T(128)S(6)} %copy.35.length, s32[128]{0:T(128)S(1)} %multiply_xor_fusion.target, bf16[512,1024]{1,0:T(8,128)(2,1)} %bitcast.88, ...), custom_call_target="tpu_custom_call" | custom-call | flops 5368709120 | bytes 15729156 | tf_op jit(solution)/shard_map/pallas_call | solution.py:123
  18.5 0.0 collective-permute-done
  18.6 0.0 collective-permute-done.1
  18.6 13.4 %shard_map.87 = (bf16[512,1024]{1,0:T(8,128)(2,1)S(1)}, bf16[512,1024]{1,0:T(8,128)(2,1)S(1)}, bf16[512,1024]{1,0:T(8,128)(2,1)S(1)}, bf16[2,256,1024]{2,1,0:T(8,128)(2,1)S(1)}, bf16[1024,256]{1,0:T(8,128)(2,1)S(1)}) custom-call(s32[1]{0:T(128)S(6)} %copy.35.length, s32[128]{0:T(128)S(1)} %multiply_xor_fusion.target, ...), custom_call_target="tpu_custom_call" | custom-call | flops 5100273664 | bytes 13632004 | tf_op jit(solution)/shard_map/pallas_call | solution.py:123
  32.1 2.0 %shard_map.88 = (bf16[512,1024]{1,0:T(8,128)(2,1)S(1)}, bf16[512,1024]{1,0:T(8,128)(2,1)S(1)}) custom-call(bf16[1024,512]{1,0:T(8,128)(2,1)S(1)} %get-tuple-element.36.ordered, bf16[512,1024]{1,0:T(8,128)(2,1)S(1)} %get-tuple-element.33.grad.grad_query), custom_call_target="tpu_custom_call" | custom-call | flops 1610612736 | bytes 4194304 | tf_op jit(solution)/shard_map/pallas_call | solution.py:123
  34.1 0.1 collective-permute-start.2
  34.2 2.6 %shard_map.89 = (bf16[512,1024]{1,0:T(8,128)(2,1)S(1)}, bf16[512,1024]{1,0:T(8,128)(2,1)S(1)}) custom-call(bf16[1024,512]{1,0:T(8,128)(2,1)S(1)} %get-tuple-element.36.ordered, bf16[512,1024]{1,0:T(8,128)(2,1)S(1)} %get-tuple-element.34.grad.grad_key, bf16[1024,256]{1,0:T(8,128)(2,1)S(1)} %get-tuple-element.39.ordered_border, ...), custom_call_target="tpu_custom_call" | custom-call | flops 1610612736 | bytes 5767168 | tf_op jit(solution)/shard_map/pallas_call | solution.py:123
  36.8 0.6 collective-permute-start.3
  37.3 0.0 collective-permute-done.2
  37.3 0.2 add_convert_fusion.2
  37.5 2.6 %shard_map.90 = (bf16[512,1024]{1,0:T(8,128)(2,1)S(1)}, bf16[512,1024]{1,0:T(8,128)(2,1)S(1)}) custom-call(bf16[1024,512]{1,0:T(8,128)(2,1)S(1)} %get-tuple-element.36.ordered, bf16[512,1024]{1,0:T(8,128)(2,1)S(1)} %get-tuple-element.35.grad.grad_value, bf16[1024,256]{1,0:T(8,128)(2,1)S(1)} %get-tuple-element.39.ordered_border, ...), custom_call_target="tpu_custom_call" | custom-call | flops 1610612736 | bytes 6291456 | tf_op jit(solution)/shard_map/pallas_call | solution.py:123
  40.1 0.1 collective-permute-start.4
  40.3 4.2 %collective-permute-start.5 = (bf16[2,2,8,8,1024]{4,3,2,1,0:T(8,128)(2,1)S(1)}, bf16[2,2,8,8,1024]{4,3,2,1,0:T(8,128)(2,1)S(1)}, u32[]{:S(2)}, u32[]{:S(2)}) collective-permute-start(bf16[2,2,8,8,1024]{4,3,2,1,0:T(8,128)(2,1)S(1)} %bitcast.91), channel_id=1, source_target_pairs={{0,16},{1,17},{2,18},{3,19},{4,20},{5,21},{6,22},{7,23},{8,24},{9,... | collective-permute-start | bytes 1572872 | tf_op jit(solution)/shard_map/ppermute | solution.py:36
  44.5 0.0 collective-permute-done.3
  44.5 0.2 fusion.rest_1_
  44.7 0.1 collective-permute-start.6
  44.8 0.0 collective-permute-done.4
  44.8 0.2 fusion.1.rest_2_.after
  45.0 2.1 %collective-permute-start.7 = (bf16[2,2,8,8,1024]{4,3,2,1,0:T(8,128)(2,1)S(1)}, bf16[2,2,8,8,1024]{4,3,2,1,0:T(8,128)(2,1)S(1)}, u32[]{:S(2)}, u32[]{:S(2)}) collective-permute-start(bf16[2,2,8,8,1024]{4,3,2,1,0:T(8,128)(2,1)S(1)} %fusion.1.rest_2_.after), channel_id=1, source_target_pairs={{0,1},{1,0},{2,3},{3,2},{4,5},{5,4},{6,7},{7,6},{8,9},{9,8},{10,11... | collective-permute-start | bytes 1572872 | tf_op jit(solution)/shard_map/ppermute | solution.py:36
  47.1 0.1 convert_add_fusion.2
  47.2 5.9 %shard_map.91.refs_3_.d_hidden = f32[512,1024]{1,0:T(8,128)S(1)} custom-call(bf16[512,1024]{1,0:T(8,128)(2,1)S(1)} %get-tuple-element.33.grad.grad_query, bf16[512,1024]{1,0:T(8,128)(2,1)S(1)} %get-tuple-element.34.grad.grad_key, bf16[512,1024]{1,0:T(8,128)(2,1)S(1)} %get-tuple-element.35.grad.grad_value, bf16[1024,1024]{1,0:T(8,128)(2,1)} %w_query.3, ...), custom_call_target="tpu_custom_call" | custom-call | flops 3221225472 | bytes 13107200 | tf_op jit(solution)/shard_map/pallas_call | solution.py:123
  53.1 0.8 collective-permute-done.6.refs_1_
  53.9 0.0 collective-permute-done.5.refs_0_
  53.9 0.3 collective-permute-done.7.refs_2_
  54.3 0.1 fusion.2.rest_2_
  54.4 2.2 %collective-permute-start.10 = (bf16[2,8,8,1024]{3,2,1,0:T(8,128)(2,1)S(1)}, bf16[2,8,8,1024]{3,2,1,0:T(8,128)(2,1)S(1)}, u32[]{:S(2)}, u32[]{:S(2)}) collective-permute-start(bf16[2,8,8,1024]{3,2,1,0:T(8,128)(2,1)S(1)} %fusion.2.rest_2_), channel_id=1, source_target_pairs={{0,16},{1,17},{2,18},{3,19},{4,20},{5,21},{6,22},{7,23},{8,24},{9,... | collective-permute-start | bytes 786440 | tf_op jit(solution)/shard_map/ppermute | solution.py:36
  56.7 0.1 fusion.6.rest_1_
  56.8 2.1 %collective-permute-start.9 = (bf16[2,8,8,1024]{3,2,1,0:T(8,128)(2,1)S(1)}, bf16[2,8,8,1024]{3,2,1,0:T(8,128)(2,1)S(1)}, u32[]{:S(2)}, u32[]{:S(2)}) collective-permute-start(bf16[2,8,8,1024]{3,2,1,0:T(8,128)(2,1)S(1)} %fusion.6.rest_1_), channel_id=1, source_target_pairs={{0,1},{1,0},{2,3},{3,2},{4,5},{5,4},{6,7},{7,6},{8,9},{9,8},{10,11... | collective-permute-start | bytes 786440 | tf_op jit(solution)/shard_map/ppermute | solution.py:36
  58.9 0.1 fusion.3.rest_0_
  58.9 0.3 collective-permute-start.8
  59.2 4.0 %shard_map.93.refs_3_.sides = bf16[256,1024]{1,0:T(8,128)(2,1)S(1)} custom-call(bf16[2,256,1024]{2,1,0:T(8,128)(2,1)S(1)} %get-tuple-element.40.border_grads.grads, bf16[1024,1024]{1,0:T(8,128)(2,1)} %w_key.7, bf16[1024,1024]{1,0:T(8,128)(2,1)} %w_value.7, bf16[2,8,8,1024]{3,2,1,0:T(8,128)(2,1)S(1)} %fusion.3.rest_0_, ...), custom_call_target="tpu_custom_call" | custom-call | flops 1073741824 | bytes 6553600 | tf_op jit(solution)/shard_map/pallas_call | solution.py:123
  63.2 0.0 collective-permute-done.10.refs_2_
  63.2 0.1 collective-permute-done.9.refs_1_
  63.2 2.3 %collective-permute-done.8.refs_0_ = bf16[2,8,8,1024]{3,2,1,0:T(8,128)(2,1)S(1)} collective-permute-done((bf16[2,8,8,1024]{3,2,1,0:T(8,128)(2,1)S(1)}, bf16[2,8,8,1024]{3,2,1,0:T(8,128)(2,1)S(1)}, u32[]{:S(2)}, u32[]{:S(2)}) %collective-permute-start.8) | collective-permute-done | bytes 262176 | tf_op jit(solution)/shard_map/ppermute | solution.py:36
  65.6 0.1 fusion.13.rest_2_
  65.6 0.1 fusion.14.rest_1_
  65.7 0.1 collective-permute-start.15
  65.8 1.9 %collective-permute-start.14 = (bf16[8,8,1024]{2,1,0:T(8,128)(2,1)S(1)}, bf16[8,8,1024]{2,1,0:T(8,128)(2,1)S(1)}, u32[]{:S(2)}, u32[]{:S(2)}) collective-permute-start(bf16[8,8,1024]{2,1,0:T(8,128)(2,1)S(1)} %fusion.14.rest_1_), channel_id=1, source_target_pairs={{0,16},{1,17},{2,18},{3,19},{4,20},{5,21},{6,22},{7,23},{8,24},{9,... | collective-permute-start | bytes 393224 | tf_op jit(solution)/shard_map/ppermute | solution.py:36
  67.7 0.1 fusion.15.rest_0_
  67.7 0.1 collective-permute-start.13
  67.9 1.4 %collective-permute-start.11 = (bf16[128,1024]{1,0:T(8,128)(2,1)S(1)}, bf16[128,1024]{1,0:T(8,128)(2,1)}, u32[]{:S(2)}, u32[]{:S(2)}) collective-permute-start(bf16[128,1024]{1,0:T(8,128)(2,1)S(1)} %get-tuple-element.51), channel_id=1, source_target_pairs={{1,2},{2,1},{3,4},{4,3},{5,6},{6,5},{7,8},{8,7},{9,10},{10,9},{11,... | collective-permute-start | bytes 786440 | tf_op jit(solution)/shard_map/ppermute | solution.py:422
  69.3 2.6 %collective-permute-start.12 = (bf16[128,1024]{1,0:T(8,128)(2,1)S(1)}, bf16[128,1024]{1,0:T(8,128)(2,1)}, u32[]{:S(2)}, u32[]{:S(2)}) collective-permute-start(bf16[128,1024]{1,0:T(8,128)(2,1)S(1)} %get-tuple-element.52.refs_3_), channel_id=1, source_target_pairs={{0,1},{1,0},{2,3},{3,2},{4,5},{5,4},{6,7},{7,6},{8,9},{9,8},{10,11... | collective-permute-start | bytes 786440 | tf_op jit(solution)/shard_map/ppermute | solution.py:421
  71.9 0.0 collective-permute-done.15.refs_2_
  71.9 0.0 collective-permute-done.14.refs_1_
  71.9 0.9 collective-permute-done.13.refs_0_
  72.8 0.2 fusion.8
  73.0 0.1 fusion.12
  73.1 0.8 pad_maximum_fusion.1
  73.9 4.8 %all-to-all-start = ((bf16[8,8,3072]{2,1,0:T(8,128)(2,1)}), bf16[8,8,3072]{2,1,0:T(8,128)(2,1)S(1)}, u32[]{:S(2)}, u32[]{:S(2)}) async-start(bf16[8,8,3072]{2,1,0:T(8,128)(2,1)} %pad_maximum_fusion.1), calls=%async_computation | async-start | bytes 786432 | tf_op jit(solution)/shard_map/all_to_all | solution.py:97
  78.7 0.0 copy-start
  78.7 0.0 copy-start.1
  78.7 0.0 collective-permute-done.11
  78.7 0.0 collective-permute-done.12
  78.7 1.2 %broadcast_select_fusion.1 = (bf16[128,1024]{1,0:T(8,128)(2,1)S(1)}, bf16[128,1024]{1,0:T(8,128)(2,1)S(1)}) fusion(bf16[128,1024]{1,0:T(8,128)(2,1)} %collective-permute-done.11, bf16[128,1024]{1,0:T(8,128)(2,1)} %collective-permute-done.12, pred[]{:T(512)S(6)} %eq.26), kind=kLoop, calls=%fused_computation.42 | loop fusion | flops 262144 | bytes 1048577 | tf_op jit(solution)/shard_map/jit(_where)/select_n | solution.py:447
  80.0 0.1 copy-done
  80.1 0.3 copy-done.1
  80.4 2.6 %shard_map.96 = bf16[512,1024]{1,0:T(8,128)(2,1)} custom-call(bf16[512,1024]{1,0:T(8,128)(2,1)S(1)} %bitcast.89, bf16[512,1024]{1,0:T(8,128)(2,1)S(1)} %bitcast.100, f32[512,1024]{1,0:T(8,128)S(1)} %shard_map.91.refs_3_.d_hidden, bf16[256,1024]{1,0:T(8,128)(2,1)S(1)} %pad_maximum_fusion.near, bf16[2,2,8,8,1024]{4,3,2,1,0:T(8,128)(2,1)S(1)} %fusion.1.rest_2_.after), custom_call_target="tpu_custom_call" | custom-call | flops 16777216 | bytes 6291456 | tf_op jit(solution)/shard_map/pallas_call | solution.py:123
  83.0 6.4 %all-to-all-done = bf16[8,8,3072]{2,1,0:T(8,128)(2,1)S(1)} async-done(((bf16[8,8,3072]{2,1,0:T(8,128)(2,1)}), bf16[8,8,3072]{2,1,0:T(8,128)(2,1)S(1)}, u32[]{:S(2)}, u32[]{:S(2)}) %all-to-all-start) | async-done | bytes 393248 | tf_op jit(solution)/shard_map/all_to_all | solution.py:97
  89.4 0.8 fusion.4
  (10 shorter events, 0.2 us)
Async XLA Ops:
  1.7 16.8 %collective-permute-start = (bf16[128,1024]{1,0:T(8,128)(2,1)S(1)}, bf16[128,1024]{1,0:T(8,128)(2,1)S(1)}, u32[]{:S(2)}, u32[]{:S(2)}) collective-permute-start(bf16[128,1024]{1,0:T(8,128)(2,1)S(1)} %get-tuple-element.57), channel_id=1, source_target_pairs={{1,2},{2,1},{3,4},{4,3},{5,6},{6,5},{7,8},{8,7},{9,10},{10,9},{11,... | collective-permute-start | bytes 786440 | tf_op jit(solution)/shard_map/ppermute | solution.py:422
  2.4 16.2 %collective-permute-start.1 = (bf16[128,1024]{1,0:T(8,128)(2,1)S(1)}, bf16[128,1024]{1,0:T(8,128)(2,1)S(1)}, u32[]{:S(2)}, u32[]{:S(2)}) collective-permute-start(bf16[128,1024]{1,0:T(8,128)(2,1)S(1)} %get-tuple-element.56), channel_id=1, source_target_pairs={{0,1},{1,0},{2,3},{3,2},{4,5},{5,4},{6,7},{7,6},{8,9},{9,8},{10,11... | collective-permute-start | bytes 786440 | tf_op jit(solution)/shard_map/ppermute | solution.py:421
  34.1 3.2 %collective-permute-start.2 = (bf16[512,1024]{1,0:T(8,128)(2,1)S(1)}, bf16[512,1024]{1,0:T(8,128)(2,1)S(1)}, u32[]{:S(2)}, u32[]{:S(2)}) collective-permute-start(bf16[512,1024]{1,0:T(8,128)(2,1)S(1)} %get-tuple-element.38), channel_id=1, source_target_pairs={{0,32},{1,33},{2,34},{3,35},{4,36},{5,37},{6,38},{7,39},{8,40},{9,... | collective-permute-start | bytes 3145736 | tf_op jit(solution)/shard_map/ppermute | solution.py:36
  36.8 7.7 %collective-permute-start.3 = (bf16[512,1024]{1,0:T(8,128)(2,1)S(1)}, bf16[512,1024]{1,0:T(8,128)(2,1)S(1)}, u32[]{:S(2)}, u32[]{:S(2)}) collective-permute-start(bf16[512,1024]{1,0:T(8,128)(2,1)S(1)} %get-tuple-element.42), channel_id=1, source_target_pairs={{0,32},{1,33},{2,34},{3,35},{4,36},{5,37},{6,38},{7,39},{8,40},{9,... | collective-permute-start | bytes 3145736 | tf_op jit(solution)/shard_map/ppermute | solution.py:36
  40.1 4.7 %collective-permute-start.4 = (bf16[512,1024]{1,0:T(8,128)(2,1)S(1)}, bf16[512,1024]{1,0:T(8,128)(2,1)S(1)}, u32[]{:S(2)}, u32[]{:S(2)}) collective-permute-start(bf16[512,1024]{1,0:T(8,128)(2,1)S(1)} %get-tuple-element.44), channel_id=1, source_target_pairs={{0,32},{1,33},{2,34},{3,35},{4,36},{5,37},{6,38},{7,39},{8,40},{9,... | collective-permute-start | bytes 3145736 | tf_op jit(solution)/shard_map/ppermute | solution.py:36
  40.3 13.7 %collective-permute-start.5 = (bf16[2,2,8,8,1024]{4,3,2,1,0:T(8,128)(2,1)S(1)}, bf16[2,2,8,8,1024]{4,3,2,1,0:T(8,128)(2,1)S(1)}, u32[]{:S(2)}, u32[]{:S(2)}) collective-permute-start(bf16[2,2,8,8,1024]{4,3,2,1,0:T(8,128)(2,1)S(1)} %bitcast.91), channel_id=1, source_target_pairs={{0,16},{1,17},{2,18},{3,19},{4,20},{5,21},{6,22},{7,23},{8,24},{9,... | collective-permute-start | bytes 1572872 | tf_op jit(solution)/shard_map/ppermute | solution.py:36
  44.7 9.3 %collective-permute-start.6 = (bf16[2,2,8,8,1024]{4,3,2,1,0:T(8,128)(2,1)S(1)}, bf16[2,2,8,8,1024]{4,3,2,1,0:T(8,128)(2,1)S(1)}, u32[]{:S(2)}, u32[]{:S(2)}) collective-permute-start(bf16[2,2,8,8,1024]{4,3,2,1,0:T(8,128)(2,1)S(1)} %fusion.rest_1_), channel_id=1, source_target_pairs={{0,4},{1,5},{2,6},{3,7},{4,0},{5,1},{6,2},{7,3},{8,12},{9,13},{10,... | collective-permute-start | bytes 1572872 | tf_op jit(solution)/shard_map/ppermute | solution.py:36
  45.0 9.3 %collective-permute-start.7 = (bf16[2,2,8,8,1024]{4,3,2,1,0:T(8,128)(2,1)S(1)}, bf16[2,2,8,8,1024]{4,3,2,1,0:T(8,128)(2,1)S(1)}, u32[]{:S(2)}, u32[]{:S(2)}) collective-permute-start(bf16[2,2,8,8,1024]{4,3,2,1,0:T(8,128)(2,1)S(1)} %fusion.1.rest_2_.after), channel_id=1, source_target_pairs={{0,1},{1,0},{2,3},{3,2},{4,5},{5,4},{6,7},{7,6},{8,9},{9,8},{10,11... | collective-permute-start | bytes 1572872 | tf_op jit(solution)/shard_map/ppermute | solution.py:36
  54.4 8.8 %collective-permute-start.10 = (bf16[2,8,8,1024]{3,2,1,0:T(8,128)(2,1)S(1)}, bf16[2,8,8,1024]{3,2,1,0:T(8,128)(2,1)S(1)}, u32[]{:S(2)}, u32[]{:S(2)}) collective-permute-start(bf16[2,8,8,1024]{3,2,1,0:T(8,128)(2,1)S(1)} %fusion.2.rest_2_), channel_id=1, source_target_pairs={{0,16},{1,17},{2,18},{3,19},{4,20},{5,21},{6,22},{7,23},{8,24},{9,... | collective-permute-start | bytes 786440 | tf_op jit(solution)/shard_map/ppermute | solution.py:36
  56.8 6.5 %collective-permute-start.9 = (bf16[2,8,8,1024]{3,2,1,0:T(8,128)(2,1)S(1)}, bf16[2,8,8,1024]{3,2,1,0:T(8,128)(2,1)S(1)}, u32[]{:S(2)}, u32[]{:S(2)}) collective-permute-start(bf16[2,8,8,1024]{3,2,1,0:T(8,128)(2,1)S(1)} %fusion.6.rest_1_), channel_id=1, source_target_pairs={{0,1},{1,0},{2,3},{3,2},{4,5},{5,4},{6,7},{7,6},{8,9},{9,8},{10,11... | collective-permute-start | bytes 786440 | tf_op jit(solution)/shard_map/ppermute | solution.py:36
  58.9 6.6 %collective-permute-start.8 = (bf16[2,8,8,1024]{3,2,1,0:T(8,128)(2,1)S(1)}, bf16[2,8,8,1024]{3,2,1,0:T(8,128)(2,1)S(1)}, u32[]{:S(2)}, u32[]{:S(2)}) collective-permute-start(bf16[2,8,8,1024]{3,2,1,0:T(8,128)(2,1)S(1)} %fusion.3.rest_0_), channel_id=1, source_target_pairs={{0,4},{1,5},{2,6},{3,7},{4,0},{5,1},{6,2},{7,3},{8,12},{9,13},{10,... | collective-permute-start | bytes 786440 | tf_op jit(solution)/shard_map/ppermute | solution.py:36
  65.7 6.2 %collective-permute-start.15 = (bf16[8,8,1024]{2,1,0:T(8,128)(2,1)S(1)}, bf16[8,8,1024]{2,1,0:T(8,128)(2,1)S(1)}, u32[]{:S(2)}, u32[]{:S(2)}) collective-permute-start(bf16[8,8,1024]{2,1,0:T(8,128)(2,1)S(1)} %fusion.13.rest_2_), channel_id=1, source_target_pairs={{0,4},{1,5},{2,6},{3,7},{4,0},{5,1},{6,2},{7,3},{8,12},{9,13},{10,... | collective-permute-start | bytes 393224 | tf_op jit(solution)/shard_map/ppermute | solution.py:36
  65.8 6.1 %collective-permute-start.14 = (bf16[8,8,1024]{2,1,0:T(8,128)(2,1)S(1)}, bf16[8,8,1024]{2,1,0:T(8,128)(2,1)S(1)}, u32[]{:S(2)}, u32[]{:S(2)}) collective-permute-start(bf16[8,8,1024]{2,1,0:T(8,128)(2,1)S(1)} %fusion.14.rest_1_), channel_id=1, source_target_pairs={{0,16},{1,17},{2,18},{3,19},{4,20},{5,21},{6,22},{7,23},{8,24},{9,... | collective-permute-start | bytes 393224 | tf_op jit(solution)/shard_map/ppermute | solution.py:36
  67.7 5.0 %collective-permute-start.13 = (bf16[8,8,1024]{2,1,0:T(8,128)(2,1)S(1)}, bf16[8,8,1024]{2,1,0:T(8,128)(2,1)S(1)}, u32[]{:S(2)}, u32[]{:S(2)}) collective-permute-start(bf16[8,8,1024]{2,1,0:T(8,128)(2,1)S(1)} %fusion.15.rest_0_), channel_id=1, source_target_pairs={{0,1},{1,0},{2,3},{3,2},{4,5},{5,4},{6,7},{7,6},{8,9},{9,8},{10,11... | collective-permute-start | bytes 393224 | tf_op jit(solution)/shard_map/ppermute | solution.py:36
  67.9 10.8 %collective-permute-start.11 = (bf16[128,1024]{1,0:T(8,128)(2,1)S(1)}, bf16[128,1024]{1,0:T(8,128)(2,1)}, u32[]{:S(2)}, u32[]{:S(2)}) collective-permute-start(bf16[128,1024]{1,0:T(8,128)(2,1)S(1)} %get-tuple-element.51), channel_id=1, source_target_pairs={{1,2},{2,1},{3,4},{4,3},{5,6},{6,5},{7,8},{8,7},{9,10},{10,9},{11,... | collective-permute-start | bytes 786440 | tf_op jit(solution)/shard_map/ppermute | solution.py:422
  69.3 9.4 %collective-permute-start.12 = (bf16[128,1024]{1,0:T(8,128)(2,1)S(1)}, bf16[128,1024]{1,0:T(8,128)(2,1)}, u32[]{:S(2)}, u32[]{:S(2)}) collective-permute-start(bf16[128,1024]{1,0:T(8,128)(2,1)S(1)} %get-tuple-element.52.refs_3_), channel_id=1, source_target_pairs={{0,1},{1,0},{2,3},{3,2},{4,5},{5,4},{6,7},{7,6},{8,9},{9,8},{10,11... | collective-permute-start | bytes 786440 | tf_op jit(solution)/shard_map/ppermute | solution.py:421
  73.9 15.6 %all-to-all-start = ((bf16[8,8,3072]{2,1,0:T(8,128)(2,1)}), bf16[8,8,3072]{2,1,0:T(8,128)(2,1)S(1)}, u32[]{:S(2)}, u32[]{:S(2)}) async-start(bf16[8,8,3072]{2,1,0:T(8,128)(2,1)} %pad_maximum_fusion.1), calls=%async_computation | async-start | bytes 786432 | tf_op jit(solution)/shard_map/all_to_all | solution.py:97
  78.7 1.4 %copy-start = (bf16[1,512,1024]{2,1,0:T(8,128)(2,1)S(1)}, bf16[1,512,1024]{2,1,0:T(8,128)(2,1)}, u32[]{:S(2)}) copy-start(bf16[1,512,1024]{2,1,0:T(8,128)(2,1)} %param.7) | copy-start | bytes 3145732
  78.7 1.7 %copy-start.1 = (bf16[1,512,1024]{2,1,0:T(8,128)(2,1)S(1)}, bf16[1,512,1024]{2,1,0:T(8,128)(2,1)}, u32[]{:S(2)}) copy-start(bf16[1,512,1024]{2,1,0:T(8,128)(2,1)} %param.8) | copy-start | bytes 3145732

commit v6 on v5

--- a/solution.py
+++ b/solution.py
@@ -171,6 +171,10 @@
     )(*values, after)
 
 
+def pair_columns():
+    return pl.ds(pl.multiple_of(pl.program_id(0) * PAIR, PAIR), PAIR)
+
+
 def front_body(length, target, frames, grads, w_query, w_key, w_value, w_out, ordered, query, keys, values, d_mixed, hidden, masked):
     @pl.when(pl.program_id(0) == 0)
     def _():
@@ -179,11 +183,12 @@
         masked[...] = jnp.where(row < length[0], grads[...].astype(F32), 0.0).astype(BF16)
 
     rows = hidden[...]
-    d_mixed[...] = dot_nt(masked[...], w_out[...]).astype(BF16)
-    query[...] = dot(rows, w_query[...]).astype(BF16)
-    keys[...] = dot(rows, w_key[...]).astype(BF16)
-    values[...] = dot(rows, w_value[...]).astype(BF16)
-    ordered[...] = dot_nt(one_hot(target, pl.program_id(0) * (PAIR // 8), PAIR // 8), rows).astype(BF16)
+    now = pair_columns()
+    d_mixed[:, now] = dot_nt(masked[...], w_out[...]).astype(BF16)
+    query[:, now] = dot(rows, w_query[...]).astype(BF16)
+    keys[:, now] = dot(rows, w_key[...]).astype(BF16)
+    values[:, now] = dot(rows, w_value[...]).astype(BF16)
+    ordered[now] = dot_nt(one_hot(target, pl.program_id(0) * (PAIR // 8), PAIR // 8), rows).astype(BF16)
 
 
 def front(length, target, frames, grads, w_query, w_key, w_value, w_out):
@@ -193,20 +198,16 @@
         [jax.ShapeDtypeStruct((D, ROWS), BF16), wide, wide, wide, wide],
         (length, target, frames, grads, w_query, w_key, w_value, w_out),
         [SCALAR, SCALAR, whole(ROWS, D), whole(ROWS, D)] + [columns(D)] * 3 + [pl.BlockSpec((PAIR, D), lambda j: (j, 0))],
-        [pl.BlockSpec((PAIR, ROWS), lambda j: (j, 0))] + [columns(ROWS)] * 4,
+        [HELD] * 5,
         [pltpu.VMEM((ROWS, D), BF16)] * 2,
         5 * ROWS * D * D,
         room=ROOM[0],
     )
 
 
-def pair_columns():
-    return pl.ds(pl.multiple_of(pl.program_id(0) * PAIR, PAIR), PAIR)
-
-
 def attend_body(
     length, target, low, high, query_all, keys_all, values_all, d_mixed_all, w_key, w_value,
-    grad_query, grad_key, grad_value, border_grads, ordered_border,
+    grad_query_all, grad_key_all, grad_value_all, border_grads_all, ordered_border,
     hidden_border, key_value, pair, score_t, prob_t,
 ):
     scale = HDIM ** (-0.5)
@@ -230,6 +231,10 @@
     query, keys, values, d_mixed = (
         ref.at[:, pair_columns()] for ref in (query_all, keys_all, values_all, d_mixed_all)
     )
+    grad_query, grad_key, grad_value = (
+        ref.at[:, pair_columns()] for ref in (grad_query_all, grad_key_all, grad_value_all)
+    )
+    border_grads = border_grads_all.at[:, :, pair_columns()]
     key_border = dot(hidden_border[...], w_key[...]).astype(BF16)
     value_border = dot(hidden_border[...], w_value[...]).astype(BF16)
     above = lax.broadcasted_iota(jnp.int32, (3 * WIN, WIN), 0)
@@ -309,7 +314,7 @@
         [own] * 3 + [jax.ShapeDtypeStruct((2, 2 * WIN, D), BF16), jax.ShapeDtypeStruct((D, 2 * WIN), BF16)],
         (length, target, low, high, query, keys, values, d_mixed, w_key, w_value),
         [SCALAR, SCALAR, whole(WIN, D), whole(WIN, D)] + [HELD] * 4 + [columns(D)] * 2,
-        [columns(ROWS)] * 3 + [pl.BlockSpec((2, 2 * WIN, PAIR), lambda j: (0, 0, j)), whole(D, 2 * WIN)],
+        [HELD] * 5,
         [
             pltpu.VMEM((2 * WIN, D), BF16),
             pltpu.VMEM((2, reach, PAIR), BF16),
@@ -325,8 +330,8 @@
 def project_body(ordered, grad, kept, sent):
     half = D // 2
     columns = grad[:, pair_columns()]
-    sent[...] = dot(ordered[half:], columns).astype(BF16)
-    kept[...] = dot(ordered[:half], columns).astype(BF16)
+    sent[:, pair_columns()] = dot(ordered[half:], columns).astype(BF16)
+    kept[:, pair_columns()] = dot(ordered[:half], columns).astype(BF16)
 
 
 def project_border_body(part, ordered, grad, ordered_border, border_grads, *rest):
@@ -334,19 +339,19 @@
     half = D // 2
     columns, border_columns = grad[:, pair_columns()], border_grads[part - 1, :, pair_columns()]
     for out, rows in ((sent, slice(half, D)), (kept, slice(0, half))):
-        out[...] = (dot(ordered[rows], columns) + dot(ordered_border[rows], border_columns)).astype(BF16)
+        out[:, pair_columns()] = (dot(ordered[rows], columns) + dot(ordered_border[rows], border_columns)).astype(BF16)
 
 
 def project(part, *ins):
     half = jax.ShapeDtypeStruct((D // 2, D), BF16)
     body = functools.partial(project_border_body, part) if part else project_body
     specs = [HELD] * min(len(ins), 4) + [AFTER] * (len(ins) - 4)
-    return call(body, [half] * 2, ins, specs, [columns(D // 2)] * 2, [], D * D * (ROWS + 2 * WIN), room=20)
+    return call(body, [half] * 2, ins, specs, [HELD] * 2, [], D * D * (ROWS + 2 * WIN), room=20)
 
 
 def back_body(grad_query, grad_key, grad_value, w_query, w_key, w_value, *rest):
     total = rest[-1]
-    total[...] = (
+    total[:, pair_columns()] = (
         dot_nt(grad_query[...], w_query[...]) + dot_nt(grad_key[...], w_key[...]) + dot_nt(grad_value[...], w_value[...])
     )
 
@@ -361,7 +366,7 @@
         jax.ShapeDtypeStruct((ROWS, D), F32),
         ins,
         [HELD] * 3 + [rows_of(D)] * 3 + [AFTER] * 3,
-        columns(ROWS),
+        HELD,
         [],
         3 * ROWS * D * D,
         room=24,
@@ -370,7 +375,7 @@
 
 def back_border_body(grads, w_key, w_value, *rest):
     sides = rest[-1]
-    sides[...] = (dot_nt(grads[0], w_key[...]) + dot_nt(grads[1], w_value[...])).astype(BF16)
+    sides[:, pair_columns()] = (dot_nt(grads[0], w_key[...]) + dot_nt(grads[1], w_value[...])).astype(BF16)
 
 
 def back_border(*ins):
@@ -379,7 +384,7 @@
         jax.ShapeDtypeStruct((2 * WIN, D), BF16),
         ins,
         [HELD] + [rows_of(D)] * 2 + [AFTER] * 3,
-        columns(2 * WIN),
+        HELD,
         [],
         4 * WIN * D * D,
         room=16,

time: 90.7 us -> 89 us (0.981)
  Pallas kernels: 43.4 us -> 41.7 us
    pallas_call x9, Pallas kernels: 43.4 us -> 41.7 us  [call(): pl.pallas_call(body, out_shape=outs, grid=(steps,), in_specs=in_specs, ou...]
  transfers between devices with their start and end apart: 17 -> 17, of which waited for: 6 -> 6; matrix products, arithmetic and copies ran while one was open for 4% -> 4% of each run, Pallas kernels for 31% -> 30%
where the time goes in v6:
time: 89 us; the launch traced here: 88.5 us
  Pallas kernels  41.7 us (47%)
  starting transfers between devices  28.5 us (32%)
  waiting for transfers between devices  11 us (12%)
  other arithmetic  4.61 us (5%)
  between operations  1.59 us (2%)
    pallas_call x9, Pallas kernels, call(): pl.pallas_call(body, out_shape=outs, grid=(steps,), in_specs=in_specs, ou...  41.7 us
    ppermute x12, starting transfers between devices, exchange(): return lax.ppermute(value, AXES, pairs)  13.8 us
    ppermute x2, starting transfers between devices, send(): return lax.ppermute(rows, 'tm', [(i, i ^ 1) for i in range(count)])  7.85 us
    all_to_all x1, waiting for transfers between devices, scatter_sum(): lax.all_to_all(value.reshape(64, -1), AXES, 0, 0, axis_index_groups=last_...  6.44 us
    all_to_all x1, starting transfers between devices, scatter_sum(): lax.all_to_all(value.reshape(64, -1), AXES, 0, 0, axis_index_groups=last_...  4.77 us
    ppermute x12, waiting for transfers between devices, exchange(): return lax.ppermute(value, AXES, pairs)  4.51 us
    ppermute x2, starting transfers between devices, send(): lax.ppermute(rows, 'tm', [(i, i + 1 if i % 2 else i - 1) for i in range(1...  2.05 us
  transfers between devices with their start and end apart: 17, of which 6 were waited for; matrix products, arithmetic and copies ran while one was open for 4% of the time, Pallas kernels for 30%

profile of v6, /device:TPU:0, one launch (start us, length us, event | category | flops | bytes accessed | tf_op | source)
XLA Modules:
  0.0 88.5 jit_solution(11486333675792002275)
XLA Ops:
  0.6 1.1 %select_bitcast_fusion = (bf16[128,1024]{1,0:T(8,128)(2,1)S(1)}, bf16[128,1024]{1,0:T(8,128)(2,1)S(1)}) fusion(pred[]{:T(512)S(6)} %eq.26, bf16[1,512,1024]{2,1,0:T(8,128)(2,1)} %param.7), kind=kLoop, calls=%fused_computation.39 | loop fusion | flops 262144 | bytes 1048577 | tf_op jit(solution)/shard_map/jit(_where)/select_n | solution.py:420
  1.7 0.7 collective-permute-start
  2.4 5.2 %collective-permute-start.1 = (bf16[128,1024]{1,0:T(8,128)(2,1)S(1)}, bf16[128,1024]{1,0:T(8,128)(2,1)S(1)}, u32[]{:S(2)}, u32[]{:S(2)}) collective-permute-start(bf16[128,1024]{1,0:T(8,128)(2,1)S(1)} %get-tuple-element.56), channel_id=1, source_target_pairs={{0,1},{1,0},{2,3},{3,2},{4,5},{5,4},{6,7},{7,6},{8,9},{9,8},{10,11... | collective-permute-start | bytes 786440 | tf_op jit(solution)/shard_map/ppermute | solution.py:426
  8.3 9.7 %shard_map.86 = (bf16[1024,512]{1,0:T(8,128)(2,1)S(1)}, bf16[512,1024]{1,0:T(8,128)(2,1)S(1)}, bf16[512,1024]{1,0:T(8,128)(2,1)S(1)}, bf16[512,1024]{1,0:T(8,128)(2,1)S(1)}, bf16[512,1024]{1,0:T(8,128)(2,1)S(1)}) custom-call(s32[1]{0:T(128)S(6)} %copy.35.length, s32[128]{0:T(128)S(1)} %multiply_xor_fusion.target, bf16[512,1024]{1,0:T(8,128)(2,1)} %bitcast.88, ...), custom_call_target="tpu_custom_call" | custom-call | flops 5368709120 | bytes 15729156 | tf_op jit(solution)/shard_map/pallas_call | solution.py:123
  18.0 0.0 collective-permute-done
  18.0 0.0 collective-permute-done.1
  18.1 13.0 %shard_map.87 = (bf16[512,1024]{1,0:T(8,128)(2,1)S(1)}, bf16[512,1024]{1,0:T(8,128)(2,1)S(1)}, bf16[512,1024]{1,0:T(8,128)(2,1)S(1)}, bf16[2,256,1024]{2,1,0:T(8,128)(2,1)S(1)}, bf16[1024,256]{1,0:T(8,128)(2,1)S(1)}) custom-call(s32[1]{0:T(128)S(6)} %copy.35.length, s32[128]{0:T(128)S(1)} %multiply_xor_fusion.target, ...), custom_call_target="tpu_custom_call" | custom-call | flops 5100273664 | bytes 13632004 | tf_op jit(solution)/shard_map/pallas_call | solution.py:123
  31.0 1.8 %shard_map.88 = (bf16[512,1024]{1,0:T(8,128)(2,1)S(1)}, bf16[512,1024]{1,0:T(8,128)(2,1)S(1)}) custom-call(bf16[1024,512]{1,0:T(8,128)(2,1)S(1)} %get-tuple-element.36.ordered, bf16[512,1024]{1,0:T(8,128)(2,1)S(1)} %get-tuple-element.33.grad.grad_query), custom_call_target="tpu_custom_call" | custom-call | flops 1610612736 | bytes 4194304 | tf_op jit(solution)/shard_map/pallas_call | solution.py:123
  32.8 0.1 collective-permute-start.2
  32.9 2.4 %shard_map.89 = (bf16[512,1024]{1,0:T(8,128)(2,1)S(1)}, bf16[512,1024]{1,0:T(8,128)(2,1)S(1)}) custom-call(bf16[1024,512]{1,0:T(8,128)(2,1)S(1)} %get-tuple-element.36.ordered, bf16[512,1024]{1,0:T(8,128)(2,1)S(1)} %get-tuple-element.34.grad.grad_key, bf16[1024,256]{1,0:T(8,128)(2,1)S(1)} %get-tuple-element.39.ordered_border, ...), custom_call_target="tpu_custom_call" | custom-call | flops 1610612736 | bytes 5767168 | tf_op jit(solution)/shard_map/pallas_call | solution.py:123
  35.3 0.6 collective-permute-start.3
  35.8 0.0 collective-permute-done.2
  35.8 0.2 add_convert_fusion.2
  36.0 2.4 %shard_map.90 = (bf16[512,1024]{1,0:T(8,128)(2,1)S(1)}, bf16[512,1024]{1,0:T(8,128)(2,1)S(1)}) custom-call(bf16[1024,512]{1,0:T(8,128)(2,1)S(1)} %get-tuple-element.36.ordered, bf16[512,1024]{1,0:T(8,128)(2,1)S(1)} %get-tuple-element.35.grad.grad_value, bf16[1024,256]{1,0:T(8,128)(2,1)S(1)} %get-tuple-element.39.ordered_border, ...), custom_call_target="tpu_custom_call" | custom-call | flops 1610612736 | bytes 6291456 | tf_op jit(solution)/shard_map/pallas_call | solution.py:123
  38.4 0.1 collective-permute-start.4
  38.5 4.2 %collective-permute-start.5 = (bf16[2,2,8,8,1024]{4,3,2,1,0:T(8,128)(2,1)S(1)}, bf16[2,2,8,8,1024]{4,3,2,1,0:T(8,128)(2,1)S(1)}, u32[]{:S(2)}, u32[]{:S(2)}) collective-permute-start(bf16[2,2,8,8,1024]{4,3,2,1,0:T(8,128)(2,1)S(1)} %bitcast.91), channel_id=1, source_target_pairs={{0,16},{1,17},{2,18},{3,19},{4,20},{5,21},{6,22},{7,23},{8,24},{9,... | collective-permute-start | bytes 1572872 | tf_op jit(solution)/shard_map/ppermute | solution.py:36
  42.8 0.0 collective-permute-done.3
  42.8 0.2 fusion.rest_1_
  43.0 0.1 collective-permute-start.6
  43.1 0.0 collective-permute-done.4
  43.1 0.2 fusion.1.rest_2_.after
  43.3 2.1 %collective-permute-start.7 = (bf16[2,2,8,8,1024]{4,3,2,1,0:T(8,128)(2,1)S(1)}, bf16[2,2,8,8,1024]{4,3,2,1,0:T(8,128)(2,1)S(1)}, u32[]{:S(2)}, u32[]{:S(2)}) collective-permute-start(bf16[2,2,8,8,1024]{4,3,2,1,0:T(8,128)(2,1)S(1)} %fusion.1.rest_2_.after), channel_id=1, source_target_pairs={{0,1},{1,0},{2,3},{3,2},{4,5},{5,4},{6,7},{7,6},{8,9},{9,8},{10,11... | collective-permute-start | bytes 1572872 | tf_op jit(solution)/shard_map/ppermute | solution.py:36
  45.4 0.1 convert_add_fusion.2
  45.5 5.9 %shard_map.91.refs_3_.d_hidden = f32[512,1024]{1,0:T(8,128)S(1)} custom-call(bf16[512,1024]{1,0:T(8,128)(2,1)S(1)} %get-tuple-element.33.grad.grad_query, bf16[512,1024]{1,0:T(8,128)(2,1)S(1)} %get-tuple-element.34.grad.grad_key, bf16[512,1024]{1,0:T(8,128)(2,1)S(1)} %get-tuple-element.35.grad.grad_value, bf16[1024,1024]{1,0:T(8,128)(2,1)} %w_query.3, ...), custom_call_target="tpu_custom_call" | custom-call | flops 3221225472 | bytes 13107200 | tf_op jit(solution)/shard_map/pallas_call | solution.py:123
  51.4 0.9 collective-permute-done.6.refs_1_
  52.2 0.0 collective-permute-done.5.refs_0_
  52.2 0.3 collective-permute-done.7.refs_2_
  52.6 0.1 fusion.2.rest_2_
  52.7 2.2 %collective-permute-start.10 = (bf16[2,8,8,1024]{3,2,1,0:T(8,128)(2,1)S(1)}, bf16[2,8,8,1024]{3,2,1,0:T(8,128)(2,1)S(1)}, u32[]{:S(2)}, u32[]{:S(2)}) collective-permute-start(bf16[2,8,8,1024]{3,2,1,0:T(8,128)(2,1)S(1)} %fusion.2.rest_2_), channel_id=1, source_target_pairs={{0,16},{1,17},{2,18},{3,19},{4,20},{5,21},{6,22},{7,23},{8,24},{9,... | collective-permute-start | bytes 786440 | tf_op jit(solution)/shard_map/ppermute | solution.py:36
  55.0 0.1 fusion.6.rest_1_
  55.1 2.1 %collective-permute-start.9 = (bf16[2,8,8,1024]{3,2,1,0:T(8,128)(2,1)S(1)}, bf16[2,8,8,1024]{3,2,1,0:T(8,128)(2,1)S(1)}, u32[]{:S(2)}, u32[]{:S(2)}) collective-permute-start(bf16[2,8,8,1024]{3,2,1,0:T(8,128)(2,1)S(1)} %fusion.6.rest_1_), channel_id=1, source_target_pairs={{0,1},{1,0},{2,3},{3,2},{4,5},{5,4},{6,7},{7,6},{8,9},{9,8},{10,11... | collective-permute-start | bytes 786440 | tf_op jit(solution)/shard_map/ppermute | solution.py:36
  57.2 0.1 fusion.3.rest_0_
  57.2 0.3 collective-permute-start.8
  57.5 3.9 %shard_map.93.refs_3_.sides = bf16[256,1024]{1,0:T(8,128)(2,1)S(1)} custom-call(bf16[2,256,1024]{2,1,0:T(8,128)(2,1)S(1)} %get-tuple-element.40.border_grads.grads, bf16[1024,1024]{1,0:T(8,128)(2,1)} %w_key.7, bf16[1024,1024]{1,0:T(8,128)(2,1)} %w_value.7, bf16[2,8,8,1024]{3,2,1,0:T(8,128)(2,1)S(1)} %fusion.3.rest_0_, ...), custom_call_target="tpu_custom_call" | custom-call | flops 1073741824 | bytes 6553600 | tf_op jit(solution)/shard_map/pallas_call | solution.py:123
  61.4 0.0 collective-permute-done.10.refs_2_
  61.5 0.1 collective-permute-done.9.refs_1_
  61.5 2.3 %collective-permute-done.8.refs_0_ = bf16[2,8,8,1024]{3,2,1,0:T(8,128)(2,1)S(1)} collective-permute-done((bf16[2,8,8,1024]{3,2,1,0:T(8,128)(2,1)S(1)}, bf16[2,8,8,1024]{3,2,1,0:T(8,128)(2,1)S(1)}, u32[]{:S(2)}, u32[]{:S(2)}) %collective-permute-start.8) | collective-permute-done | bytes 262176 | tf_op jit(solution)/shard_map/ppermute | solution.py:36
  63.9 0.1 fusion.13.rest_2_
  63.9 0.1 fusion.14.rest_1_
  64.0 0.1 collective-permute-start.15
  64.1 1.9 %collective-permute-start.14 = (bf16[8,8,1024]{2,1,0:T(8,128)(2,1)S(1)}, bf16[8,8,1024]{2,1,0:T(8,128)(2,1)S(1)}, u32[]{:S(2)}, u32[]{:S(2)}) collective-permute-start(bf16[8,8,1024]{2,1,0:T(8,128)(2,1)S(1)} %fusion.14.rest_1_), channel_id=1, source_target_pairs={{0,16},{1,17},{2,18},{3,19},{4,20},{5,21},{6,22},{7,23},{8,24},{9,... | collective-permute-start | bytes 393224 | tf_op jit(solution)/shard_map/ppermute | solution.py:36
  66.0 0.1 fusion.15.rest_0_
  66.0 0.1 collective-permute-start.13
  66.1 0.1 shard_map.95
  66.2 1.4 %collective-permute-start.11 = (bf16[128,1024]{1,0:T(8,128)(2,1)S(1)}, bf16[128,1024]{1,0:T(8,128)(2,1)}, u32[]{:S(2)}, u32[]{:S(2)}) collective-permute-start(bf16[128,1024]{1,0:T(8,128)(2,1)S(1)} %get-tuple-element.51), channel_id=1, source_target_pairs={{1,2},{2,1},{3,4},{4,3},{5,6},{6,5},{7,8},{8,7},{9,10},{10,9},{11,... | collective-permute-start | bytes 786440 | tf_op jit(solution)/shard_map/ppermute | solution.py:427
  67.6 2.6 %collective-permute-start.12 = (bf16[128,1024]{1,0:T(8,128)(2,1)S(1)}, bf16[128,1024]{1,0:T(8,128)(2,1)}, u32[]{:S(2)}, u32[]{:S(2)}) collective-permute-start(bf16[128,1024]{1,0:T(8,128)(2,1)S(1)} %get-tuple-element.52.refs_3_), channel_id=1, source_target_pairs={{0,1},{1,0},{2,3},{3,2},{4,5},{5,4},{6,7},{7,6},{8,9},{9,8},{10,11... | collective-permute-start | bytes 786440 | tf_op jit(solution)/shard_map/ppermute | solution.py:426
  70.2 0.0 collective-permute-done.15.refs_2_
  70.2 0.0 collective-permute-done.14.refs_1_
  70.2 0.9 collective-permute-done.13.refs_0_
  71.1 0.2 fusion.8
  71.3 0.1 fusion.12
  71.4 0.8 pad_maximum_fusion.1
  72.2 4.8 %all-to-all-start = ((bf16[8,8,3072]{2,1,0:T(8,128)(2,1)}), bf16[8,8,3072]{2,1,0:T(8,128)(2,1)S(1)}, u32[]{:S(2)}, u32[]{:S(2)}) async-start(bf16[8,8,3072]{2,1,0:T(8,128)(2,1)} %pad_maximum_fusion.1), calls=%async_computation | async-start | bytes 786432 | tf_op jit(solution)/shard_map/all_to_all | solution.py:97
  77.0 0.0 copy-start
  77.0 0.0 copy-start.1
  77.0 0.0 collective-permute-done.11
  77.0 0.0 collective-permute-done.12
  77.0 1.2 %broadcast_select_fusion.1 = (bf16[128,1024]{1,0:T(8,128)(2,1)S(1)}, bf16[128,1024]{1,0:T(8,128)(2,1)S(1)}) fusion(bf16[128,1024]{1,0:T(8,128)(2,1)} %collective-permute-done.11, bf16[128,1024]{1,0:T(8,128)(2,1)} %collective-permute-done.12, pred[]{:T(512)S(6)} %eq.26), kind=kLoop, calls=%fused_computation.42 | loop fusion | flops 262144 | bytes 1048577 | tf_op jit(solution)/shard_map/jit(_where)/select_n | solution.py:452
  78.3 0.1 copy-done
  78.3 0.3 copy-done.1
  78.7 2.6 %shard_map.96 = bf16[512,1024]{1,0:T(8,128)(2,1)} custom-call(bf16[512,1024]{1,0:T(8,128)(2,1)S(1)} %bitcast.89, bf16[512,1024]{1,0:T(8,128)(2,1)S(1)} %bitcast.100, f32[512,1024]{1,0:T(8,128)S(1)} %shard_map.91.refs_3_.d_hidden, bf16[256,1024]{1,0:T(8,128)(2,1)S(1)} %pad_maximum_fusion.near, bf16[2,2,8,8,1024]{4,3,2,1,0:T(8,128)(2,1)S(1)} %fusion.1.rest_2_.after), custom_call_target="tpu_custom_call" | custom-call | flops 16777216 | bytes 6291456 | tf_op jit(solution)/shard_map/pallas_call | solution.py:123
  81.3 6.4 %all-to-all-done = bf16[8,8,3072]{2,1,0:T(8,128)(2,1)S(1)} async-done(((bf16[8,8,3072]{2,1,0:T(8,128)(2,1)}), bf16[8,8,3072]{2,1,0:T(8,128)(2,1)S(1)}, u32[]{:S(2)}, u32[]{:S(2)}) %all-to-all-start) | async-done | bytes 393248 | tf_op jit(solution)/shard_map/all_to_all | solution.py:97
  87.7 0.8 fusion.4
  (9 shorter events, 0.2 us)
Async XLA Ops:
  1.7 16.3 %collective-permute-start = (bf16[128,1024]{1,0:T(8,128)(2,1)S(1)}, bf16[128,1024]{1,0:T(8,128)(2,1)S(1)}, u32[]{:S(2)}, u32[]{:S(2)}) collective-permute-start(bf16[128,1024]{1,0:T(8,128)(2,1)S(1)} %get-tuple-element.57), channel_id=1, source_target_pairs={{1,2},{2,1},{3,4},{4,3},{5,6},{6,5},{7,8},{8,7},{9,10},{10,9},{11,... | collective-permute-start | bytes 786440 | tf_op jit(solution)/shard_map/ppermute | solution.py:427
  2.4 15.6 %collective-permute-start.1 = (bf16[128,1024]{1,0:T(8,128)(2,1)S(1)}, bf16[128,1024]{1,0:T(8,128)(2,1)S(1)}, u32[]{:S(2)}, u32[]{:S(2)}) collective-permute-start(bf16[128,1024]{1,0:T(8,128)(2,1)S(1)} %get-tuple-element.56), channel_id=1, source_target_pairs={{0,1},{1,0},{2,3},{3,2},{4,5},{5,4},{6,7},{7,6},{8,9},{9,8},{10,11... | collective-permute-start | bytes 786440 | tf_op jit(solution)/shard_map/ppermute | solution.py:426
  32.8 3.0 %collective-permute-start.2 = (bf16[512,1024]{1,0:T(8,128)(2,1)S(1)}, bf16[512,1024]{1,0:T(8,128)(2,1)S(1)}, u32[]{:S(2)}, u32[]{:S(2)}) collective-permute-start(bf16[512,1024]{1,0:T(8,128)(2,1)S(1)} %get-tuple-element.38), channel_id=1, source_target_pairs={{0,32},{1,33},{2,34},{3,35},{4,36},{5,37},{6,38},{7,39},{8,40},{9,... | collective-permute-start | bytes 3145736 | tf_op jit(solution)/shard_map/ppermute | solution.py:36
  35.3 7.5 %collective-permute-start.3 = (bf16[512,1024]{1,0:T(8,128)(2,1)S(1)}, bf16[512,1024]{1,0:T(8,128)(2,1)S(1)}, u32[]{:S(2)}, u32[]{:S(2)}) collective-permute-start(bf16[512,1024]{1,0:T(8,128)(2,1)S(1)} %get-tuple-element.42), channel_id=1, source_target_pairs={{0,32},{1,33},{2,34},{3,35},{4,36},{5,37},{6,38},{7,39},{8,40},{9,... | collective-permute-start | bytes 3145736 | tf_op jit(solution)/shard_map/ppermute | solution.py:36
  38.4 4.7 %collective-permute-start.4 = (bf16[512,1024]{1,0:T(8,128)(2,1)S(1)}, bf16[512,1024]{1,0:T(8,128)(2,1)S(1)}, u32[]{:S(2)}, u32[]{:S(2)}) collective-permute-start(bf16[512,1024]{1,0:T(8,128)(2,1)S(1)} %get-tuple-element.44), channel_id=1, source_target_pairs={{0,32},{1,33},{2,34},{3,35},{4,36},{5,37},{6,38},{7,39},{8,40},{9,... | collective-permute-start | bytes 3145736 | tf_op jit(solution)/shard_map/ppermute | solution.py:36
  38.5 13.7 %collective-permute-start.5 = (bf16[2,2,8,8,1024]{4,3,2,1,0:T(8,128)(2,1)S(1)}, bf16[2,2,8,8,1024]{4,3,2,1,0:T(8,128)(2,1)S(1)}, u32[]{:S(2)}, u32[]{:S(2)}) collective-permute-start(bf16[2,2,8,8,1024]{4,3,2,1,0:T(8,128)(2,1)S(1)} %bitcast.91), channel_id=1, source_target_pairs={{0,16},{1,17},{2,18},{3,19},{4,20},{5,21},{6,22},{7,23},{8,24},{9,... | collective-permute-start | bytes 1572872 | tf_op jit(solution)/shard_map/ppermute | solution.py:36
  43.0 9.3 %collective-permute-start.6 = (bf16[2,2,8,8,1024]{4,3,2,1,0:T(8,128)(2,1)S(1)}, bf16[2,2,8,8,1024]{4,3,2,1,0:T(8,128)(2,1)S(1)}, u32[]{:S(2)}, u32[]{:S(2)}) collective-permute-start(bf16[2,2,8,8,1024]{4,3,2,1,0:T(8,128)(2,1)S(1)} %fusion.rest_1_), channel_id=1, source_target_pairs={{0,4},{1,5},{2,6},{3,7},{4,0},{5,1},{6,2},{7,3},{8,12},{9,13},{10,... | collective-permute-start | bytes 1572872 | tf_op jit(solution)/shard_map/ppermute | solution.py:36
  43.3 9.3 %collective-permute-start.7 = (bf16[2,2,8,8,1024]{4,3,2,1,0:T(8,128)(2,1)S(1)}, bf16[2,2,8,8,1024]{4,3,2,1,0:T(8,128)(2,1)S(1)}, u32[]{:S(2)}, u32[]{:S(2)}) collective-permute-start(bf16[2,2,8,8,1024]{4,3,2,1,0:T(8,128)(2,1)S(1)} %fusion.1.rest_2_.after), channel_id=1, source_target_pairs={{0,1},{1,0},{2,3},{3,2},{4,5},{5,4},{6,7},{7,6},{8,9},{9,8},{10,11... | collective-permute-start | bytes 1572872 | tf_op jit(solution)/shard_map/ppermute | solution.py:36
  52.7 8.7 %collective-permute-start.10 = (bf16[2,8,8,1024]{3,2,1,0:T(8,128)(2,1)S(1)}, bf16[2,8,8,1024]{3,2,1,0:T(8,128)(2,1)S(1)}, u32[]{:S(2)}, u32[]{:S(2)}) collective-permute-start(bf16[2,8,8,1024]{3,2,1,0:T(8,128)(2,1)S(1)} %fusion.2.rest_2_), channel_id=1, source_target_pairs={{0,16},{1,17},{2,18},{3,19},{4,20},{5,21},{6,22},{7,23},{8,24},{9,... | collective-permute-start | bytes 786440 | tf_op jit(solution)/shard_map/ppermute | solution.py:36
  55.1 6.5 %collective-permute-start.9 = (bf16[2,8,8,1024]{3,2,1,0:T(8,128)(2,1)S(1)}, bf16[2,8,8,1024]{3,2,1,0:T(8,128)(2,1)S(1)}, u32[]{:S(2)}, u32[]{:S(2)}) collective-permute-start(bf16[2,8,8,1024]{3,2,1,0:T(8,128)(2,1)S(1)} %fusion.6.rest_1_), channel_id=1, source_target_pairs={{0,1},{1,0},{2,3},{3,2},{4,5},{5,4},{6,7},{7,6},{8,9},{9,8},{10,11... | collective-permute-start | bytes 786440 | tf_op jit(solution)/shard_map/ppermute | solution.py:36
  57.2 6.6 %collective-permute-start.8 = (bf16[2,8,8,1024]{3,2,1,0:T(8,128)(2,1)S(1)}, bf16[2,8,8,1024]{3,2,1,0:T(8,128)(2,1)S(1)}, u32[]{:S(2)}, u32[]{:S(2)}) collective-permute-start(bf16[2,8,8,1024]{3,2,1,0:T(8,128)(2,1)S(1)} %fusion.3.rest_0_), channel_id=1, source_target_pairs={{0,4},{1,5},{2,6},{3,7},{4,0},{5,1},{6,2},{7,3},{8,12},{9,13},{10,... | collective-permute-start | bytes 786440 | tf_op jit(solution)/shard_map/ppermute | solution.py:36
  64.0 6.2 %collective-permute-start.15 = (bf16[8,8,1024]{2,1,0:T(8,128)(2,1)S(1)}, bf16[8,8,1024]{2,1,0:T(8,128)(2,1)S(1)}, u32[]{:S(2)}, u32[]{:S(2)}) collective-permute-start(bf16[8,8,1024]{2,1,0:T(8,128)(2,1)S(1)} %fusion.13.rest_2_), channel_id=1, source_target_pairs={{0,4},{1,5},{2,6},{3,7},{4,0},{5,1},{6,2},{7,3},{8,12},{9,13},{10,... | collective-permute-start | bytes 393224 | tf_op jit(solution)/shard_map/ppermute | solution.py:36
  64.1 6.1 %collective-permute-start.14 = (bf16[8,8,1024]{2,1,0:T(8,128)(2,1)S(1)}, bf16[8,8,1024]{2,1,0:T(8,128)(2,1)S(1)}, u32[]{:S(2)}, u32[]{:S(2)}) collective-permute-start(bf16[8,8,1024]{2,1,0:T(8,128)(2,1)S(1)} %fusion.14.rest_1_), channel_id=1, source_target_pairs={{0,16},{1,17},{2,18},{3,19},{4,20},{5,21},{6,22},{7,23},{8,24},{9,... | collective-permute-start | bytes 393224 | tf_op jit(solution)/shard_map/ppermute | solution.py:36
  66.0 5.0 %collective-permute-start.13 = (bf16[8,8,1024]{2,1,0:T(8,128)(2,1)S(1)}, bf16[8,8,1024]{2,1,0:T(8,128)(2,1)S(1)}, u32[]{:S(2)}, u32[]{:S(2)}) collective-permute-start(bf16[8,8,1024]{2,1,0:T(8,128)(2,1)S(1)} %fusion.15.rest_0_), channel_id=1, source_target_pairs={{0,1},{1,0},{2,3},{3,2},{4,5},{5,4},{6,7},{7,6},{8,9},{9,8},{10,11... | collective-permute-start | bytes 393224 | tf_op jit(solution)/shard_map/ppermute | solution.py:36
  66.2 10.8 %collective-permute-start.11 = (bf16[128,1024]{1,0:T(8,128)(2,1)S(1)}, bf16[128,1024]{1,0:T(8,128)(2,1)}, u32[]{:S(2)}, u32[]{:S(2)}) collective-permute-start(bf16[128,1024]{1,0:T(8,128)(2,1)S(1)} %get-tuple-element.51), channel_id=1, source_target_pairs={{1,2},{2,1},{3,4},{4,3},{5,6},{6,5},{7,8},{8,7},{9,10},{10,9},{11,... | collective-permute-start | bytes 786440 | tf_op jit(solution)/shard_map/ppermute | solution.py:427
  67.6 9.4 %collective-permute-start.12 = (bf16[128,1024]{1,0:T(8,128)(2,1)S(1)}, bf16[128,1024]{1,0:T(8,128)(2,1)}, u32[]{:S(2)}, u32[]{:S(2)}) collective-permute-start(bf16[128,1024]{1,0:T(8,128)(2,1)S(1)} %get-tuple-element.52.refs_3_), channel_id=1, source_target_pairs={{0,1},{1,0},{2,3},{3,2},{4,5},{5,4},{6,7},{7,6},{8,9},{9,8},{10,11... | collective-permute-start | bytes 786440 | tf_op jit(solution)/shard_map/ppermute | solution.py:426
  72.2 15.5 %all-to-all-start = ((bf16[8,8,3072]{2,1,0:T(8,128)(2,1)}), bf16[8,8,3072]{2,1,0:T(8,128)(2,1)S(1)}, u32[]{:S(2)}, u32[]{:S(2)}) async-start(bf16[8,8,3072]{2,1,0:T(8,128)(2,1)} %pad_maximum_fusion.1), calls=%async_computation | async-start | bytes 786432 | tf_op jit(solution)/shard_map/all_to_all | solution.py:97
  77.0 1.4 %copy-start = (bf16[1,512,1024]{2,1,0:T(8,128)(2,1)S(1)}, bf16[1,512,1024]{2,1,0:T(8,128)(2,1)}, u32[]{:S(2)}) copy-start(bf16[1,512,1024]{2,1,0:T(8,128)(2,1)} %param.7) | copy-start | bytes 3145732
  77.0 1.7 %copy-start.1 = (bf16[1,512,1024]{2,1,0:T(8,128)(2,1)S(1)}, bf16[1,512,1024]{2,1,0:T(8,128)(2,1)}, u32[]{:S(2)}) copy-start(bf16[1,512,1024]{2,1,0:T(8,128)(2,1)} %param.8) | copy-start | bytes 3145732

commit v7 on v6

--- a/solution.py
+++ b/solution.py
@@ -329,24 +329,25 @@
 
 def project_body(ordered, grad, kept, sent):
     half = D // 2
-    columns = grad[:, pair_columns()]
-    sent[:, pair_columns()] = dot(ordered[half:], columns).astype(BF16)
-    kept[:, pair_columns()] = dot(ordered[:half], columns).astype(BF16)
+    for now in (slice(j * PAIR, (j + 1) * PAIR) for j in range(STEPS)):
+        sent[:, now] = dot(ordered[half:], grad[:, now]).astype(BF16)
+        kept[:, now] = dot(ordered[:half], grad[:, now]).astype(BF16)
 
 
 def project_border_body(part, ordered, grad, ordered_border, border_grads, *rest):
     kept, sent = rest[-2:]
     half = D // 2
-    columns, border_columns = grad[:, pair_columns()], border_grads[part - 1, :, pair_columns()]
-    for out, rows in ((sent, slice(half, D)), (kept, slice(0, half))):
-        out[:, pair_columns()] = (dot(ordered[rows], columns) + dot(ordered_border[rows], border_columns)).astype(BF16)
+    for now in (slice(j * PAIR, (j + 1) * PAIR) for j in range(STEPS)):
+        for out, rows in ((sent, slice(half, D)), (kept, slice(0, half))):
+            own, border = dot(ordered[rows], grad[:, now]), dot(ordered_border[rows], border_grads[part - 1, :, now])
+            out[:, now] = (own + border).astype(BF16)
 
 
 def project(part, *ins):
     half = jax.ShapeDtypeStruct((D // 2, D), BF16)
     body = functools.partial(project_border_body, part) if part else project_body
     specs = [HELD] * min(len(ins), 4) + [AFTER] * (len(ins) - 4)
-    return call(body, [half] * 2, ins, specs, [HELD] * 2, [], D * D * (ROWS + 2 * WIN), room=20)
+    return call(body, [half] * 2, ins, specs, [HELD] * 2, [], D * D * (ROWS + 2 * WIN), steps=1, room=20)
 
 
 def back_body(grad_query, grad_key, grad_value, w_query, w_key, w_value, *rest):

time: 89 us -> 87.7 us (0.985)
  Pallas kernels: 41.7 us -> 40 us
    pallas_call x9, Pallas kernels: 41.7 us -> 40 us  [call(): pl.pallas_call(body, out_shape=outs, grid=(steps,), in_specs=in_specs, ou...]
  transfers between devices with their start and end apart: 17 -> 17, of which waited for: 6 -> 7; matrix products, arithmetic and copies ran while one was open for 4% -> 4% of each run, Pallas kernels for 30% -> 30%
where the time goes in v7:
time: 87.7 us; the launch traced here: 87.3 us
  Pallas kernels  40 us (46%)
  starting transfers between devices  28.6 us (33%)
  waiting for transfers between devices  11.2 us (13%)
  other arithmetic  4.61 us (5%)
  between operations  1.58 us (2%)
    pallas_call x9, Pallas kernels, call(): pl.pallas_call(body, out_shape=outs, grid=(steps,), in_specs=in_specs, ou...  40 us
    ppermute x12, starting transfers between devices, exchange(): return lax.ppermute(value, AXES, pairs)  13.9 us
    ppermute x2, starting transfers between devices, send(): return lax.ppermute(rows, 'tm', [(i, i ^ 1) for i in range(count)])  7.85 us
    all_to_all x1, waiting for transfers between devices, scatter_sum(): lax.all_to_all(value.reshape(64, -1), AXES, 0, 0, axis_index_groups=last_...  6.44 us
    ppermute x12, waiting for transfers between devices, exchange(): return lax.ppermute(value, AXES, pairs)  4.78 us
    all_to_all x1, starting transfers between devices, scatter_sum(): lax.all_to_all(value.reshape(64, -1), AXES, 0, 0, axis_index_groups=last_...  4.77 us
    ppermute x2, starting transfers between devices, send(): lax.ppermute(rows, 'tm', [(i, i + 1 if i % 2 else i - 1) for i in range(1...  2.05 us
  transfers between devices with their start and end apart: 17, of which 7 were waited for; matrix products, arithmetic and copies ran while one was open for 4% of the time, Pallas kernels for 30%

profile of v7, /device:TPU:0, one launch (start us, length us, event | category | flops | bytes accessed | tf_op | source)
XLA Modules:
  0.0 87.3 jit_solution(14294346351841238688)
XLA Ops:
  0.6 1.1 %select_bitcast_fusion = (bf16[128,1024]{1,0:T(8,128)(2,1)S(1)}, bf16[128,1024]{1,0:T(8,128)(2,1)S(1)}) fusion(pred[]{:T(512)S(6)} %eq.26, bf16[1,512,1024]{2,1,0:T(8,128)(2,1)} %param.7), kind=kLoop, calls=%fused_computation.39 | loop fusion | flops 262144 | bytes 1048577 | tf_op jit(solution)/shard_map/jit(_where)/select_n | solution.py:421
  1.7 0.7 collective-permute-start
  2.4 5.2 %collective-permute-start.1 = (bf16[128,1024]{1,0:T(8,128)(2,1)S(1)}, bf16[128,1024]{1,0:T(8,128)(2,1)S(1)}, u32[]{:S(2)}, u32[]{:S(2)}) collective-permute-start(bf16[128,1024]{1,0:T(8,128)(2,1)S(1)} %get-tuple-element.56), channel_id=1, source_target_pairs={{0,1},{1,0},{2,3},{3,2},{4,5},{5,4},{6,7},{7,6},{8,9},{9,8},{10,11... | collective-permute-start | bytes 786440 | tf_op jit(solution)/shard_map/ppermute | solution.py:427
  8.3 9.7 %shard_map.86 = (bf16[1024,512]{1,0:T(8,128)(2,1)S(1)}, bf16[512,1024]{1,0:T(8,128)(2,1)S(1)}, bf16[512,1024]{1,0:T(8,128)(2,1)S(1)}, bf16[512,1024]{1,0:T(8,128)(2,1)S(1)}, bf16[512,1024]{1,0:T(8,128)(2,1)S(1)}) custom-call(s32[1]{0:T(128)S(6)} %copy.35.length, s32[128]{0:T(128)S(1)} %multiply_xor_fusion.target, bf16[512,1024]{1,0:T(8,128)(2,1)} %bitcast.88, ...), custom_call_target="tpu_custom_call" | custom-call | flops 5368709120 | bytes 15729156 | tf_op jit(solution)/shard_map/pallas_call | solution.py:123
  18.0 0.0 collective-permute-done
  18.0 0.0 collective-permute-done.1
  18.1 13.0 %shard_map.87 = (bf16[512,1024]{1,0:T(8,128)(2,1)S(1)}, bf16[512,1024]{1,0:T(8,128)(2,1)S(1)}, bf16[512,1024]{1,0:T(8,128)(2,1)S(1)}, bf16[2,256,1024]{2,1,0:T(8,128)(2,1)S(1)}, bf16[1024,256]{1,0:T(8,128)(2,1)S(1)}) custom-call(s32[1]{0:T(128)S(6)} %copy.35.length, s32[128]{0:T(128)S(1)} %multiply_xor_fusion.target, ...), custom_call_target="tpu_custom_call" | custom-call | flops 5100273664 | bytes 13632004 | tf_op jit(solution)/shard_map/pallas_call | solution.py:123
  31.0 1.3 %shard_map.88 = (bf16[512,1024]{1,0:T(8,128)(2,1)S(1)}, bf16[512,1024]{1,0:T(8,128)(2,1)S(1)}) custom-call(bf16[1024,512]{1,0:T(8,128)(2,1)S(1)} %get-tuple-element.36.ordered, bf16[512,1024]{1,0:T(8,128)(2,1)S(1)} %get-tuple-element.33.grad.grad_query), custom_call_target="tpu_custom_call" | custom-call | flops 1610612736 | bytes 4194304 | tf_op jit(solution)/shard_map/pallas_call | solution.py:123
  32.3 0.1 collective-permute-start.2
  32.4 1.8 %shard_map.89 = (bf16[512,1024]{1,0:T(8,128)(2,1)S(1)}, bf16[512,1024]{1,0:T(8,128)(2,1)S(1)}) custom-call(bf16[1024,512]{1,0:T(8,128)(2,1)S(1)} %get-tuple-element.36.ordered, bf16[512,1024]{1,0:T(8,128)(2,1)S(1)} %get-tuple-element.34.grad.grad_key, bf16[1024,256]{1,0:T(8,128)(2,1)S(1)} %get-tuple-element.39.ordered_border, ...), custom_call_target="tpu_custom_call" | custom-call | flops 1610612736 | bytes 5767168 | tf_op jit(solution)/shard_map/pallas_call | solution.py:123
  34.2 0.6 collective-permute-start.3
  34.8 0.3 collective-permute-done.2
  35.0 0.2 add_convert_fusion.2
  35.2 1.8 %shard_map.90 = (bf16[512,1024]{1,0:T(8,128)(2,1)S(1)}, bf16[512,1024]{1,0:T(8,128)(2,1)S(1)}) custom-call(bf16[1024,512]{1,0:T(8,128)(2,1)S(1)} %get-tuple-element.36.ordered, bf16[512,1024]{1,0:T(8,128)(2,1)S(1)} %get-tuple-element.35.grad.grad_value, bf16[1024,256]{1,0:T(8,128)(2,1)S(1)} %get-tuple-element.39.ordered_border, ...), custom_call_target="tpu_custom_call" | custom-call | flops 1610612736 | bytes 6291456 | tf_op jit(solution)/shard_map/pallas_call | solution.py:123
  37.0 0.2 collective-permute-start.4
  37.3 4.2 %collective-permute-start.5 = (bf16[2,2,8,8,1024]{4,3,2,1,0:T(8,128)(2,1)S(1)}, bf16[2,2,8,8,1024]{4,3,2,1,0:T(8,128)(2,1)S(1)}, u32[]{:S(2)}, u32[]{:S(2)}) collective-permute-start(bf16[2,2,8,8,1024]{4,3,2,1,0:T(8,128)(2,1)S(1)} %bitcast.91), channel_id=1, source_target_pairs={{0,16},{1,17},{2,18},{3,19},{4,20},{5,21},{6,22},{7,23},{8,24},{9,... | collective-permute-start | bytes 1572872 | tf_op jit(solution)/shard_map/ppermute | solution.py:36
  41.5 0.0 collective-permute-done.3
  41.5 0.2 fusion.rest_1_
  41.7 0.1 collective-permute-start.6
  41.8 0.0 collective-permute-done.4
  41.8 0.2 fusion.1.rest_2_.after
  42.0 2.3 %collective-permute-start.7 = (bf16[2,2,8,8,1024]{4,3,2,1,0:T(8,128)(2,1)S(1)}, bf16[2,2,8,8,1024]{4,3,2,1,0:T(8,128)(2,1)S(1)}, u32[]{:S(2)}, u32[]{:S(2)}) collective-permute-start(bf16[2,2,8,8,1024]{4,3,2,1,0:T(8,128)(2,1)S(1)} %fusion.1.rest_2_.after), channel_id=1, source_target_pairs={{0,1},{1,0},{2,3},{3,2},{4,5},{5,4},{6,7},{7,6},{8,9},{9,8},{10,11... | collective-permute-start | bytes 1572872 | tf_op jit(solution)/shard_map/ppermute | solution.py:36
  44.3 0.1 convert_add_fusion.2
  44.4 5.9 %shard_map.91.refs_3_.d_hidden = f32[512,1024]{1,0:T(8,128)S(1)} custom-call(bf16[512,1024]{1,0:T(8,128)(2,1)S(1)} %get-tuple-element.33.grad.grad_query, bf16[512,1024]{1,0:T(8,128)(2,1)S(1)} %get-tuple-element.34.grad.grad_key, bf16[512,1024]{1,0:T(8,128)(2,1)S(1)} %get-tuple-element.35.grad.grad_value, bf16[1024,1024]{1,0:T(8,128)(2,1)} %w_query.3, ...), custom_call_target="tpu_custom_call" | custom-call | flops 3221225472 | bytes 13107200 | tf_op jit(solution)/shard_map/pallas_call | solution.py:123
  50.3 0.7 collective-permute-done.6.refs_1_
  51.0 0.0 collective-permute-done.5.refs_0_
  51.0 0.5 collective-permute-done.7.refs_2_
  51.5 0.1 fusion.2.rest_2_
  51.6 2.1 %collective-permute-start.10 = (bf16[2,8,8,1024]{3,2,1,0:T(8,128)(2,1)S(1)}, bf16[2,8,8,1024]{3,2,1,0:T(8,128)(2,1)S(1)}, u32[]{:S(2)}, u32[]{:S(2)}) collective-permute-start(bf16[2,8,8,1024]{3,2,1,0:T(8,128)(2,1)S(1)} %fusion.2.rest_2_), channel_id=1, source_target_pairs={{0,16},{1,17},{2,18},{3,19},{4,20},{5,21},{6,22},{7,23},{8,24},{9,... | collective-permute-start | bytes 786440 | tf_op jit(solution)/shard_map/ppermute | solution.py:36
  53.8 0.1 fusion.6.rest_1_
  53.9 2.1 %collective-permute-start.9 = (bf16[2,8,8,1024]{3,2,1,0:T(8,128)(2,1)S(1)}, bf16[2,8,8,1024]{3,2,1,0:T(8,128)(2,1)S(1)}, u32[]{:S(2)}, u32[]{:S(2)}) collective-permute-start(bf16[2,8,8,1024]{3,2,1,0:T(8,128)(2,1)S(1)} %fusion.6.rest_1_), channel_id=1, source_target_pairs={{0,1},{1,0},{2,3},{3,2},{4,5},{5,4},{6,7},{7,6},{8,9},{9,8},{10,11... | collective-permute-start | bytes 786440 | tf_op jit(solution)/shard_map/ppermute | solution.py:36
  56.0 0.1 fusion.3.rest_0_
  56.0 0.1 collective-permute-start.8
  56.1 3.9 %shard_map.93.refs_3_.sides = bf16[256,1024]{1,0:T(8,128)(2,1)S(1)} custom-call(bf16[2,256,1024]{2,1,0:T(8,128)(2,1)S(1)} %get-tuple-element.40.border_grads.grads, bf16[1024,1024]{1,0:T(8,128)(2,1)} %w_key.7, bf16[1024,1024]{1,0:T(8,128)(2,1)} %w_value.7, bf16[2,8,8,1024]{3,2,1,0:T(8,128)(2,1)S(1)} %fusion.3.rest_0_, ...), custom_call_target="tpu_custom_call" | custom-call | flops 1073741824 | bytes 6553600 | tf_op jit(solution)/shard_map/pallas_call | solution.py:123
  60.1 0.0 collective-permute-done.10.refs_2_
  60.1 0.3 collective-permute-done.9.refs_1_
  60.3 2.1 %collective-permute-done.8.refs_0_ = bf16[2,8,8,1024]{3,2,1,0:T(8,128)(2,1)S(1)} collective-permute-done((bf16[2,8,8,1024]{3,2,1,0:T(8,128)(2,1)S(1)}, bf16[2,8,8,1024]{3,2,1,0:T(8,128)(2,1)S(1)}, u32[]{:S(2)}, u32[]{:S(2)}) %collective-permute-start.8) | collective-permute-done | bytes 262176 | tf_op jit(solution)/shard_map/ppermute | solution.py:36
  62.5 0.1 fusion.13.rest_2_
  62.6 0.1 fusion.14.rest_1_
  62.6 0.1 collective-permute-start.15
  62.7 2.0 %collective-permute-start.14 = (bf16[8,8,1024]{2,1,0:T(8,128)(2,1)S(1)}, bf16[8,8,1024]{2,1,0:T(8,128)(2,1)S(1)}, u32[]{:S(2)}, u32[]{:S(2)}) collective-permute-start(bf16[8,8,1024]{2,1,0:T(8,128)(2,1)S(1)} %fusion.14.rest_1_), channel_id=1, source_target_pairs={{0,16},{1,17},{2,18},{3,19},{4,20},{5,21},{6,22},{7,23},{8,24},{9,... | collective-permute-start | bytes 393224 | tf_op jit(solution)/shard_map/ppermute | solution.py:36
  64.7 0.1 fusion.15.rest_0_
  64.8 0.1 collective-permute-start.13
  64.9 0.1 shard_map.95
  64.9 1.4 %collective-permute-start.11 = (bf16[128,1024]{1,0:T(8,128)(2,1)S(1)}, bf16[128,1024]{1,0:T(8,128)(2,1)}, u32[]{:S(2)}, u32[]{:S(2)}) collective-permute-start(bf16[128,1024]{1,0:T(8,128)(2,1)S(1)} %get-tuple-element.51), channel_id=1, source_target_pairs={{1,2},{2,1},{3,4},{4,3},{5,6},{6,5},{7,8},{8,7},{9,10},{10,9},{11,... | collective-permute-start | bytes 786440 | tf_op jit(solution)/shard_map/ppermute | solution.py:428
  66.3 2.6 %collective-permute-start.12 = (bf16[128,1024]{1,0:T(8,128)(2,1)S(1)}, bf16[128,1024]{1,0:T(8,128)(2,1)}, u32[]{:S(2)}, u32[]{:S(2)}) collective-permute-start(bf16[128,1024]{1,0:T(8,128)(2,1)S(1)} %get-tuple-element.52.refs_3_), channel_id=1, source_target_pairs={{0,1},{1,0},{2,3},{3,2},{4,5},{5,4},{6,7},{7,6},{8,9},{9,8},{10,11... | collective-permute-start | bytes 786440 | tf_op jit(solution)/shard_map/ppermute | solution.py:427
  68.9 0.0 collective-permute-done.15.refs_2_
  68.9 0.0 collective-permute-done.14.refs_1_
  68.9 0.9 %collective-permute-done.13.refs_0_ = bf16[8,8,1024]{2,1,0:T(8,128)(2,1)S(1)} collective-permute-done((bf16[8,8,1024]{2,1,0:T(8,128)(2,1)S(1)}, bf16[8,8,1024]{2,1,0:T(8,128)(2,1)S(1)}, u32[]{:S(2)}, u32[]{:S(2)}) %collective-permute-start.13) | collective-permute-done | bytes 131104 | tf_op jit(solution)/shard_map/ppermute | solution.py:36
  69.8 0.2 fusion.8
  70.0 0.1 fusion.12
  70.1 0.8 pad_maximum_fusion.1
  70.9 4.8 %all-to-all-start = ((bf16[8,8,3072]{2,1,0:T(8,128)(2,1)}), bf16[8,8,3072]{2,1,0:T(8,128)(2,1)S(1)}, u32[]{:S(2)}, u32[]{:S(2)}) async-start(bf16[8,8,3072]{2,1,0:T(8,128)(2,1)} %pad_maximum_fusion.1), calls=%async_computation | async-start | bytes 786432 | tf_op jit(solution)/shard_map/all_to_all | solution.py:97
  75.7 0.0 copy-start
  75.7 0.0 copy-start.1
  75.7 0.0 collective-permute-done.11
  75.7 0.0 collective-permute-done.12
  75.7 1.2 %broadcast_select_fusion.1 = (bf16[128,1024]{1,0:T(8,128)(2,1)S(1)}, bf16[128,1024]{1,0:T(8,128)(2,1)S(1)}) fusion(bf16[128,1024]{1,0:T(8,128)(2,1)} %collective-permute-done.11, bf16[128,1024]{1,0:T(8,128)(2,1)} %collective-permute-done.12, pred[]{:T(512)S(6)} %eq.26), kind=kLoop, calls=%fused_computation.42 | loop fusion | flops 262144 | bytes 1048577 | tf_op jit(solution)/shard_map/jit(_where)/select_n | solution.py:453
  77.0 0.1 copy-done
  77.1 0.3 copy-done.1
  77.4 2.6 %shard_map.96 = bf16[512,1024]{1,0:T(8,128)(2,1)} custom-call(bf16[512,1024]{1,0:T(8,128)(2,1)S(1)} %bitcast.89, bf16[512,1024]{1,0:T(8,128)(2,1)S(1)} %bitcast.100, f32[512,1024]{1,0:T(8,128)S(1)} %shard_map.91.refs_3_.d_hidden, bf16[256,1024]{1,0:T(8,128)(2,1)S(1)} %pad_maximum_fusion.near, bf16[2,2,8,8,1024]{4,3,2,1,0:T(8,128)(2,1)S(1)} %fusion.1.rest_2_.after), custom_call_target="tpu_custom_call" | custom-call | flops 16777216 | bytes 6291456 | tf_op jit(solution)/shard_map/pallas_call | solution.py:123
  80.0 6.4 %all-to-all-done = bf16[8,8,3072]{2,1,0:T(8,128)(2,1)S(1)} async-done(((bf16[8,8,3072]{2,1,0:T(8,128)(2,1)}), bf16[8,8,3072]{2,1,0:T(8,128)(2,1)S(1)}, u32[]{:S(2)}, u32[]{:S(2)}) %all-to-all-start) | async-done | bytes 393248 | tf_op jit(solution)/shard_map/all_to_all | solution.py:97
  86.5 0.8 fusion.4
  (9 shorter events, 0.2 us)
Async XLA Ops:
  1.7 16.3 %collective-permute-start = (bf16[128,1024]{1,0:T(8,128)(2,1)S(1)}, bf16[128,1024]{1,0:T(8,128)(2,1)S(1)}, u32[]{:S(2)}, u32[]{:S(2)}) collective-permute-start(bf16[128,1024]{1,0:T(8,128)(2,1)S(1)} %get-tuple-element.57), channel_id=1, source_target_pairs={{1,2},{2,1},{3,4},{4,3},{5,6},{6,5},{7,8},{8,7},{9,10},{10,9},{11,... | collective-permute-start | bytes 786440 | tf_op jit(solution)/shard_map/ppermute | solution.py:428
  2.4 15.6 %collective-permute-start.1 = (bf16[128,1024]{1,0:T(8,128)(2,1)S(1)}, bf16[128,1024]{1,0:T(8,128)(2,1)S(1)}, u32[]{:S(2)}, u32[]{:S(2)}) collective-permute-start(bf16[128,1024]{1,0:T(8,128)(2,1)S(1)} %get-tuple-element.56), channel_id=1, source_target_pairs={{0,1},{1,0},{2,3},{3,2},{4,5},{5,4},{6,7},{7,6},{8,9},{9,8},{10,11... | collective-permute-start | bytes 786440 | tf_op jit(solution)/shard_map/ppermute | solution.py:427
  32.3 2.7 %collective-permute-start.2 = (bf16[512,1024]{1,0:T(8,128)(2,1)S(1)}, bf16[512,1024]{1,0:T(8,128)(2,1)S(1)}, u32[]{:S(2)}, u32[]{:S(2)}) collective-permute-start(bf16[512,1024]{1,0:T(8,128)(2,1)S(1)} %get-tuple-element.38), channel_id=1, source_target_pairs={{0,32},{1,33},{2,34},{3,35},{4,36},{5,37},{6,38},{7,39},{8,40},{9,... | collective-permute-start | bytes 3145736 | tf_op jit(solution)/shard_map/ppermute | solution.py:36
  34.2 7.3 %collective-permute-start.3 = (bf16[512,1024]{1,0:T(8,128)(2,1)S(1)}, bf16[512,1024]{1,0:T(8,128)(2,1)S(1)}, u32[]{:S(2)}, u32[]{:S(2)}) collective-permute-start(bf16[512,1024]{1,0:T(8,128)(2,1)S(1)} %get-tuple-element.42), channel_id=1, source_target_pairs={{0,32},{1,33},{2,34},{3,35},{4,36},{5,37},{6,38},{7,39},{8,40},{9,... | collective-permute-start | bytes 3145736 | tf_op jit(solution)/shard_map/ppermute | solution.py:36
  37.0 4.8 %collective-permute-start.4 = (bf16[512,1024]{1,0:T(8,128)(2,1)S(1)}, bf16[512,1024]{1,0:T(8,128)(2,1)S(1)}, u32[]{:S(2)}, u32[]{:S(2)}) collective-permute-start(bf16[512,1024]{1,0:T(8,128)(2,1)S(1)} %get-tuple-element.44), channel_id=1, source_target_pairs={{0,32},{1,33},{2,34},{3,35},{4,36},{5,37},{6,38},{7,39},{8,40},{9,... | collective-permute-start | bytes 3145736 | tf_op jit(solution)/shard_map/ppermute | solution.py:36
  37.3 13.7 %collective-permute-start.5 = (bf16[2,2,8,8,1024]{4,3,2,1,0:T(8,128)(2,1)S(1)}, bf16[2,2,8,8,1024]{4,3,2,1,0:T(8,128)(2,1)S(1)}, u32[]{:S(2)}, u32[]{:S(2)}) collective-permute-start(bf16[2,2,8,8,1024]{4,3,2,1,0:T(8,128)(2,1)S(1)} %bitcast.91), channel_id=1, source_target_pairs={{0,16},{1,17},{2,18},{3,19},{4,20},{5,21},{6,22},{7,23},{8,24},{9,... | collective-permute-start | bytes 1572872 | tf_op jit(solution)/shard_map/ppermute | solution.py:36
  41.7 9.3 %collective-permute-start.6 = (bf16[2,2,8,8,1024]{4,3,2,1,0:T(8,128)(2,1)S(1)}, bf16[2,2,8,8,1024]{4,3,2,1,0:T(8,128)(2,1)S(1)}, u32[]{:S(2)}, u32[]{:S(2)}) collective-permute-start(bf16[2,2,8,8,1024]{4,3,2,1,0:T(8,128)(2,1)S(1)} %fusion.rest_1_), channel_id=1, source_target_pairs={{0,4},{1,5},{2,6},{3,7},{4,0},{5,1},{6,2},{7,3},{8,12},{9,13},{10,... | collective-permute-start | bytes 1572872 | tf_op jit(solution)/shard_map/ppermute | solution.py:36
  42.0 9.4 %collective-permute-start.7 = (bf16[2,2,8,8,1024]{4,3,2,1,0:T(8,128)(2,1)S(1)}, bf16[2,2,8,8,1024]{4,3,2,1,0:T(8,128)(2,1)S(1)}, u32[]{:S(2)}, u32[]{:S(2)}) collective-permute-start(bf16[2,2,8,8,1024]{4,3,2,1,0:T(8,128)(2,1)S(1)} %fusion.1.rest_2_.after), channel_id=1, source_target_pairs={{0,1},{1,0},{2,3},{3,2},{4,5},{5,4},{6,7},{7,6},{8,9},{9,8},{10,11... | collective-permute-start | bytes 1572872 | tf_op jit(solution)/shard_map/ppermute | solution.py:36
  51.6 8.5 %collective-permute-start.10 = (bf16[2,8,8,1024]{3,2,1,0:T(8,128)(2,1)S(1)}, bf16[2,8,8,1024]{3,2,1,0:T(8,128)(2,1)S(1)}, u32[]{:S(2)}, u32[]{:S(2)}) collective-permute-start(bf16[2,8,8,1024]{3,2,1,0:T(8,128)(2,1)S(1)} %fusion.2.rest_2_), channel_id=1, source_target_pairs={{0,16},{1,17},{2,18},{3,19},{4,20},{5,21},{6,22},{7,23},{8,24},{9,... | collective-permute-start | bytes 786440 | tf_op jit(solution)/shard_map/ppermute | solution.py:36
  53.9 6.5 %collective-permute-start.9 = (bf16[2,8,8,1024]{3,2,1,0:T(8,128)(2,1)S(1)}, bf16[2,8,8,1024]{3,2,1,0:T(8,128)(2,1)S(1)}, u32[]{:S(2)}, u32[]{:S(2)}) collective-permute-start(bf16[2,8,8,1024]{3,2,1,0:T(8,128)(2,1)S(1)} %fusion.6.rest_1_), channel_id=1, source_target_pairs={{0,1},{1,0},{2,3},{3,2},{4,5},{5,4},{6,7},{7,6},{8,9},{9,8},{10,11... | collective-permute-start | bytes 786440 | tf_op jit(solution)/shard_map/ppermute | solution.py:36
  56.0 6.5 %collective-permute-start.8 = (bf16[2,8,8,1024]{3,2,1,0:T(8,128)(2,1)S(1)}, bf16[2,8,8,1024]{3,2,1,0:T(8,128)(2,1)S(1)}, u32[]{:S(2)}, u32[]{:S(2)}) collective-permute-start(bf16[2,8,8,1024]{3,2,1,0:T(8,128)(2,1)S(1)} %fusion.3.rest_0_), channel_id=1, source_target_pairs={{0,4},{1,5},{2,6},{3,7},{4,0},{5,1},{6,2},{7,3},{8,12},{9,13},{10,... | collective-permute-start | bytes 786440 | tf_op jit(solution)/shard_map/ppermute | solution.py:36
  62.6 6.3 %collective-permute-start.15 = (bf16[8,8,1024]{2,1,0:T(8,128)(2,1)S(1)}, bf16[8,8,1024]{2,1,0:T(8,128)(2,1)S(1)}, u32[]{:S(2)}, u32[]{:S(2)}) collective-permute-start(bf16[8,8,1024]{2,1,0:T(8,128)(2,1)S(1)} %fusion.13.rest_2_), channel_id=1, source_target_pairs={{0,4},{1,5},{2,6},{3,7},{4,0},{5,1},{6,2},{7,3},{8,12},{9,13},{10,... | collective-permute-start | bytes 393224 | tf_op jit(solution)/shard_map/ppermute | solution.py:36
  62.7 6.2 %collective-permute-start.14 = (bf16[8,8,1024]{2,1,0:T(8,128)(2,1)S(1)}, bf16[8,8,1024]{2,1,0:T(8,128)(2,1)S(1)}, u32[]{:S(2)}, u32[]{:S(2)}) collective-permute-start(bf16[8,8,1024]{2,1,0:T(8,128)(2,1)S(1)} %fusion.14.rest_1_), channel_id=1, source_target_pairs={{0,16},{1,17},{2,18},{3,19},{4,20},{5,21},{6,22},{7,23},{8,24},{9,... | collective-permute-start | bytes 393224 | tf_op jit(solution)/shard_map/ppermute | solution.py:36
  64.8 5.0 %collective-permute-start.13 = (bf16[8,8,1024]{2,1,0:T(8,128)(2,1)S(1)}, bf16[8,8,1024]{2,1,0:T(8,128)(2,1)S(1)}, u32[]{:S(2)}, u32[]{:S(2)}) collective-permute-start(bf16[8,8,1024]{2,1,0:T(8,128)(2,1)S(1)} %fusion.15.rest_0_), channel_id=1, source_target_pairs={{0,1},{1,0},{2,3},{3,2},{4,5},{5,4},{6,7},{7,6},{8,9},{9,8},{10,11... | collective-permute-start | bytes 393224 | tf_op jit(solution)/shard_map/ppermute | solution.py:36
  64.9 10.8 %collective-permute-start.11 = (bf16[128,1024]{1,0:T(8,128)(2,1)S(1)}, bf16[128,1024]{1,0:T(8,128)(2,1)}, u32[]{:S(2)}, u32[]{:S(2)}) collective-permute-start(bf16[128,1024]{1,0:T(8,128)(2,1)S(1)} %get-tuple-element.51), channel_id=1, source_target_pairs={{1,2},{2,1},{3,4},{4,3},{5,6},{6,5},{7,8},{8,7},{9,10},{10,9},{11,... | collective-permute-start | bytes 786440 | tf_op jit(solution)/shard_map/ppermute | solution.py:428
  66.3 9.4 %collective-permute-start.12 = (bf16[128,1024]{1,0:T(8,128)(2,1)S(1)}, bf16[128,1024]{1,0:T(8,128)(2,1)}, u32[]{:S(2)}, u32[]{:S(2)}) collective-permute-start(bf16[128,1024]{1,0:T(8,128)(2,1)S(1)} %get-tuple-element.52.refs_3_), channel_id=1, source_target_pairs={{0,1},{1,0},{2,3},{3,2},{4,5},{5,4},{6,7},{7,6},{8,9},{9,8},{10,11... | collective-permute-start | bytes 786440 | tf_op jit(solution)/shard_map/ppermute | solution.py:427
  70.9 15.6 %all-to-all-start = ((bf16[8,8,3072]{2,1,0:T(8,128)(2,1)}), bf16[8,8,3072]{2,1,0:T(8,128)(2,1)S(1)}, u32[]{:S(2)}, u32[]{:S(2)}) async-start(bf16[8,8,3072]{2,1,0:T(8,128)(2,1)} %pad_maximum_fusion.1), calls=%async_computation | async-start | bytes 786432 | tf_op jit(solution)/shard_map/all_to_all | solution.py:97
  75.7 1.4 %copy-start = (bf16[1,512,1024]{2,1,0:T(8,128)(2,1)S(1)}, bf16[1,512,1024]{2,1,0:T(8,128)(2,1)}, u32[]{:S(2)}) copy-start(bf16[1,512,1024]{2,1,0:T(8,128)(2,1)} %param.7) | copy-start | bytes 3145732
  75.7 1.7 %copy-start.1 = (bf16[1,512,1024]{2,1,0:T(8,128)(2,1)S(1)}, bf16[1,512,1024]{2,1,0:T(8,128)(2,1)}, u32[]{:S(2)}) copy-start(bf16[1,512,1024]{2,1,0:T(8,128)(2,1)} %param.8) | copy-start | bytes 3145732

commit v8 on v7

--- a/solution.py
+++ b/solution.py
@@ -297,13 +297,21 @@
     for i in range(blocks):
         soften(0, i, first[i])
         second.append(products(1, i))
-    jobs = [(query_grads, 0), (query_grads, 1), (key_grads, 0), (key_grads, 1), (key_grads, 2)]
+        if i == 1:
+            query_grads(0, 0)
+            key_grads(0, 0)
     for i in range(blocks):
         soften(1, i, second[i])
-        for job, part in jobs[i : i + 1] if i < 3 else jobs[3:]:
-            job(0, part)
-    for job, part in jobs:
-        job(1, part)
+        if i == 0:
+            query_grads(0, 1)
+            key_grads(0, 1)
+        if i == 1:
+            key_grads(0, 2)
+            query_grads(1, 0)
+            key_grads(1, 0)
+    query_grads(1, 1)
+    key_grads(1, 1)
+    key_grads(1, 2)
 
 
 def attend(length, target, low, high, query, keys, values, d_mixed, w_key, w_value):

time: 87.7 us -> 87.6 us (level)
  no operation moved by 1% of the time
where the time goes in v8:
time: 87.6 us; the launch traced here: 87.2 us
  Pallas kernels  39.9 us (46%)
  starting transfers between devices  28.6 us (33%)
  waiting for transfers between devices  11.2 us (13%)
  other arithmetic  4.61 us (5%)
  between operations  1.58 us (2%)
    pallas_call x9, Pallas kernels, call(): pl.pallas_call(body, out_shape=outs, grid=(steps,), in_specs=in_specs, ou...  39.9 us
    ppermute x12, starting transfers between devices, exchange(): return lax.ppermute(value, AXES, pairs)  13.9 us
    ppermute x2, starting transfers between devices, send(): return lax.ppermute(rows, 'tm', [(i, i ^ 1) for i in range(count)])  7.85 us
    all_to_all x1, waiting for transfers between devices, scatter_sum(): lax.all_to_all(value.reshape(64, -1), AXES, 0, 0, axis_index_groups=last_...  6.44 us
    ppermute x12, waiting for transfers between devices, exchange(): return lax.ppermute(value, AXES, pairs)  4.77 us
    all_to_all x1, starting transfers between devices, scatter_sum(): lax.all_to_all(value.reshape(64, -1), AXES, 0, 0, axis_index_groups=last_...  4.77 us
    ppermute x2, starting transfers between devices, send(): lax.ppermute(rows, 'tm', [(i, i + 1 if i % 2 else i - 1) for i in range(1...  2.05 us
  transfers between devices with their start and end apart: 17, of which 7 were waited for; matrix products, arithmetic and copies ran while one was open for 4% of the time, Pallas kernels for 30%

profile of v8, /device:TPU:0, one launch (start us, length us, event | category | flops | bytes accessed | tf_op | source)
XLA Modules:
  0.0 87.2 jit_solution(149353928293356964)
XLA Ops:
  0.6 1.1 %select_bitcast_fusion = (bf16[128,1024]{1,0:T(8,128)(2,1)S(1)}, bf16[128,1024]{1,0:T(8,128)(2,1)S(1)}) fusion(pred[]{:T(512)S(6)} %eq.26, bf16[1,512,1024]{2,1,0:T(8,128)(2,1)} %param.7), kind=kLoop, calls=%fused_computation.39 | loop fusion | flops 262144 | bytes 1048577 | tf_op jit(solution)/shard_map/jit(_where)/select_n | solution.py:429
  1.7 0.7 collective-permute-start
  2.4 5.2 %collective-permute-start.1 = (bf16[128,1024]{1,0:T(8,128)(2,1)S(1)}, bf16[128,1024]{1,0:T(8,128)(2,1)S(1)}, u32[]{:S(2)}, u32[]{:S(2)}) collective-permute-start(bf16[128,1024]{1,0:T(8,128)(2,1)S(1)} %get-tuple-element.56), channel_id=1, source_target_pairs={{0,1},{1,0},{2,3},{3,2},{4,5},{5,4},{6,7},{7,6},{8,9},{9,8},{10,11... | collective-permute-start | bytes 786440 | tf_op jit(solution)/shard_map/ppermute | solution.py:435
  8.3 9.7 %shard_map.86 = (bf16[1024,512]{1,0:T(8,128)(2,1)S(1)}, bf16[512,1024]{1,0:T(8,128)(2,1)S(1)}, bf16[512,1024]{1,0:T(8,128)(2,1)S(1)}, bf16[512,1024]{1,0:T(8,128)(2,1)S(1)}, bf16[512,1024]{1,0:T(8,128)(2,1)S(1)}) custom-call(s32[1]{0:T(128)S(6)} %copy.35.length, s32[128]{0:T(128)S(1)} %multiply_xor_fusion.target, bf16[512,1024]{1,0:T(8,128)(2,1)} %bitcast.88, ...), custom_call_target="tpu_custom_call" | custom-call | flops 5368709120 | bytes 15729156 | tf_op jit(solution)/shard_map/pallas_call | solution.py:123
  18.0 0.0 collective-permute-done
  18.0 0.0 collective-permute-done.1
  18.1 12.9 %shard_map.87 = (bf16[512,1024]{1,0:T(8,128)(2,1)S(1)}, bf16[512,1024]{1,0:T(8,128)(2,1)S(1)}, bf16[512,1024]{1,0:T(8,128)(2,1)S(1)}, bf16[2,256,1024]{2,1,0:T(8,128)(2,1)S(1)}, bf16[1024,256]{1,0:T(8,128)(2,1)S(1)}) custom-call(s32[1]{0:T(128)S(6)} %copy.35.length, s32[128]{0:T(128)S(1)} %multiply_xor_fusion.target, ...), custom_call_target="tpu_custom_call" | custom-call | flops 5100273664 | bytes 13632004 | tf_op jit(solution)/shard_map/pallas_call | solution.py:123
  30.9 1.3 %shard_map.88 = (bf16[512,1024]{1,0:T(8,128)(2,1)S(1)}, bf16[512,1024]{1,0:T(8,128)(2,1)S(1)}) custom-call(bf16[1024,512]{1,0:T(8,128)(2,1)S(1)} %get-tuple-element.36.ordered, bf16[512,1024]{1,0:T(8,128)(2,1)S(1)} %get-tuple-element.33.grad.grad_query), custom_call_target="tpu_custom_call" | custom-call | flops 1610612736 | bytes 4194304 | tf_op jit(solution)/shard_map/pallas_call | solution.py:123
  32.2 0.1 collective-permute-start.2
  32.3 1.8 %shard_map.89 = (bf16[512,1024]{1,0:T(8,128)(2,1)S(1)}, bf16[512,1024]{1,0:T(8,128)(2,1)S(1)}) custom-call(bf16[1024,512]{1,0:T(8,128)(2,1)S(1)} %get-tuple-element.36.ordered, bf16[512,1024]{1,0:T(8,128)(2,1)S(1)} %get-tuple-element.34.grad.grad_key, bf16[1024,256]{1,0:T(8,128)(2,1)S(1)} %get-tuple-element.39.ordered_border, ...), custom_call_target="tpu_custom_call" | custom-call | flops 1610612736 | bytes 5767168 | tf_op jit(solution)/shard_map/pallas_call | solution.py:123
  34.1 0.6 collective-permute-start.3
  34.7 0.3 collective-permute-done.2
  34.9 0.2 add_convert_fusion.2
  35.1 1.8 %shard_map.90 = (bf16[512,1024]{1,0:T(8,128)(2,1)S(1)}, bf16[512,1024]{1,0:T(8,128)(2,1)S(1)}) custom-call(bf16[1024,512]{1,0:T(8,128)(2,1)S(1)} %get-tuple-element.36.ordered, bf16[512,1024]{1,0:T(8,128)(2,1)S(1)} %get-tuple-element.35.grad.grad_value, bf16[1024,256]{1,0:T(8,128)(2,1)S(1)} %get-tuple-element.39.ordered_border, ...), custom_call_target="tpu_custom_call" | custom-call | flops 1610612736 | bytes 6291456 | tf_op jit(solution)/shard_map/pallas_call | solution.py:123
  36.9 0.2 collective-permute-start.4
  37.2 4.2 %collective-permute-start.5 = (bf16[2,2,8,8,1024]{4,3,2,1,0:T(8,128)(2,1)S(1)}, bf16[2,2,8,8,1024]{4,3,2,1,0:T(8,128)(2,1)S(1)}, u32[]{:S(2)}, u32[]{:S(2)}) collective-permute-start(bf16[2,2,8,8,1024]{4,3,2,1,0:T(8,128)(2,1)S(1)} %bitcast.91), channel_id=1, source_target_pairs={{0,16},{1,17},{2,18},{3,19},{4,20},{5,21},{6,22},{7,23},{8,24},{9,... | collective-permute-start | bytes 1572872 | tf_op jit(solution)/shard_map/ppermute | solution.py:36
  41.4 0.0 collective-permute-done.3
  41.4 0.2 fusion.rest_1_
  41.6 0.1 collective-permute-start.6
  41.8 0.0 collective-permute-done.4
  41.8 0.2 fusion.1.rest_2_.after
  42.0 2.3 %collective-permute-start.7 = (bf16[2,2,8,8,1024]{4,3,2,1,0:T(8,128)(2,1)S(1)}, bf16[2,2,8,8,1024]{4,3,2,1,0:T(8,128)(2,1)S(1)}, u32[]{:S(2)}, u32[]{:S(2)}) collective-permute-start(bf16[2,2,8,8,1024]{4,3,2,1,0:T(8,128)(2,1)S(1)} %fusion.1.rest_2_.after), channel_id=1, source_target_pairs={{0,1},{1,0},{2,3},{3,2},{4,5},{5,4},{6,7},{7,6},{8,9},{9,8},{10,11... | collective-permute-start | bytes 1572872 | tf_op jit(solution)/shard_map/ppermute | solution.py:36
  44.2 0.1 convert_add_fusion.2
  44.3 5.9 %shard_map.91.refs_3_.d_hidden = f32[512,1024]{1,0:T(8,128)S(1)} custom-call(bf16[512,1024]{1,0:T(8,128)(2,1)S(1)} %get-tuple-element.33.grad.grad_query, bf16[512,1024]{1,0:T(8,128)(2,1)S(1)} %get-tuple-element.34.grad.grad_key, bf16[512,1024]{1,0:T(8,128)(2,1)S(1)} %get-tuple-element.35.grad.grad_value, bf16[1024,1024]{1,0:T(8,128)(2,1)} %w_query.3, ...), custom_call_target="tpu_custom_call" | custom-call | flops 3221225472 | bytes 13107200 | tf_op jit(solution)/shard_map/pallas_call | solution.py:123
  50.2 0.7 collective-permute-done.6.refs_1_
  50.9 0.0 collective-permute-done.5.refs_0_
  50.9 0.5 collective-permute-done.7.refs_2_
  51.4 0.1 fusion.2.rest_2_
  51.5 2.1 %collective-permute-start.10 = (bf16[2,8,8,1024]{3,2,1,0:T(8,128)(2,1)S(1)}, bf16[2,8,8,1024]{3,2,1,0:T(8,128)(2,1)S(1)}, u32[]{:S(2)}, u32[]{:S(2)}) collective-permute-start(bf16[2,8,8,1024]{3,2,1,0:T(8,128)(2,1)S(1)} %fusion.2.rest_2_), channel_id=1, source_target_pairs={{0,16},{1,17},{2,18},{3,19},{4,20},{5,21},{6,22},{7,23},{8,24},{9,... | collective-permute-start | bytes 786440 | tf_op jit(solution)/shard_map/ppermute | solution.py:36
  53.7 0.1 fusion.6.rest_1_
  53.8 2.1 %collective-permute-start.9 = (bf16[2,8,8,1024]{3,2,1,0:T(8,128)(2,1)S(1)}, bf16[2,8,8,1024]{3,2,1,0:T(8,128)(2,1)S(1)}, u32[]{:S(2)}, u32[]{:S(2)}) collective-permute-start(bf16[2,8,8,1024]{3,2,1,0:T(8,128)(2,1)S(1)} %fusion.6.rest_1_), channel_id=1, source_target_pairs={{0,1},{1,0},{2,3},{3,2},{4,5},{5,4},{6,7},{7,6},{8,9},{9,8},{10,11... | collective-permute-start | bytes 786440 | tf_op jit(solution)/shard_map/ppermute | solution.py:36
  55.9 0.1 fusion.3.rest_0_
  55.9 0.1 collective-permute-start.8
  56.0 3.9 %shard_map.93.refs_3_.sides = bf16[256,1024]{1,0:T(8,128)(2,1)S(1)} custom-call(bf16[2,256,1024]{2,1,0:T(8,128)(2,1)S(1)} %get-tuple-element.40.border_grads.grads, bf16[1024,1024]{1,0:T(8,128)(2,1)} %w_key.7, bf16[1024,1024]{1,0:T(8,128)(2,1)} %w_value.7, bf16[2,8,8,1024]{3,2,1,0:T(8,128)(2,1)S(1)} %fusion.3.rest_0_, ...), custom_call_target="tpu_custom_call" | custom-call | flops 1073741824 | bytes 6553600 | tf_op jit(solution)/shard_map/pallas_call | solution.py:123
  60.0 0.0 collective-permute-done.10.refs_2_
  60.0 0.3 collective-permute-done.9.refs_1_
  60.3 2.1 %collective-permute-done.8.refs_0_ = bf16[2,8,8,1024]{3,2,1,0:T(8,128)(2,1)S(1)} collective-permute-done((bf16[2,8,8,1024]{3,2,1,0:T(8,128)(2,1)S(1)}, bf16[2,8,8,1024]{3,2,1,0:T(8,128)(2,1)S(1)}, u32[]{:S(2)}, u32[]{:S(2)}) %collective-permute-start.8) | collective-permute-done | bytes 262176 | tf_op jit(solution)/shard_map/ppermute | solution.py:36
  62.4 0.1 fusion.13.rest_2_
  62.5 0.1 fusion.14.rest_1_
  62.6 0.1 collective-permute-start.15
  62.6 2.0 %collective-permute-start.14 = (bf16[8,8,1024]{2,1,0:T(8,128)(2,1)S(1)}, bf16[8,8,1024]{2,1,0:T(8,128)(2,1)S(1)}, u32[]{:S(2)}, u32[]{:S(2)}) collective-permute-start(bf16[8,8,1024]{2,1,0:T(8,128)(2,1)S(1)} %fusion.14.rest_1_), channel_id=1, source_target_pairs={{0,16},{1,17},{2,18},{3,19},{4,20},{5,21},{6,22},{7,23},{8,24},{9,... | collective-permute-start | bytes 393224 | tf_op jit(solution)/shard_map/ppermute | solution.py:36
  64.6 0.1 fusion.15.rest_0_
  64.7 0.1 collective-permute-start.13
  64.8 0.1 shard_map.95
  64.9 1.4 %collective-permute-start.11 = (bf16[128,1024]{1,0:T(8,128)(2,1)S(1)}, bf16[128,1024]{1,0:T(8,128)(2,1)}, u32[]{:S(2)}, u32[]{:S(2)}) collective-permute-start(bf16[128,1024]{1,0:T(8,128)(2,1)S(1)} %get-tuple-element.51), channel_id=1, source_target_pairs={{1,2},{2,1},{3,4},{4,3},{5,6},{6,5},{7,8},{8,7},{9,10},{10,9},{11,... | collective-permute-start | bytes 786440 | tf_op jit(solution)/shard_map/ppermute | solution.py:436
  66.2 2.6 %collective-permute-start.12 = (bf16[128,1024]{1,0:T(8,128)(2,1)S(1)}, bf16[128,1024]{1,0:T(8,128)(2,1)}, u32[]{:S(2)}, u32[]{:S(2)}) collective-permute-start(bf16[128,1024]{1,0:T(8,128)(2,1)S(1)} %get-tuple-element.52.refs_3_), channel_id=1, source_target_pairs={{0,1},{1,0},{2,3},{3,2},{4,5},{5,4},{6,7},{7,6},{8,9},{9,8},{10,11... | collective-permute-start | bytes 786440 | tf_op jit(solution)/shard_map/ppermute | solution.py:435
  68.8 0.0 collective-permute-done.15.refs_2_
  68.8 0.0 collective-permute-done.14.refs_1_
  68.8 0.9 %collective-permute-done.13.refs_0_ = bf16[8,8,1024]{2,1,0:T(8,128)(2,1)S(1)} collective-permute-done((bf16[8,8,1024]{2,1,0:T(8,128)(2,1)S(1)}, bf16[8,8,1024]{2,1,0:T(8,128)(2,1)S(1)}, u32[]{:S(2)}, u32[]{:S(2)}) %collective-permute-start.13) | collective-permute-done | bytes 131104 | tf_op jit(solution)/shard_map/ppermute | solution.py:36
  69.7 0.2 fusion.8
  70.0 0.1 fusion.12
  70.1 0.8 pad_maximum_fusion.1
  70.8 4.8 %all-to-all-start = ((bf16[8,8,3072]{2,1,0:T(8,128)(2,1)}), bf16[8,8,3072]{2,1,0:T(8,128)(2,1)S(1)}, u32[]{:S(2)}, u32[]{:S(2)}) async-start(bf16[8,8,3072]{2,1,0:T(8,128)(2,1)} %pad_maximum_fusion.1), calls=%async_computation | async-start | bytes 786432 | tf_op jit(solution)/shard_map/all_to_all | solution.py:97
  75.6 0.0 copy-start
  75.6 0.0 copy-start.1
  75.6 0.0 collective-permute-done.11
  75.6 0.0 collective-permute-done.12
  75.6 1.2 %broadcast_select_fusion.1 = (bf16[128,1024]{1,0:T(8,128)(2,1)S(1)}, bf16[128,1024]{1,0:T(8,128)(2,1)S(1)}) fusion(bf16[128,1024]{1,0:T(8,128)(2,1)} %collective-permute-done.11, bf16[128,1024]{1,0:T(8,128)(2,1)} %collective-permute-done.12, pred[]{:T(512)S(6)} %eq.26), kind=kLoop, calls=%fused_computation.42 | loop fusion | flops 262144 | bytes 1048577 | tf_op jit(solution)/shard_map/jit(_where)/select_n | solution.py:461
  76.9 0.1 copy-done
  77.0 0.3 copy-done.1
  77.3 2.6 %shard_map.96 = bf16[512,1024]{1,0:T(8,128)(2,1)} custom-call(bf16[512,1024]{1,0:T(8,128)(2,1)S(1)} %bitcast.89, bf16[512,1024]{1,0:T(8,128)(2,1)S(1)} %bitcast.100, f32[512,1024]{1,0:T(8,128)S(1)} %shard_map.91.refs_3_.d_hidden, bf16[256,1024]{1,0:T(8,128)(2,1)S(1)} %pad_maximum_fusion.near, bf16[2,2,8,8,1024]{4,3,2,1,0:T(8,128)(2,1)S(1)} %fusion.1.rest_2_.after), custom_call_target="tpu_custom_call" | custom-call | flops 16777216 | bytes 6291456 | tf_op jit(solution)/shard_map/pallas_call | solution.py:123
  80.0 6.4 %all-to-all-done = bf16[8,8,3072]{2,1,0:T(8,128)(2,1)S(1)} async-done(((bf16[8,8,3072]{2,1,0:T(8,128)(2,1)}), bf16[8,8,3072]{2,1,0:T(8,128)(2,1)S(1)}, u32[]{:S(2)}, u32[]{:S(2)}) %all-to-all-start) | async-done | bytes 393248 | tf_op jit(solution)/shard_map/all_to_all | solution.py:97
  86.4 0.8 fusion.4
  (9 shorter events, 0.2 us)
Async XLA Ops:
  1.7 16.3 %collective-permute-start = (bf16[128,1024]{1,0:T(8,128)(2,1)S(1)}, bf16[128,1024]{1,0:T(8,128)(2,1)S(1)}, u32[]{:S(2)}, u32[]{:S(2)}) collective-permute-start(bf16[128,1024]{1,0:T(8,128)(2,1)S(1)} %get-tuple-element.57), channel_id=1, source_target_pairs={{1,2},{2,1},{3,4},{4,3},{5,6},{6,5},{7,8},{8,7},{9,10},{10,9},{11,... | collective-permute-start | bytes 786440 | tf_op jit(solution)/shard_map/ppermute | solution.py:436
  2.4 15.6 %collective-permute-start.1 = (bf16[128,1024]{1,0:T(8,128)(2,1)S(1)}, bf16[128,1024]{1,0:T(8,128)(2,1)S(1)}, u32[]{:S(2)}, u32[]{:S(2)}) collective-permute-start(bf16[128,1024]{1,0:T(8,128)(2,1)S(1)} %get-tuple-element.56), channel_id=1, source_target_pairs={{0,1},{1,0},{2,3},{3,2},{4,5},{5,4},{6,7},{7,6},{8,9},{9,8},{10,11... | collective-permute-start | bytes 786440 | tf_op jit(solution)/shard_map/ppermute | solution.py:435
  32.2 2.7 %collective-permute-start.2 = (bf16[512,1024]{1,0:T(8,128)(2,1)S(1)}, bf16[512,1024]{1,0:T(8,128)(2,1)S(1)}, u32[]{:S(2)}, u32[]{:S(2)}) collective-permute-start(bf16[512,1024]{1,0:T(8,128)(2,1)S(1)} %get-tuple-element.38), channel_id=1, source_target_pairs={{0,32},{1,33},{2,34},{3,35},{4,36},{5,37},{6,38},{7,39},{8,40},{9,... | collective-permute-start | bytes 3145736 | tf_op jit(solution)/shard_map/ppermute | solution.py:36
  34.1 7.3 %collective-permute-start.3 = (bf16[512,1024]{1,0:T(8,128)(2,1)S(1)}, bf16[512,1024]{1,0:T(8,128)(2,1)S(1)}, u32[]{:S(2)}, u32[]{:S(2)}) collective-permute-start(bf16[512,1024]{1,0:T(8,128)(2,1)S(1)} %get-tuple-element.42), channel_id=1, source_target_pairs={{0,32},{1,33},{2,34},{3,35},{4,36},{5,37},{6,38},{7,39},{8,40},{9,... | collective-permute-start | bytes 3145736 | tf_op jit(solution)/shard_map/ppermute | solution.py:36
  36.9 4.8 %collective-permute-start.4 = (bf16[512,1024]{1,0:T(8,128)(2,1)S(1)}, bf16[512,1024]{1,0:T(8,128)(2,1)S(1)}, u32[]{:S(2)}, u32[]{:S(2)}) collective-permute-start(bf16[512,1024]{1,0:T(8,128)(2,1)S(1)} %get-tuple-element.44), channel_id=1, source_target_pairs={{0,32},{1,33},{2,34},{3,35},{4,36},{5,37},{6,38},{7,39},{8,40},{9,... | collective-permute-start | bytes 3145736 | tf_op jit(solution)/shard_map/ppermute | solution.py:36
  37.2 13.7 %collective-permute-start.5 = (bf16[2,2,8,8,1024]{4,3,2,1,0:T(8,128)(2,1)S(1)}, bf16[2,2,8,8,1024]{4,3,2,1,0:T(8,128)(2,1)S(1)}, u32[]{:S(2)}, u32[]{:S(2)}) collective-permute-start(bf16[2,2,8,8,1024]{4,3,2,1,0:T(8,128)(2,1)S(1)} %bitcast.91), channel_id=1, source_target_pairs={{0,16},{1,17},{2,18},{3,19},{4,20},{5,21},{6,22},{7,23},{8,24},{9,... | collective-permute-start | bytes 1572872 | tf_op jit(solution)/shard_map/ppermute | solution.py:36
  41.6 9.3 %collective-permute-start.6 = (bf16[2,2,8,8,1024]{4,3,2,1,0:T(8,128)(2,1)S(1)}, bf16[2,2,8,8,1024]{4,3,2,1,0:T(8,128)(2,1)S(1)}, u32[]{:S(2)}, u32[]{:S(2)}) collective-permute-start(bf16[2,2,8,8,1024]{4,3,2,1,0:T(8,128)(2,1)S(1)} %fusion.rest_1_), channel_id=1, source_target_pairs={{0,4},{1,5},{2,6},{3,7},{4,0},{5,1},{6,2},{7,3},{8,12},{9,13},{10,... | collective-permute-start | bytes 1572872 | tf_op jit(solution)/shard_map/ppermute | solution.py:36
  42.0 9.4 %collective-permute-start.7 = (bf16[2,2,8,8,1024]{4,3,2,1,0:T(8,128)(2,1)S(1)}, bf16[2,2,8,8,1024]{4,3,2,1,0:T(8,128)(2,1)S(1)}, u32[]{:S(2)}, u32[]{:S(2)}) collective-permute-start(bf16[2,2,8,8,1024]{4,3,2,1,0:T(8,128)(2,1)S(1)} %fusion.1.rest_2_.after), channel_id=1, source_target_pairs={{0,1},{1,0},{2,3},{3,2},{4,5},{5,4},{6,7},{7,6},{8,9},{9,8},{10,11... | collective-permute-start | bytes 1572872 | tf_op jit(solution)/shard_map/ppermute | solution.py:36
  51.5 8.5 %collective-permute-start.10 = (bf16[2,8,8,1024]{3,2,1,0:T(8,128)(2,1)S(1)}, bf16[2,8,8,1024]{3,2,1,0:T(8,128)(2,1)S(1)}, u32[]{:S(2)}, u32[]{:S(2)}) collective-permute-start(bf16[2,8,8,1024]{3,2,1,0:T(8,128)(2,1)S(1)} %fusion.2.rest_2_), channel_id=1, source_target_pairs={{0,16},{1,17},{2,18},{3,19},{4,20},{5,21},{6,22},{7,23},{8,24},{9,... | collective-permute-start | bytes 786440 | tf_op jit(solution)/shard_map/ppermute | solution.py:36
  53.8 6.5 %collective-permute-start.9 = (bf16[2,8,8,1024]{3,2,1,0:T(8,128)(2,1)S(1)}, bf16[2,8,8,1024]{3,2,1,0:T(8,128)(2,1)S(1)}, u32[]{:S(2)}, u32[]{:S(2)}) collective-permute-start(bf16[2,8,8,1024]{3,2,1,0:T(8,128)(2,1)S(1)} %fusion.6.rest_1_), channel_id=1, source_target_pairs={{0,1},{1,0},{2,3},{3,2},{4,5},{5,4},{6,7},{7,6},{8,9},{9,8},{10,11... | collective-permute-start | bytes 786440 | tf_op jit(solution)/shard_map/ppermute | solution.py:36
  55.9 6.5 %collective-permute-start.8 = (bf16[2,8,8,1024]{3,2,1,0:T(8,128)(2,1)S(1)}, bf16[2,8,8,1024]{3,2,1,0:T(8,128)(2,1)S(1)}, u32[]{:S(2)}, u32[]{:S(2)}) collective-permute-start(bf16[2,8,8,1024]{3,2,1,0:T(8,128)(2,1)S(1)} %fusion.3.rest_0_), channel_id=1, source_target_pairs={{0,4},{1,5},{2,6},{3,7},{4,0},{5,1},{6,2},{7,3},{8,12},{9,13},{10,... | collective-permute-start | bytes 786440 | tf_op jit(solution)/shard_map/ppermute | solution.py:36
  62.6 6.3 %collective-permute-start.15 = (bf16[8,8,1024]{2,1,0:T(8,128)(2,1)S(1)}, bf16[8,8,1024]{2,1,0:T(8,128)(2,1)S(1)}, u32[]{:S(2)}, u32[]{:S(2)}) collective-permute-start(bf16[8,8,1024]{2,1,0:T(8,128)(2,1)S(1)} %fusion.13.rest_2_), channel_id=1, source_target_pairs={{0,4},{1,5},{2,6},{3,7},{4,0},{5,1},{6,2},{7,3},{8,12},{9,13},{10,... | collective-permute-start | bytes 393224 | tf_op jit(solution)/shard_map/ppermute | solution.py:36
  62.6 6.2 %collective-permute-start.14 = (bf16[8,8,1024]{2,1,0:T(8,128)(2,1)S(1)}, bf16[8,8,1024]{2,1,0:T(8,128)(2,1)S(1)}, u32[]{:S(2)}, u32[]{:S(2)}) collective-permute-start(bf16[8,8,1024]{2,1,0:T(8,128)(2,1)S(1)} %fusion.14.rest_1_), channel_id=1, source_target_pairs={{0,16},{1,17},{2,18},{3,19},{4,20},{5,21},{6,22},{7,23},{8,24},{9,... | collective-permute-start | bytes 393224 | tf_op jit(solution)/shard_map/ppermute | solution.py:36
  64.7 5.0 %collective-permute-start.13 = (bf16[8,8,1024]{2,1,0:T(8,128)(2,1)S(1)}, bf16[8,8,1024]{2,1,0:T(8,128)(2,1)S(1)}, u32[]{:S(2)}, u32[]{:S(2)}) collective-permute-start(bf16[8,8,1024]{2,1,0:T(8,128)(2,1)S(1)} %fusion.15.rest_0_), channel_id=1, source_target_pairs={{0,1},{1,0},{2,3},{3,2},{4,5},{5,4},{6,7},{7,6},{8,9},{9,8},{10,11... | collective-permute-start | bytes 393224 | tf_op jit(solution)/shard_map/ppermute | solution.py:36
  64.9 10.8 %collective-permute-start.11 = (bf16[128,1024]{1,0:T(8,128)(2,1)S(1)}, bf16[128,1024]{1,0:T(8,128)(2,1)}, u32[]{:S(2)}, u32[]{:S(2)}) collective-permute-start(bf16[128,1024]{1,0:T(8,128)(2,1)S(1)} %get-tuple-element.51), channel_id=1, source_target_pairs={{1,2},{2,1},{3,4},{4,3},{5,6},{6,5},{7,8},{8,7},{9,10},{10,9},{11,... | collective-permute-start | bytes 786440 | tf_op jit(solution)/shard_map/ppermute | solution.py:436
  66.2 9.4 %collective-permute-start.12 = (bf16[128,1024]{1,0:T(8,128)(2,1)S(1)}, bf16[128,1024]{1,0:T(8,128)(2,1)}, u32[]{:S(2)}, u32[]{:S(2)}) collective-permute-start(bf16[128,1024]{1,0:T(8,128)(2,1)S(1)} %get-tuple-element.52.refs_3_), channel_id=1, source_target_pairs={{0,1},{1,0},{2,3},{3,2},{4,5},{5,4},{6,7},{7,6},{8,9},{9,8},{10,11... | collective-permute-start | bytes 786440 | tf_op jit(solution)/shard_map/ppermute | solution.py:435
  70.8 15.6 %all-to-all-start = ((bf16[8,8,3072]{2,1,0:T(8,128)(2,1)}), bf16[8,8,3072]{2,1,0:T(8,128)(2,1)S(1)}, u32[]{:S(2)}, u32[]{:S(2)}) async-start(bf16[8,8,3072]{2,1,0:T(8,128)(2,1)} %pad_maximum_fusion.1), calls=%async_computation | async-start | bytes 786432 | tf_op jit(solution)/shard_map/all_to_all | solution.py:97
  75.6 1.4 %copy-start = (bf16[1,512,1024]{2,1,0:T(8,128)(2,1)S(1)}, bf16[1,512,1024]{2,1,0:T(8,128)(2,1)}, u32[]{:S(2)}) copy-start(bf16[1,512,1024]{2,1,0:T(8,128)(2,1)} %param.7) | copy-start | bytes 3145732
  75.6 1.7 %copy-start.1 = (bf16[1,512,1024]{2,1,0:T(8,128)(2,1)S(1)}, bf16[1,512,1024]{2,1,0:T(8,128)(2,1)}, u32[]{:S(2)}) copy-start(bf16[1,512,1024]{2,1,0:T(8,128)(2,1)} %param.8) | copy-start | bytes 3145732
